TPU v7x, 32 devices: a whole 2x2x4 slice. The times are simulated.
32 devices in a mesh: grp: 2 (over y), dp: 4 (over x, core), mp: 4 (over z).
Axes of the slice: x: 2, y: 2, z: 4, core: 2. Of those that a mesh axis runs over, the one named last changes fastest.
Arguments:
- teacher_hidden: bfloat16 [4096, 8192], P('dp', 'mp'), may hold values from -6 to 6
- teacher_gain: bfloat16 [8192], P('mp'), may hold values from 0.25 to 1.75
- teacher_value: bfloat16 [8192, 1024], P('mp', 'grp'), may hold values from -0.0625 to 0.0625
- student_hidden: bfloat16 [4096, 4096], P(('dp', 'mp')), may hold values from -6 to 6
- student_gain: bfloat16 [4096], replicated, may hold values from 0.25 to 1.75
- student_value: bfloat16 [4096, 1024], P(('dp', 'mp'), 'grp'), may hold values from -0.09375 to 0.09375
- segment_ids: int32 [4, 1024], P('dp'), may hold values from 0 to 7, never falling along the last dimension, each value on 1 to 384 neighbouring positions
Outputs:
- value_grad: float32 [4096, 1024], P(('dp', 'mp'), 'grp')
Inputs may be any that keep to these rules, and one draw needn't show every extreme that they name: `segment_ids`: in every row the ids never fall; each id from 0 to 7 covers 1 to 384 consecutive positions, and one covers exactly 384.
All inputs are finite; a program needn't handle non-finite values.
Results may differ from a plain program's by a relative error of at most 0.0031.
Values may be sent and summed in bfloat16 or wider, within the bound.
No kernel may reach another device: no remote copies, remote signals or barrier semaphores. Data moves between devices by JAX's collectives and lax.ppermute only.
A program may use at most 64 MiB of HBM per device.

v0:
```python
import jax
import jax.numpy as jnp
from jax import lax
from jax.sharding import PartitionSpec as P

DT = 8192
KV = 1024
NSEG = 8


norm_eps = 1e-05
power_eps = 1e-06


def per_device(
    teacher_hidden,
    teacher_gain,
    teacher_value,
    student_hidden,
    student_gain,
    student_value,
    segment_ids,
):
    tok_dev = student_hidden.shape[0]
    member = lax.axis_index("mp")
    teacher_wide = teacher_hidden.astype(jnp.float32)
    scaled = (teacher_wide * teacher_gain.astype(jnp.float32)).astype(jnp.bfloat16)
    row_block = scaled
    projected = lax.psum_scatter(
        jnp.dot(row_block, teacher_value, preferred_element_type=jnp.float32),
        "mp",
        scatter_dimension=0,
        tiled=True,
    )
    squares = lax.psum_scatter(
        jnp.sum(teacher_wide * teacher_wide, axis=1), "mp", scatter_dimension=0, tiled=True
    )
    teacher_scale = lax.rsqrt(squares / DT + norm_eps)
    target = projected * teacher_scale[:, None]
    power_half = jnp.sum(target * target, axis=1)
    target_power = lax.psum(power_half, "grp") / KV + power_eps
    student_wide = student_hidden.astype(jnp.float32)
    student_scale = lax.rsqrt(
        jnp.mean(student_wide * student_wide, axis=1, keepdims=True) + norm_eps
    )
    normed = (student_wide * student_scale * student_gain.astype(jnp.float32)).astype(jnp.bfloat16)
    states = jnp.dot(
        normed,
        lax.all_gather(student_value, ("dp", "mp"), axis=0, tiled=True),
        preferred_element_type=jnp.float32,
    )
    matches = segment_ids[:, :, None] == jnp.arange(NSEG, dtype=jnp.int32)[None, None, :]
    counts = jnp.sum(matches.astype(jnp.int32), axis=1)
    lengths = jnp.sum(jnp.where(matches, counts[:, None, :], 0), axis=2).reshape(-1)
    doc_length = lax.dynamic_slice_in_dim(lengths, member * tok_dev, tok_dev, 0).astype(jnp.float32)
    weighted = ((states - target) / (doc_length * target_power)[:, None]).astype(jnp.bfloat16)
    row_block = normed
    return lax.psum_scatter(
        lax.dot_general(
            row_block, weighted, (((0,), (0,)), ((), ())), preferred_element_type=jnp.float32
        ),
        ("dp", "mp"),
        scatter_dimension=0,
        tiled=True,
    )


def solution(mesh):
    return jax.shard_map(
        per_device,
        mesh=mesh,
        in_specs=(
            P("dp", "mp"),
            P("mp"),
            P("mp", "grp"),
            P(("dp", "mp"), None),
            P(),
            P(("dp", "mp"), "grp"),
            P("dp", None),
        ),
        out_specs=P(("dp", "mp"), "grp"),
        check_vma=False,
    )
```

profile of v0, /device:TPU:0, one launch (start us, length us, event | category | flops | bytes accessed | tf_op | source)
XLA Modules:
  0.0 216.4 jit_solution(2342135819563822087)
XLA Ops:
  7.4 0.0 copy-start
  7.4 0.0 reduce-scatter.3.cloned.1.call-start
  7.4 0.8 convert_element_type.39
  8.2 0.8 copy-done
  9.0 0.0 copy-start.2
  9.0 0.0 copy-start.3
  9.0 5.9 %fusion.5 = f32[1024,512]{1,0:T(8,128)} fusion(bf16[2048,512]{1,0:T(8,128)(2,1)S(1)} %copy-done, bf16[1024,2048]{1,0:T(8,128)(2,1)} %param.7, f32[2048]{0:T(1024)S(1)} %convert_element_type.39), kind=kOutput, calls=%fused_computation.9 | convolution fusion | flops 2153775104 | bytes 8396800 | tf_op jit(solution)/shard_map/dot_general | solution.py:30
  14.9 0.0 copy-start.1
  14.9 0.0 reduce-scatter.3.cloned.1.call-update
  14.9 0.0 all-gather.2.cloned.1.call-start
  15.0 0.5 all-gather.2.cloned.1.call-update
  15.5 0.0 reduce-scatter.5.cloned.1.call-start
  15.5 0.0 copy-done.2
  15.6 0.0 copy-done.3
  15.6 0.6 dynamic-slice.2
  16.8 3.1 %fusion.1 = f32[1024]{0:T(1024)S(1)} fusion(bf16[1024,2048]{1,0:T(8,128)(2,1)} %param.7), kind=kLoop, calls=%fused_computation.3 | loop fusion | flops 6290432 | bytes 4198400 | tf_op jit(solution)/shard_map/reduce_sum | solution.py:36
  19.9 13.7 %all-reduce = f32[1024]{0:T(1024)S(1)} all-reduce(f32[1024]{0:T(1024)S(1)} %fusion.1), channel_id=3, replica_groups=mesh['grp'=2,'dp'=4,'mp'=4] {'mp'}, use_global_device_ids=true, to_apply=%region_3.0.clone | all-reduce | flops 1024 | bytes 8192
  33.6 0.1 fusion.17
  33.7 0.0 copy-done.1
  33.7 0.1 convert_reduce_fusion
  33.8 0.1 select_reduce_fusion
  33.9 2.1 fusion.2
  36.0 31.6 %reduce-scatter.3.cloned.1.call-done = f32[256,512]{1,0:T(8,128)} async-done(((f32[1024,512]{1,0:T(8,128)}), f32[256,512]{1,0:T(8,128)}) %reduce-scatter.3.cloned.1.call-update) | async-done | bytes 524304 | tf_op jit(solution)/shard_map/reduce_scatter | solution.py:29
  67.6 1.2 multiply_reduce_fusion
  68.9 4.9 %psum.7 = f32[256]{0:T(256)S(1)} all-reduce(f32[256]{0:T(256)S(1)} %multiply_reduce_fusion), channel_id=1, replica_groups=mesh['grp'=2,'dp'=4,'mp'=4] {'grp'}, use_global_device_ids=true, to_apply=%region_7.8 | all-reduce | flops 256 | bytes 2048 | tf_op jit(solution)/shard_map/psum | solution.py:41
  73.8 0.1 add_multiply_fusion
  73.9 23.9 %all-gather.2.cloned.1.call-done = bf16[4096,512]{1,0:T(8,128)(2,1)} async-done(((bf16[256,512]{1,0:T(8,128)(2,1)}), bf16[4096,512]{1,0:T(8,128)(2,1)}) %all-gather.2.cloned.1.call-update) | async-done | bytes 4194320 | tf_op jit(solution)/shard_map/all_gather | solution.py:49
  97.8 9.3 %fusion.10 = f32[4096,512]{1,0:T(8,128)} fusion(bf16[4096,512]{1,0:T(8,128)(2,1)} %all-gather.2.cloned.1.call-done, bf16[256,4096]{1,0:T(8,128)(2,1)} %param.10, f32[4096]{0:T(1024)S(1)} %convert_element_type.36, f32[256]{0:T(256)S(1)} %add_rsqrt_fusion, f32[256,512]{1,0:T(8,128)} %reduce-scatter.3.cloned.1.call-done, f32[256]{0:T(256)S(1)} %add_multiply_fusion, ...), kind=kOutput, calls=%fused_computation.14 | convolution fusion | flops 2156396544 | bytes 15223808 | tf_op jit(solution)/shard_map/dot_general | solution.py:59
  107.1 0.0 reduce-scatter.5.cloned.1.call-update
  107.1 101.9 %reduce-scatter.5.cloned.1.call-done = f32[256,512]{1,0:T(8,128)} async-done(((f32[4096,512]{1,0:T(8,128)}), f32[256,512]{1,0:T(8,128)}) %reduce-scatter.5.cloned.1.call-update) | async-done | bytes 524304 | tf_op jit(solution)/shard_map/reduce_scatter | solution.py:58
  (2 shorter events, 0.0 us)
Async XLA Ops:
  7.4 1.6 copy-start
  7.4 60.3 %reduce-scatter.3.cloned.1.call-start = ((), (), s32[]{:S(2)}) async-start(), calls=%async_computation.3 | async-start | bytes 2621440 | tf_op jit(solution)/shard_map/reduce_scatter | solution.py:29
  9.0 6.6 %copy-start.2 = (bf16[4096]{0:T(1024)(128)(2,1)S(1)}, bf16[4096]{0:T(1024)(128)(2,1)}, u32[]{:S(2)}) copy-start(bf16[4096]{0:T(1024)(128)(2,1)} %param.11) | copy-start | bytes 24580
  9.0 6.6 %copy-start.3 = (u32[32]{0:T(128)S(1)}, u32[32]{0:T(128)}, u32[]{:S(2)}) copy-start(u32[32]{0:T(128)} %constant.30) | copy-start | bytes 388
  14.9 18.8 %copy-start.1 = (s32[1,1024]{1,0:T(1,128)S(1)}, s32[1,1024]{1,0:T(1,128)}, u32[]{:S(2)}) copy-start(s32[1,1024]{1,0:T(1,128)} %param.13) | copy-start | bytes 12292
  14.9 82.9 %all-gather.2.cloned.1.call-start = ((), (), s32[]{:S(2)}) async-start(), calls=%async_computation.2 | async-start | bytes 4456448 | tf_op jit(solution)/shard_map/all_gather | solution.py:49
  15.5 193.5 %reduce-scatter.5.cloned.1.call-start = ((), (), s32[]{:S(2)}) async-start(), calls=%async_computation.4 | async-start | bytes 8912896 | tf_op jit(solution)/shard_map/reduce_scatter | solution.py:58
Sparse Core Ops, SparseCore 0:
  15.0 52.5 reduce-scatter.2
Sparse Core Ops, SparseCore 1:
  17.6 80.1 all-gather.1
  107.2 101.7 reduce-scatter.4
where the time goes:
time: 217 us; the launch traced here: 216 us
  waiting for transfers between devices  158 us (73%)
  blocking collectives  18.7 us (9%)
  between operations  15.6 us (7%)
  matrix products  15.2 us (7%)
  other arithmetic  7.61 us (4%)
    reduce_scatter x1, waiting for transfers between devices, per_device(): lax.psum_scatter(lax.dot_general(row_block, weighted, (((0,), (0,)), ((),...  102 us
    reduce_scatter x1, waiting for transfers between devices, per_device(): lax.psum_scatter(jnp.dot(row_block, teacher_value, preferred_element_type...  31.6 us
    all_gather x1, waiting for transfers between devices, per_device(): lax.all_gather(student_value, ('dp', 'mp'), axis=0, tiled=True)  23.9 us
    unnamed x1, blocking collectives  13.7 us
    dot_general x1, matrix products, per_device(): lax.dot_general(row_block, weighted, (((0,), (0,)), ((), ())), preferred_...  9.28 us
    dot_general x1, matrix products, per_device(): jnp.dot(row_block, teacher_value, preferred_element_type=jnp.float32)  5.9 us
    psum x1, blocking collectives, per_device(): target_power = lax.psum(power_half, 'grp') / KV + power_eps  4.94 us
  transfers between devices with their start and end apart: 3, of which 3 were waited for; matrix products, arithmetic and copies ran while one was open for 3% of the time, Pallas kernels for 0%

commit v1 on v0

v1 whole, which is shorter than its diff:
```python
import math

import jax
import jax.numpy as jnp
from jax import lax
from jax.sharding import PartitionSpec as P

NSEG = 8

norm_eps = 1e-05
power_eps = 1e-06

HIDDEN_MAX = 6.0
GAIN_MAX = 1.75
TEACHER_VALUE_MAX = 0.0625
STUDENT_VALUE_MAX = 0.09375
HALF_MAX = 60000.0


def half_scale(bound):
    return 2.0 ** math.floor(math.log2(HALF_MAX / bound))


def solution(mesh):
    sizes = dict(mesh.shape)
    grp, dp, mp = sizes["grp"], sizes["dp"], sizes["mp"]
    cores = 2 if dp % 2 == 0 else 1
    chips = dp // cores

    def swap(value, axis, step):
        return lax.ppermute(value, axis, [(i, i ^ step) for i in range(sizes[axis])])

    def per_device(
        teacher_hidden,
        teacher_gain,
        teacher_value,
        student_hidden,
        student_gain,
        student_value,
        segment_ids,
    ):
        f32, bf16, f16 = jnp.float32, jnp.bfloat16, jnp.float16
        tok, ds = student_hidden.shape
        kv_part = student_value.shape[1]
        rows = student_value.shape[0]
        dt_part = teacher_hidden.shape[1]
        dt, kv = dt_part * mp, kv_part * grp
        member = lax.axis_index("mp")
        place = lax.axis_index("dp")
        chip, core = place // cores, place % cores

        column = {0: student_value}
        step = mp // 2
        while step:
            offsets = sorted(column)
            sent = jnp.concatenate([column[o] for o in offsets], axis=0)
            got = swap(sent, "mp", step)
            for i, o in enumerate(offsets):
                column[o ^ step] = got[i * rows : (i + 1) * rows]
            step //= 2

        student_wide = student_hidden.astype(f32)
        student_scale = lax.rsqrt(
            jnp.mean(student_wide * student_wide, axis=1, keepdims=True) + norm_eps
        )
        normed = (student_wide * student_scale * student_gain.astype(f32)).astype(bf16)
        wide = ds // chips
        features = [
            lax.dynamic_slice_in_dim(normed, (chip ^ j) * wide, wide, 1) for j in range(chips)
        ]
        features = [features[0]] + [
            swap(features[j], "dp", cores * j) for j in range(1, chips)
        ]

        teacher_factor = half_scale(dt_part * HIDDEN_MAX * GAIN_MAX * TEACHER_VALUE_MAX)
        order = sorted(range(1, mp), key=lambda k: -k) + [0]
        if mp == 4:
            order = [2, 3, 1, 0]
        gain = teacher_gain.astype(f32)
        projected, squares = None, None
        for k in order:
            block = lax.dynamic_slice_in_dim(teacher_hidden, (member ^ k) * tok, tok, 0)
            wide_block = block.astype(f32)
            part = jnp.dot(
                (wide_block * gain).astype(bf16), teacher_value, preferred_element_type=f32
            )
            square = jnp.sum(wide_block * wide_block, axis=1)
            if k:
                part = swap((part * teacher_factor).astype(f16), "mp", k).astype(f32)
                part = part * (1.0 / teacher_factor)
                square = swap(square, "mp", k)
            projected = part if projected is None else projected + part
            squares = square if squares is None else squares + square
        teacher_scale = lax.rsqrt(squares / dt + norm_eps)
        target = projected * teacher_scale[:, None]
        power_half = jnp.sum(target * target, axis=1)
        power = power_half
        for k in range(1, grp):
            power = power + swap(power_half, "grp", k)
        target_power = power / kv + power_eps

        gathered = jnp.zeros((mp, rows, kv_part), bf16)
        for o, block in column.items():
            gathered = lax.dynamic_update_slice(gathered, block[None], (member ^ o, 0, 0))
        gathered = gathered.reshape(mp * rows, kv_part)
        if cores == 2:
            other = swap(gathered, "dp", 1)
            first = jnp.where(core == 0, gathered, other)
            second = jnp.where(core == 0, other, gathered)
            gathered = jnp.concatenate([first, second], axis=0)
        states_factor = half_scale(GAIN_MAX * ds * STUDENT_VALUE_MAX)
        states = jnp.dot(features[0], gathered, preferred_element_type=f32)
        for j in range(1, chips):
            part = jnp.dot(features[j], gathered, preferred_element_type=f32)
            part = swap((part * states_factor).astype(f16), "dp", cores * j).astype(f32)
            states = states + part * (1.0 / states_factor)

        matches = segment_ids[:, :, None] == jnp.arange(NSEG, dtype=jnp.int32)[None, None, :]
        counts = jnp.sum(matches.astype(jnp.int32), axis=1)
        lengths = jnp.sum(jnp.where(matches, counts[:, None, :], 0), axis=2).reshape(-1)
        doc_length = lax.dynamic_slice_in_dim(lengths, member * tok, tok, 0).astype(f32)
        weighted = ((states - target) / (doc_length * target_power)[:, None]).astype(bf16)

        seen = [weighted] + [swap(weighted, "dp", cores * j) for j in range(1, chips)]
        seen = jnp.concatenate(seen, axis=0)
        held = jnp.concatenate(features, axis=0)
        narrow = wide // cores
        mine = lax.dynamic_slice_in_dim(held, core * narrow, narrow, 1)
        if cores == 2:
            theirs = lax.dynamic_slice_in_dim(held, (1 - core) * narrow, narrow, 1)
            mine = jnp.concatenate([mine, swap(theirs, "dp", 1)], axis=0)
            seen = jnp.concatenate([seen, swap(seen, "dp", 1)], axis=0)
        total = None
        for k in order:
            block = lax.dynamic_slice_in_dim(mine, (member ^ k) * rows, rows, 1)
            part = lax.dot_general(
                block, seen, (((0,), (0,)), ((), ())), preferred_element_type=f32
            )
            if k:
                part = swap(part.astype(bf16), "mp", k).astype(f32)
            total = part if total is None else total + part
        return total

    return jax.shard_map(
        per_device,
        mesh=mesh,
        in_specs=(
            P("dp", "mp"),
            P("mp"),
            P("mp", "grp"),
            P(("dp", "mp"), None),
            P(),
            P(("dp", "mp"), "grp"),
            P("dp", None),
        ),
        out_specs=P(("dp", "mp"), "grp"),
        check_vma=False,
    )
```

time: 217 us -> 118 us (0.54)
  waiting for transfers between devices: 158 us -> 55.4 us
  starting transfers between devices: 0.09 us -> 26 us
  blocking collectives: 18.7 us -> 0 us
  between operations: 15.6 us -> 0.18 us
  local copies, waits for them, and re-layouts: 1.36 us -> 6.96 us
  other arithmetic: 7.61 us -> 12.3 us
    reduce_scatter x2 -> x0, waiting for transfers between devices: 133 us -> none  [the longest x1 102 us: per_device(): lax.psum_scatter(lax.dot_general(row_block, weighted, (((0,), (0,)), ((),...]
    ppermute x0 -> x18, waiting for transfers between devices: none -> 55.4 us  [swap(): lax.ppermute(value, axis, [(i, i ^ step) for i in range(sizes[axis])])]
    ppermute x0 -> x18, starting transfers between devices: none -> 26 us  [swap(): lax.ppermute(value, axis, [(i, i ^ step) for i in range(sizes[axis])])]
    all_gather x1 -> x0, waiting for transfers between devices: 23.9 us -> none  [per_device(): lax.all_gather(student_value, ('dp', 'mp'), axis=0, tiled=True)]
    unnamed x1 -> x0, blocking collectives: 13.7 us -> none
    psum x1 -> x0, blocking collectives: 4.94 us -> none  [per_device(): target_power = lax.psum(power_half, 'grp') / KV + power_eps]
    dynamic_update_slice x0 -> x4, local copies, waits for them, and re-layouts: none -> 4.76 us  [per_device(): lax.dynamic_update_slice(gathered, block[None], (member ^ o, 0, 0))]
    concatenate x0 -> x3, other arithmetic: none -> 2.24 us  [the longest x1 1.37 us: per_device(): held = jnp.concatenate(features, axis=0)]
  transfers between devices with their start and end apart: 3 -> 18, of which waited for: 3 -> 8; matrix products, arithmetic and copies ran while one was open for 3% -> 28% of each run, Pallas kernels for 0% -> 0%
where the time goes in v1:
time: 118 us; the launch traced here: 116 us
  waiting for transfers between devices  55.4 us (47%)
  starting transfers between devices  26 us (22%)
  matrix products  15.6 us (13%)
  other arithmetic  12.3 us (10%)
  local copies, waits for them, and re-layouts  6.96 us (6%)
    ppermute x18, waiting for transfers between devices, swap(): lax.ppermute(value, axis, [(i, i ^ step) for i in range(sizes[axis])])  55.4 us
    ppermute x18, starting transfers between devices, swap(): lax.ppermute(value, axis, [(i, i ^ step) for i in range(sizes[axis])])  26 us
    dot_general x4, matrix products, per_device(): jnp.dot((wide_block * gain).astype(bf16), teacher_value, preferred_elemen...  10.2 us
    dynamic_update_slice x4, local copies, waits for them, and re-layouts, per_device(): lax.dynamic_update_slice(gathered, block[None], (member ^ o, 0, 0))  4.76 us
    reduce_sum x1, other arithmetic, per_device(): square = jnp.sum(wide_block * wide_block, axis=1)  3.07 us
    dot_general x4, matrix products, per_device(): lax.dot_general(block, seen, (((0,), (0,)), ((), ())), preferred_element_...  2.7 us
  transfers between devices with their start and end apart: 18, of which 8 were waited for; matrix products, arithmetic and copies ran while one was open for 28% of the time, Pallas kernels for 0%

profile of v1, /device:TPU:0, one launch (start us, length us, event | category | flops | bytes accessed | tf_op | source)
XLA Modules:
  0.0 116.4 jit_solution(11400462521695389632)
XLA Ops:
  0.0 0.0 copy-start
  0.0 4.0 %collective-permute-start.2 = (bf16[256,512]{1,0:T(8,128)(2,1)}, bf16[256,512]{1,0:T(8,128)(2,1)S(1)}, u32[]{:S(2)}, u32[]{:S(2)}) collective-permute-start(bf16[256,512]{1,0:T(8,128)(2,1)} %param.12), channel_id=1, source_target_pairs={{0,2},{1,3},{2,0},{3,1},{4,6},{5,7},{6,4},{7,5},{8,10},{9,11},{10,... | collective-permute-start | bytes 786440 | tf_op jit(solution)/shard_map/ppermute | solution.py:31
  4.0 0.7 convert_element_type.96
  4.7 2.1 %fusion = f32[256]{0:T(256)S(1)} fusion(bf16[256,4096]{1,0:T(8,128)(2,1)} %param.10), kind=kLoop, calls=%fused_computation.2 | loop fusion | flops 3145472 | bytes 2098176 | tf_op jit(solution)/shard_map/reduce_sum | solution.py:64
  6.8 2.2 %fusion.2 = bf16[256,4096]{1,0:T(8,128)(2,1)S(1)} fusion(bf16[256,4096]{1,0:T(8,128)(2,1)} %param.10, f32[4096]{0:T(1024)S(1)} %convert_element_type.96, f32[256]{0:T(256)S(1)} %add_rsqrt_fusion.1), kind=kLoop, calls=%fused_computation.4 | loop fusion | flops 4194304 | bytes 4211712 | tf_op jit(solution)/shard_map/convert_element_type | solution.py:66
  9.1 1.1 constant_dynamic-slice_fusion
  10.2 1.5 %collective-permute-start = (bf16[256,2048]{1,0:T(8,128)(2,1)}, bf16[256,2048]{1,0:T(8,128)(2,1)}, u32[]{:S(2)}, u32[]{:S(2)}) collective-permute-start(bf16[256,2048]{1,0:T(8,128)(2,1)} %get-tuple-element.13), channel_id=1, source_target_pairs={{0,8},{4,12},{8,0},{12,4},{1,9},{5,13},{9,1},{13,5},{2,10},{6,14},... | collective-permute-start | bytes 3145736 | tf_op jit(solution)/shard_map/ppermute | solution.py:31
  11.7 3.1 %fusion.6 = (f32[256]{0:T(256)S(1)}, f32[256]{0:T(256)S(1)}, f32[256]{0:T(256)S(1)}, f32[256]{0:T(256)S(1)}) fusion(bf16[1024,2048]{1,0:T(8,128)(2,1)} %param.7, s32[]{:T(128)S(6)} %select_n.90, s32[]{:T(128)S(6)} %select_n.82, s32[]{:T(128)S(6)} %select_n.91, s32[]{:T(128)S(6)} %select_n.92), kind=kLoop, calls=%fused_computation.28 | loop fusion | flops 6290432 | bytes 4198416 | tf_op jit(solution)/shard_map/reduce_sum | solution.py:87
  14.7 1.6 %collective-permute-start.10 = (f32[256]{0:T(256)S(1)}, f32[256]{0:T(256)S(1)}, u32[]{:S(2)}, u32[]{:S(2)}) collective-permute-start(f32[256]{0:T(256)S(1)} %get-tuple-element.5), channel_id=1, source_target_pairs={{0,3},{1,2},{2,1},{3,0},{4,7},{5,6},{6,5},{7,4},{8,11},{9,10},{10,... | collective-permute-start | bytes 3080 | tf_op jit(solution)/shard_map/ppermute | solution.py:31
  16.3 0.1 collective-permute-start.11
  16.5 2.7 %collective-permute-start.9 = (f32[256]{0:T(256)S(1)}, f32[256]{0:T(256)S(1)}, u32[]{:S(2)}, u32[]{:S(2)}) collective-permute-start(f32[256]{0:T(256)S(1)} %get-tuple-element.6), channel_id=1, source_target_pairs={{0,2},{1,3},{2,0},{3,1},{4,6},{5,7},{6,4},{7,5},{8,10},{9,11},{10,... | collective-permute-start | bytes 3080 | tf_op jit(solution)/shard_map/ppermute | solution.py:31
  19.2 0.0 copy-done.3
  19.2 2.7 %fusion.16 = f16[256,512]{1,0:T(8,128)(2,1)} fusion(bf16[2048,512]{1,0:T(8,128)(2,1)S(1)} %copy-done, f32[2048]{0:T(1024)S(1)} %convert_element_type.101, bf16[1024,2048]{1,0:T(8,128)(2,1)} %param.7, s32[]{:T(128)S(6)} %select_n.82), kind=kOutput, calls=%fused_computation.42 | convolution fusion | flops 538705920 | bytes 3416068 | tf_op jit(solution)/shard_map/dot_general | solution.py:84
  21.9 0.0 collective-permute-done.2
  21.9 0.8 pad_maximum_fusion.16
  22.7 0.7 collective-permute-start.3
  23.4 1.1 broadcast_in_dim.18
  24.5 0.7 bitcast_dynamic-update-slice_fusion.1
  25.2 2.7 %fusion.17 = f16[256,512]{1,0:T(8,128)(2,1)} fusion(bf16[2048,512]{1,0:T(8,128)(2,1)S(1)} %copy-done, f32[2048]{0:T(1024)S(1)} %convert_element_type.101, bf16[1024,2048]{1,0:T(8,128)(2,1)} %param.7, s32[]{:T(128)S(6)} %select_n.90), kind=kOutput, calls=%fused_computation.43 | convolution fusion | flops 538705920 | bytes 3416068 | tf_op jit(solution)/shard_map/dot_general | solution.py:84
  27.9 0.7 bitcast_dynamic-update-slice_fusion
  28.6 6.7 %collective-permute-done.3 = bf16[512,512]{1,0:T(8,128)(2,1)} collective-permute-done((bf16[512,512]{1,0:T(8,128)(2,1)}, bf16[512,512]{1,0:T(8,128)(2,1)}, u32[]{:S(2)}, u32[]{:S(2)}) %collective-permute-start.3) | collective-permute-done | bytes 524320 | tf_op jit(solution)/shard_map/ppermute | solution.py:31
  35.3 1.7 %fusion.47 = bf16[4,256,512]{2,1,0:T(8,128)(2,1)} fusion(bf16[4,256,512]{2,1,0:T(8,128)(2,1)} %bitcast_dynamic-update-slice_fusion, s32[]{:T(128)S(6)} %select_n.86, bf16[512,512]{1,0:T(8,128)(2,1)} %collective-permute-done.3), kind=kLoop, calls=%fused_computation.78 | loop fusion | bytes 524292 | tf_op jit(solution)/shard_map/dynamic_update_slice | solution.py:104
  37.0 1.7 %fusion.46 = bf16[4,256,512]{2,1,0:T(8,128)(2,1)} fusion(bf16[4,256,512]{2,1,0:T(8,128)(2,1)} %fusion.47, s32[]{:T(128)S(6)} %select_n.87, bf16[512,512]{1,0:T(8,128)(2,1)} %collective-permute-done.3), kind=kLoop, calls=%fused_computation.76 | loop fusion | bytes 524292 | tf_op jit(solution)/shard_map/dynamic_update_slice | solution.py:104
  38.7 0.0 collective-permute-start.4
  38.7 2.6 %fusion.18 = f16[256,512]{1,0:T(8,128)(2,1)} fusion(bf16[2048,512]{1,0:T(8,128)(2,1)S(1)} %copy-done, f32[2048]{0:T(1024)S(1)} %convert_element_type.101, bf16[1024,2048]{1,0:T(8,128)(2,1)} %param.7, s32[]{:T(128)S(6)} %select_n.91), kind=kOutput, calls=%fused_computation.44 | convolution fusion | flops 538705920 | bytes 3416068 | tf_op jit(solution)/shard_map/dot_general | solution.py:84
  41.3 0.1 convert_reduce_fusion
  41.4 0.0 collective-permute-done.10
  41.4 0.5 collective-permute-start.6
  42.0 0.0 collective-permute-done.11
  42.0 2.5 %collective-permute-start.7 = (f16[256,512]{1,0:T(8,128)(2,1)}, f16[256,512]{1,0:T(8,128)(2,1)}, u32[]{:S(2)}, u32[]{:S(2)}) collective-permute-start(f16[256,512]{1,0:T(8,128)(2,1)} %fusion.17), channel_id=1, source_target_pairs={{0,3},{1,2},{2,1},{3,0},{4,7},{5,6},{6,5},{7,4},{8,11},{9,10},{10,... | collective-permute-start | bytes 786440 | tf_op jit(solution)/shard_map/ppermute | solution.py:31
  44.5 0.0 collective-permute-done.9
  44.5 0.5 collective-permute-start.8
  45.0 0.1 select_reduce_fusion
  45.1 17.8 %collective-permute-done.6 = f16[256,512]{1,0:T(8,128)(2,1)} collective-permute-done((f16[256,512]{1,0:T(8,128)(2,1)}, f16[256,512]{1,0:T(8,128)(2,1)}, u32[]{:S(2)}, u32[]{:S(2)}) %collective-permute-start.6) | collective-permute-done | bytes 262176 | tf_op jit(solution)/shard_map/ppermute | solution.py:31
  62.9 0.0 collective-permute-done.7
  62.9 1.1 collective-permute-done.8
  64.0 2.3 %multiply_reduce_fusion = (f32[256]{0:T(256)S(1)}, f32[256,512]{1,0:T(8,128)S(1)}) fusion(f32[256]{0:T(256)S(1)} %add_rsqrt_fusion, bf16[2048,512]{1,0:T(8,128)(2,1)S(1)} %copy-done, f32[2048]{0:T(1024)S(1)} %convert_element_type.101, bf16[1024,2048]{1,0:T(8,128)(2,1)} %param.7, s32[]{:T(128)S(6)} %select_n.92, f16[256,512]{1,0:T(8,128)(2,1)} %collective-permute-done.8, ...), kind=kOutput, calls=%fused_computation.73 | convolution fusion | flops 539754240 | bytes 4466692 | tf_op jit(solution)/shard_map/dot_general | solution.py:84
  66.3 1.6 %collective-permute-start.12 = (f32[256]{0:T(256)S(1)}, f32[256]{0:T(256)S(1)}, u32[]{:S(2)}, u32[]{:S(2)}) collective-permute-start(f32[256]{0:T(256)S(1)} %get-tuple-element.15), channel_id=1, source_target_pairs={{0,16},{16,0},{1,17},{17,1},{2,18},{18,2},{3,19},{19,3},{4,20},{20... | collective-permute-start | bytes 3080 | tf_op jit(solution)/shard_map/ppermute | solution.py:31
  67.9 0.0 collective-permute-done.4
  67.9 1.7 %broadcast_select_fusion.1 = (bf16[1024,512]{1,0:T(8,128)(2,1)S(1)}, bf16[1024,512]{1,0:T(8,128)(2,1)S(1)}) fusion(bf16[1024,512]{1,0:T(8,128)(2,1)} %collective-permute-done.4, pred[]{:T(512)S(6)} %eq.31, bf16[4,256,512]{2,1,0:T(8,128)(2,1)} %fusion.46), kind=kLoop, calls=%fused_computation.58 | loop fusion | flops 1048576 | bytes 4194305 | tf_op jit(solution)/shard_map/jit(_where)/select_n | solution.py:108
  69.6 0.0 collective-permute-done
  69.6 1.9 %fusion.19 = f16[256,512]{1,0:T(8,128)(2,1)S(1)} fusion(bf16[256,2048]{1,0:T(8,128)(2,1)} %collective-permute-done, bf16[1024,512]{1,0:T(8,128)(2,1)S(1)} %get-tuple-element.10, bf16[1024,512]{1,0:T(8,128)(2,1)S(1)} %get-tuple-element.9), kind=kOutput, calls=%fused_computation.48 | convolution fusion | flops 541327360 | bytes 3407872 | tf_op jit(solution)/shard_map/dot_general | solution.py:114
  71.5 0.6 collective-permute-start.5
  72.1 0.0 collective-permute-done.12
  72.1 0.1 add_multiply_fusion.1
  72.2 1.4 %fusion.25 = (bf16[512,1024]{1,0:T(8,128)(2,1)S(1)}, bf16[512,1024]{1,0:T(8,128)(2,1)S(1)}) fusion(s32[]{:T(128)S(6)} %select_n.81, bf16[256,2048]{1,0:T(8,128)(2,1)S(1)} %get-tuple-element.14, bf16[256,2048]{1,0:T(8,128)(2,1)} %collective-permute-done, s32[]{:T(128)S(6)} %select_n.80), kind=kLoop, calls=%fused_computation.50 | loop fusion | flops 4194304 | bytes 4194312 | tf_op jit(solution)/shard_map/concatenate | solution.py:126
  73.6 0.1 collective-permute-start.1
  73.7 4.9 %collective-permute-done.5 = f16[256,512]{1,0:T(8,128)(2,1)S(1)} collective-permute-done((f16[256,512]{1,0:T(8,128)(2,1)S(1)}, f16[256,512]{1,0:T(8,128)(2,1)S(1)}, u32[]{:S(2)}, u32[]{:S(2)}) %collective-permute-start.5) | collective-permute-done | bytes 262176 | tf_op jit(solution)/shard_map/ppermute | solution.py:31
  78.6 0.7 fusion.32
  79.3 0.6 collective-permute-start.13
  79.9 5.9 %collective-permute-done.13 = bf16[256,512]{1,0:T(8,128)(2,1)S(1)} collective-permute-done((bf16[256,512]{1,0:T(8,128)(2,1)S(1)}, bf16[256,512]{1,0:T(8,128)(2,1)S(1)}, u32[]{:S(2)}, u32[]{:S(2)}) %collective-permute-start.13) | collective-permute-done | bytes 262176 | tf_op jit(solution)/shard_map/ppermute | solution.py:31
  85.8 0.1 collective-permute-start.14
  85.9 0.0 collective-permute-done.1
  85.9 1.9 %collective-permute-done.14 = bf16[512,512]{1,0:T(8,128)(2,1)S(1)} collective-permute-done((bf16[512,512]{1,0:T(8,128)(2,1)S(1)}, bf16[512,512]{1,0:T(8,128)(2,1)S(1)}, u32[]{:S(2)}, u32[]{:S(2)}) %collective-permute-start.14) | collective-permute-done | bytes 524320 | tf_op jit(solution)/shard_map/ppermute | solution.py:31
  87.8 0.5 convolution_convert_fusion.2
  88.3 6.6 %collective-permute-start.15 = (bf16[256,512]{1,0:T(8,128)(2,1)S(1)}, bf16[256,512]{1,0:T(8,128)(2,1)S(1)}, u32[]{:S(2)}, u32[]{:S(2)}) collective-permute-start(bf16[256,512]{1,0:T(8,128)(2,1)S(1)} %convolution_convert_fusion.2), channel_id=1, source_target_pairs={{0,2},{1,3},{2,0},{3,1},{4,6},{5,7},{6,4},{7,5},{8,10},{9,11},{10,... | collective-permute-start | bytes 786440 | tf_op jit(solution)/shard_map/ppermute | solution.py:31
  94.9 0.5 convolution_convert_fusion.1
  95.3 2.2 %collective-permute-start.16 = (bf16[256,512]{1,0:T(8,128)(2,1)S(1)}, bf16[256,512]{1,0:T(8,128)(2,1)S(1)}, u32[]{:S(2)}, u32[]{:S(2)}) collective-permute-start(bf16[256,512]{1,0:T(8,128)(2,1)S(1)} %convolution_convert_fusion.1), channel_id=1, source_target_pairs={{0,3},{1,2},{2,1},{3,0},{4,7},{5,6},{6,5},{7,4},{8,11},{9,10},{10,... | collective-permute-start | bytes 786440 | tf_op jit(solution)/shard_map/ppermute | solution.py:31
  97.6 0.5 convolution_convert_fusion
  98.1 0.1 collective-permute-start.17
  98.1 15.1 %collective-permute-done.15 = bf16[256,512]{1,0:T(8,128)(2,1)S(1)} collective-permute-done((bf16[256,512]{1,0:T(8,128)(2,1)S(1)}, bf16[256,512]{1,0:T(8,128)(2,1)S(1)}, u32[]{:S(2)}, u32[]{:S(2)}) %collective-permute-start.15) | collective-permute-done | bytes 262176 | tf_op jit(solution)/shard_map/ppermute | solution.py:31
  113.2 0.0 collective-permute-done.16
  113.2 1.9 %collective-permute-done.17 = bf16[256,512]{1,0:T(8,128)(2,1)S(1)} collective-permute-done((bf16[256,512]{1,0:T(8,128)(2,1)S(1)}, bf16[256,512]{1,0:T(8,128)(2,1)S(1)}, u32[]{:S(2)}, u32[]{:S(2)}) %collective-permute-start.17) | collective-permute-done | bytes 262176 | tf_op jit(solution)/shard_map/ppermute | solution.py:31
  115.2 1.3 %add_add_fusion = f32[256,512]{1,0:T(8,128)} fusion(bf16[256,512]{1,0:T(8,128)(2,1)S(1)} %collective-permute-done.17, bf16[256,512]{1,0:T(8,128)(2,1)S(1)} %collective-permute-done.16, bf16[256,512]{1,0:T(8,128)(2,1)S(1)} %collective-permute-done.15, s32[]{:T(128)S(6)} %select_n.92, bf16[512,1024]{1,0:T(8,128)(2,1)S(1)} %get-tuple-element.12, ...), kind=kOutput, calls=%fused_computation.72 | convolution fusion | flops 273416192 | bytes 4456452 | tf_op jit(solution)/shard_map/dot_general | solution.py:136
  (10 shorter events, 0.1 us)
Async XLA Ops:
  0.0 19.2 %copy-start = (bf16[2048,512]{1,0:T(8,128)(2,1)S(1)}, bf16[2048,512]{1,0:T(8,128)(2,1)}, u32[]{:S(2)}) copy-start(bf16[2048,512]{1,0:T(8,128)(2,1)} %param.9) | copy-start | bytes 6291460
  0.0 21.9 %collective-permute-start.2 = (bf16[256,512]{1,0:T(8,128)(2,1)}, bf16[256,512]{1,0:T(8,128)(2,1)S(1)}, u32[]{:S(2)}, u32[]{:S(2)}) collective-permute-start(bf16[256,512]{1,0:T(8,128)(2,1)} %param.12), channel_id=1, source_target_pairs={{0,2},{1,3},{2,0},{3,1},{4,6},{5,7},{6,4},{7,5},{8,10},{9,11},{10,... | collective-permute-start | bytes 786440 | tf_op jit(solution)/shard_map/ppermute | solution.py:31
  10.2 59.4 %collective-permute-start = (bf16[256,2048]{1,0:T(8,128)(2,1)}, bf16[256,2048]{1,0:T(8,128)(2,1)}, u32[]{:S(2)}, u32[]{:S(2)}) collective-permute-start(bf16[256,2048]{1,0:T(8,128)(2,1)} %get-tuple-element.13), channel_id=1, source_target_pairs={{0,8},{4,12},{8,0},{12,4},{1,9},{5,13},{9,1},{13,5},{2,10},{6,14},... | collective-permute-start | bytes 3145736 | tf_op jit(solution)/shard_map/ppermute | solution.py:31
  11.7 7.5 %copy-start.3 = (bf16[2048]{0:T(1024)(128)(2,1)S(1)}, bf16[2048]{0:T(1024)(128)(2,1)}, u32[]{:S(2)}) copy-start(bf16[2048]{0:T(1024)(128)(2,1)} %param.8) | copy-start | bytes 12292
  14.7 26.7 %collective-permute-start.10 = (f32[256]{0:T(256)S(1)}, f32[256]{0:T(256)S(1)}, u32[]{:S(2)}, u32[]{:S(2)}) collective-permute-start(f32[256]{0:T(256)S(1)} %get-tuple-element.5), channel_id=1, source_target_pairs={{0,3},{1,2},{2,1},{3,0},{4,7},{5,6},{6,5},{7,4},{8,11},{9,10},{10,... | collective-permute-start | bytes 3080 | tf_op jit(solution)/shard_map/ppermute | solution.py:31
  16.3 25.7 %collective-permute-start.11 = (f32[256]{0:T(256)S(1)}, f32[256]{0:T(256)S(1)}, u32[]{:S(2)}, u32[]{:S(2)}) collective-permute-start(f32[256]{0:T(256)S(1)} %get-tuple-element.7), channel_id=1, source_target_pairs={{0,1},{1,0},{2,3},{3,2},{4,5},{5,4},{6,7},{7,6},{8,9},{9,8},{10,11... | collective-permute-start | bytes 3080 | tf_op jit(solution)/shard_map/ppermute | solution.py:31
  16.5 28.1 %collective-permute-start.9 = (f32[256]{0:T(256)S(1)}, f32[256]{0:T(256)S(1)}, u32[]{:S(2)}, u32[]{:S(2)}) collective-permute-start(f32[256]{0:T(256)S(1)} %get-tuple-element.6), channel_id=1, source_target_pairs={{0,2},{1,3},{2,0},{3,1},{4,6},{5,7},{6,4},{7,5},{8,10},{9,11},{10,... | collective-permute-start | bytes 3080 | tf_op jit(solution)/shard_map/ppermute | solution.py:31
  19.2 2.7 %copy-start.1 = (bf16[256,512]{1,0:T(8,128)(2,1)S(1)}, bf16[256,512]{1,0:T(8,128)(2,1)}, u32[]{:S(2)}) copy-start(bf16[256,512]{1,0:T(8,128)(2,1)} %param.12) | copy-start | bytes 786436
  22.7 12.6 %collective-permute-start.3 = (bf16[512,512]{1,0:T(8,128)(2,1)}, bf16[512,512]{1,0:T(8,128)(2,1)}, u32[]{:S(2)}, u32[]{:S(2)}) collective-permute-start(bf16[512,512]{1,0:T(8,128)(2,1)} %pad_maximum_fusion.16), channel_id=1, source_target_pairs={{0,1},{1,0},{2,3},{3,2},{4,5},{5,4},{6,7},{7,6},{8,9},{9,8},{10,11... | collective-permute-start | bytes 1572872 | tf_op jit(solution)/shard_map/ppermute | solution.py:31
  38.7 2.7 %copy-start.2 = (s32[1,1024]{1,0:T(1,128)S(1)}, s32[1,1024]{1,0:T(1,128)}, u32[]{:S(2)}) copy-start(s32[1,1024]{1,0:T(1,128)} %param.13) | copy-start | bytes 12292
  38.7 29.2 %collective-permute-start.4 = (bf16[1024,512]{1,0:T(8,128)(2,1)}, bf16[1024,512]{1,0:T(8,128)(2,1)}, u32[]{:S(2)}, u32[]{:S(2)}) collective-permute-start(bf16[1024,512]{1,0:T(8,128)(2,1)} %bitcast.4), channel_id=1, source_target_pairs={{0,4},{4,0},{8,12},{12,8},{1,5},{5,1},{9,13},{13,9},{2,6},{6,2},{1... | collective-permute-start | bytes 3145736 | tf_op jit(solution)/shard_map/ppermute | solution.py:31
  41.4 21.5 %collective-permute-start.6 = (f16[256,512]{1,0:T(8,128)(2,1)}, f16[256,512]{1,0:T(8,128)(2,1)}, u32[]{:S(2)}, u32[]{:S(2)}) collective-permute-start(f16[256,512]{1,0:T(8,128)(2,1)} %fusion.16), channel_id=1, source_target_pairs={{0,2},{1,3},{2,0},{3,1},{4,6},{5,7},{6,4},{7,5},{8,10},{9,11},{10,... | collective-permute-start | bytes 786440 | tf_op jit(solution)/shard_map/ppermute | solution.py:31
  42.0 20.9 %collective-permute-start.7 = (f16[256,512]{1,0:T(8,128)(2,1)}, f16[256,512]{1,0:T(8,128)(2,1)}, u32[]{:S(2)}, u32[]{:S(2)}) collective-permute-start(f16[256,512]{1,0:T(8,128)(2,1)} %fusion.17), channel_id=1, source_target_pairs={{0,3},{1,2},{2,1},{3,0},{4,7},{5,6},{6,5},{7,4},{8,11},{9,10},{10,... | collective-permute-start | bytes 786440 | tf_op jit(solution)/shard_map/ppermute | solution.py:31
  44.5 19.5 %collective-permute-start.8 = (f16[256,512]{1,0:T(8,128)(2,1)}, f16[256,512]{1,0:T(8,128)(2,1)}, u32[]{:S(2)}, u32[]{:S(2)}) collective-permute-start(f16[256,512]{1,0:T(8,128)(2,1)} %fusion.18), channel_id=1, source_target_pairs={{0,1},{1,0},{2,3},{3,2},{4,5},{5,4},{6,7},{7,6},{8,9},{9,8},{10,11... | collective-permute-start | bytes 786440 | tf_op jit(solution)/shard_map/ppermute | solution.py:31
  66.3 5.8 %collective-permute-start.12 = (f32[256]{0:T(256)S(1)}, f32[256]{0:T(256)S(1)}, u32[]{:S(2)}, u32[]{:S(2)}) collective-permute-start(f32[256]{0:T(256)S(1)} %get-tuple-element.15), channel_id=1, source_target_pairs={{0,16},{16,0},{1,17},{17,1},{2,18},{18,2},{3,19},{19,3},{4,20},{20... | collective-permute-start | bytes 3080 | tf_op jit(solution)/shard_map/ppermute | solution.py:31
  71.5 7.1 %collective-permute-start.5 = (f16[256,512]{1,0:T(8,128)(2,1)S(1)}, f16[256,512]{1,0:T(8,128)(2,1)S(1)}, u32[]{:S(2)}, u32[]{:S(2)}) collective-permute-start(f16[256,512]{1,0:T(8,128)(2,1)S(1)} %fusion.19), channel_id=1, source_target_pairs={{0,8},{4,12},{8,0},{12,4},{1,9},{5,13},{9,1},{13,5},{2,10},{6,14},... | collective-permute-start | bytes 786440 | tf_op jit(solution)/shard_map/ppermute | solution.py:31
  73.6 12.3 %collective-permute-start.1 = (bf16[512,1024]{1,0:T(8,128)(2,1)S(1)}, bf16[512,1024]{1,0:T(8,128)(2,1)S(1)}, u32[]{:S(2)}, u32[]{:S(2)}) collective-permute-start(bf16[512,1024]{1,0:T(8,128)(2,1)S(1)} %get-tuple-element.11), channel_id=1, source_target_pairs={{0,4},{4,0},{8,12},{12,8},{1,5},{5,1},{9,13},{13,9},{2,6},{6,2},{1... | collective-permute-start | bytes 3145736 | tf_op jit(solution)/shard_map/ppermute | solution.py:31
  79.3 6.4 %collective-permute-start.13 = (bf16[256,512]{1,0:T(8,128)(2,1)S(1)}, bf16[256,512]{1,0:T(8,128)(2,1)S(1)}, u32[]{:S(2)}, u32[]{:S(2)}) collective-permute-start(bf16[256,512]{1,0:T(8,128)(2,1)S(1)} %fusion.32), channel_id=1, source_target_pairs={{0,8},{4,12},{8,0},{12,4},{1,9},{5,13},{9,1},{13,5},{2,10},{6,14},... | collective-permute-start | bytes 786440 | tf_op jit(solution)/shard_map/ppermute | solution.py:31
  85.8 2.0 %collective-permute-start.14 = (bf16[512,512]{1,0:T(8,128)(2,1)S(1)}, bf16[512,512]{1,0:T(8,128)(2,1)S(1)}, u32[]{:S(2)}, u32[]{:S(2)}) collective-permute-start(bf16[512,512]{1,0:T(8,128)(2,1)S(1)} %pad_maximum_fusion.17), channel_id=1, source_target_pairs={{0,4},{4,0},{8,12},{12,8},{1,5},{5,1},{9,13},{13,9},{2,6},{6,2},{1... | collective-permute-start | bytes 1572872 | tf_op jit(solution)/shard_map/ppermute | solution.py:31
  88.3 25.0 %collective-permute-start.15 = (bf16[256,512]{1,0:T(8,128)(2,1)S(1)}, bf16[256,512]{1,0:T(8,128)(2,1)S(1)}, u32[]{:S(2)}, u32[]{:S(2)}) collective-permute-start(bf16[256,512]{1,0:T(8,128)(2,1)S(1)} %convolution_convert_fusion.2), channel_id=1, source_target_pairs={{0,2},{1,3},{2,0},{3,1},{4,6},{5,7},{6,4},{7,5},{8,10},{9,11},{10,... | collective-permute-start | bytes 786440 | tf_op jit(solution)/shard_map/ppermute | solution.py:31
  95.3 17.9 %collective-permute-start.16 = (bf16[256,512]{1,0:T(8,128)(2,1)S(1)}, bf16[256,512]{1,0:T(8,128)(2,1)S(1)}, u32[]{:S(2)}, u32[]{:S(2)}) collective-permute-start(bf16[256,512]{1,0:T(8,128)(2,1)S(1)} %convolution_convert_fusion.1), channel_id=1, source_target_pairs={{0,3},{1,2},{2,1},{3,0},{4,7},{5,6},{6,5},{7,4},{8,11},{9,10},{10,... | collective-permute-start | bytes 786440 | tf_op jit(solution)/shard_map/ppermute | solution.py:31
  98.1 17.1 %collective-permute-start.17 = (bf16[256,512]{1,0:T(8,128)(2,1)S(1)}, bf16[256,512]{1,0:T(8,128)(2,1)S(1)}, u32[]{:S(2)}, u32[]{:S(2)}) collective-permute-start(bf16[256,512]{1,0:T(8,128)(2,1)S(1)} %convolution_convert_fusion), channel_id=1, source_target_pairs={{0,1},{1,0},{2,3},{3,2},{4,5},{5,4},{6,7},{7,6},{8,9},{9,8},{10,11... | collective-permute-start | bytes 786440 | tf_op jit(solution)/shard_map/ppermute | solution.py:31

commit v2 on v1

v2 whole, which is shorter than its diff:
```python
import math

import jax
import jax.numpy as jnp
from jax import lax
from jax.experimental import pallas as pl
from jax.experimental.pallas import tpu as pltpu
from jax.sharding import PartitionSpec as P

NSEG = 8

norm_eps = 1e-05
power_eps = 1e-06

HIDDEN_MAX = 6.0
GAIN_MAX = 1.75
TEACHER_VALUE_MAX = 0.0625
STUDENT_VALUE_MAX = 0.09375
HALF_MAX = 60000.0


def half_scale(bound):
    return 2.0 ** math.floor(math.log2(HALF_MAX / bound))


VMEM_BYTES = 24 * 2**20
SQUARE_FACTOR = 1024.0
EXTRA_ROWS = 16


def call(kernel, scalars, arrays, in_hbm, out, scratch, name):
    arrays = [pltpu.with_memory_space_constraint(a, pltpu.HBM) for a in arrays[:in_hbm]] + list(
        arrays[in_hbm:]
    )
    return pl.pallas_call(
        kernel,
        out_shape=[pltpu.VMEM(shape, dtype) for shape, dtype in out],
        grid_spec=pltpu.PrefetchScalarGridSpec(
            num_scalar_prefetch=1,
            grid=(),
            in_specs=[pl.BlockSpec(memory_space=pltpu.HBM)] * in_hbm
            + [pl.BlockSpec(memory_space=pltpu.VMEM)] * (len(arrays) - in_hbm),
            out_specs=[pl.BlockSpec(memory_space=pltpu.VMEM)] * len(out),
            scratch_shapes=scratch,
        ),
        compiler_params=pltpu.CompilerParams(vmem_limit_bytes=VMEM_BYTES),
        cost_estimate=pl.CostEstimate(flops=1, bytes_accessed=1, transcendentals=0),
        name=name,
    )(scalars.astype(jnp.int32), *arrays)


def lane_sum(wide, lanes):
    for c in range(0, wide.shape[1], 128):
        lanes = lanes + wide[:, c : c + 128]
    return lanes


def prepare(places, student, student_gain, hidden, gain, value, chips, cores, dt, factor):
    number = places.shape[0] - 2
    tok, ds = student.shape
    depth, kv = value.shape
    wide = ds // (chips * cores)
    chunk = math.gcd(512, wide)
    deep = math.gcd(512, depth)
    pieces = 4 if tok % 64 == 0 else 1
    rows = tok // pieces
    shared = cores + chips - 1

    def kernel(places_ref, student_ref, hidden_ref, value_ref, student_gain_ref, gain_ref, *refs):
        feature_refs, out_refs = refs[:shared], refs[shared : shared + number]
        student_held, held, value_held, scaled, square_ref, sems = refs[shared + number :]
        student_copies = []
        for p in range(pieces):
            at = pl.ds(p * rows, rows)
            student_copies.append(
                pltpu.make_async_copy(student_ref.at[at], student_held.at[at], sems.at[p])
            )
            student_copies[-1].start()
        copies = []
        for i in range(number):
            at = pl.ds(pl.multiple_of(places_ref[i] * tok, tok), tok)
            copies.append(
                pltpu.make_async_copy(hidden_ref.at[at], held.at[i], sems.at[pieces + i])
            )
            copies[-1].start()
        value_copy = pltpu.make_async_copy(value_ref, value_held, sems.at[pieces + number])
        value_copy.start()

        def normalise_rows(r, _):
            at = pl.ds(pl.multiple_of(r * 16, 16), 16)
            lanes = jnp.zeros((16, 128), jnp.float32)
            for c in range(0, ds, chunk):
                part = student_held[at, c : c + chunk].astype(jnp.float32)
                lanes = lane_sum(part * part, lanes)
            mean = jnp.sum(lanes, axis=1, keepdims=True) * (1.0 / ds)
            scale = lax.rsqrt(mean + norm_eps)
            for n in range(chips * cores):
                j, h = n // cores, n % cores
                chip = jnp.bitwise_xor(places_ref[number], j)
                core = jnp.bitwise_xor(places_ref[number + 1], h)
                base = (chip * cores + core) * wide
                feature_ref = feature_refs[cores - 1 + j if j else h]
                to = pl.ds(pl.multiple_of((h * tok if j else 0) + r * 16, 16), 16)
                for c in range(0, wide, chunk):
                    src = pl.ds(pl.multiple_of(base + c, chunk), chunk)
                    part = student_held[at, src].astype(jnp.float32) * scale
                    part = part * student_gain_ref[:, src].astype(jnp.float32)
                    feature_ref[to, c : c + chunk] = part.astype(jnp.bfloat16)
            return 0

        for p, copy in enumerate(student_copies):
            copy.wait()
            lax.fori_loop(p * rows // 16, (p + 1) * rows // 16, normalise_rows, 0, unroll=2)

        for i in range(number):
            copies[i].wait()

            def scale_rows(r, _, i=i):
                at = pl.ds(pl.multiple_of(r * 16, 16), 16)
                to = pl.ds(pl.multiple_of(i * tok + r * 16, 16), 16)
                lanes = jnp.zeros((16, 128), jnp.float32)
                for c in range(0, depth, deep):
                    part = held[i, at, c : c + deep].astype(jnp.float32)
                    lanes = lane_sum(part * part, lanes)
                    part = part * gain_ref[:, c : c + deep].astype(jnp.float32)
                    scaled[to, c : c + deep] = part.astype(jnp.bfloat16)
                square_ref[to, :] = lanes
                return 0

            lax.fori_loop(0, tok // 16, scale_rows, 0, unroll=4)
        value_copy.wait()
        product = jnp.dot(scaled[...], value_held[...], preferred_element_type=jnp.float32)
        ones = jnp.ones((8, 128), jnp.bfloat16)
        across = (((1,), (1,)), ((), ()))
        rest = square_ref[...]
        square = jnp.zeros((8, number * tok), jnp.float32)
        for _ in range(3):
            piece = rest.astype(jnp.bfloat16)
            rest = rest - piece.astype(jnp.float32)
            square += lax.dot_general(ones, piece, across, preferred_element_type=jnp.float32)
        square = square * (SQUARE_FACTOR / dt)
        first = square.astype(jnp.bfloat16).astype(jnp.float32)
        rest = (square - first) * 256.0
        second = rest.astype(jnp.bfloat16).astype(jnp.float32)
        third = (rest - second) * 256.0
        row = lax.broadcasted_iota(jnp.int32, (8, number * tok), 0)
        split = jnp.where(row == 0, first, jnp.where(row == 1, second, third))
        for i, out_ref in enumerate(out_refs):
            out_ref[:tok, :] = product[i * tok : (i + 1) * tok, :] * factor
            out_ref[tok:, :] = jnp.zeros((EXTRA_ROWS, kv), jnp.float32)
            out_ref[tok : tok + 8, :tok] = split[:, i * tok : (i + 1) * tok]

    results = call(
        kernel,
        places,
        [student, hidden, value, student_gain.reshape(1, ds), gain.reshape(1, depth)],
        3,
        [((tok, wide), jnp.bfloat16)] * cores
        + [((cores * tok, wide), jnp.bfloat16)] * (chips - 1)
        + [((tok + EXTRA_ROWS, kv), jnp.float32)] * number,
        [
            pltpu.VMEM((tok, ds), jnp.bfloat16),
            pltpu.VMEM((number, tok, depth), jnp.bfloat16),
            pltpu.VMEM((depth, kv), jnp.bfloat16),
            pltpu.VMEM((number * tok, depth), jnp.bfloat16),
            pltpu.VMEM((number * tok, 128), jnp.float32),
            pltpu.SemaphoreType.DMA((pieces + number + 1,)),
        ],
        "prepare",
    )
    return results[:cores], results[cores:shared], results[shared:]


def states_part(columns, features, values, rows, factor):
    cores = len(values)
    tok, wide = features[0].shape[0] * len(features) // cores, features[0].shape[1]
    kv = values[0][0].shape[1]
    flat = [v for of_core in values for v in of_core]
    spots = [
        (h, n, b)
        for h, of_core in enumerate(values)
        for n, v in enumerate(of_core)
        for b in range(v.shape[0] // rows)
    ]
    each = len(values[0])
    per_core = len(spots) // cores
    place = [(h, 0) if len(features) == cores else (0, h * tok) for h in range(cores)]
    alone = len(features) < cores
    if rows % 128:
        total = jnp.zeros((tok, kv), jnp.float32)
        for i, (h, n, b) in enumerate(spots):
            at = (place[h][1], columns[i % per_core] * rows)
            part = lax.dynamic_slice(features[place[h][0]], at, (tok, rows))
            block = lax.slice_in_dim(values[h][n], b * rows, (b + 1) * rows)
            total += jnp.dot(part, block, preferred_element_type=jnp.float32)
        return total * factor, features[-1][-tok:]

    def kernel(columns_ref, *refs):
        feature_refs, refs = refs[: len(features)], refs[len(features) :]
        value_refs, out_refs = refs[: len(flat)], refs[len(flat) :]
        total = jnp.zeros((tok, kv), jnp.float32)
        for i, (h, n, b) in enumerate(spots):
            start = pl.multiple_of(columns_ref[i % per_core] * rows, rows)
            array, above = place[h]
            total += jnp.dot(
                feature_refs[array][above : above + tok, pl.ds(start, rows)],
                value_refs[h * each + n][b * rows : (b + 1) * rows, :],
                preferred_element_type=jnp.float32,
            )
        out_refs[0][...] = total * factor
        if alone:
            out_refs[1][...] = feature_refs[-1][-tok:, :]

    out = [((tok, kv), jnp.float32)] + [((tok, wide), jnp.bfloat16)] * alone
    results = call(kernel, columns, [*features, *flat], 0, out, [], "states_part")
    return results[0], results[1] if alone else features[-1]


def turned(columns, blocks, rows):
    number = columns.shape[0]
    tok = blocks[0].shape[0]

    def kernel(columns_ref, *refs):
        block_refs, out_ref = refs[:-1], refs[-1]
        for i in range(number):
            src = pl.ds(pl.multiple_of(columns_ref[i] * rows, rows), rows)
            for b, block_ref in enumerate(block_refs):
                out_ref[i * rows : (i + 1) * rows, b * tok : (b + 1) * tok] = block_ref[:tok, src].T

    out = [((number * rows, len(blocks) * tok), jnp.bfloat16)]
    return call(kernel, columns, blocks, 0, out, [], "turned")[0]


def gradient_blocks(held, seen, number):
    rows, tok = held.shape[0] // number, seen[0].shape[0]
    kv = seen[0].shape[1]

    def kernel(_, held_ref, *refs):
        seen_refs, out_refs = refs[: len(seen)], refs[len(seen) :]
        for i, out_ref in enumerate(out_refs):
            total = jnp.zeros((rows, kv), jnp.float32)
            for b, seen_ref in enumerate(seen_refs):
                total += jnp.dot(
                    held_ref[i * rows : (i + 1) * rows, b * tok : (b + 1) * tok],
                    seen_ref[...],
                    preferred_element_type=jnp.float32,
                )
            out_ref[...] = total.astype(out_ref.dtype)

    out = [((rows, kv), jnp.bfloat16)] * (number - 1) + [((rows, kv), jnp.float32)]
    return call(kernel, jnp.zeros(1), [held, *seen], 0, out, [], "gradient_blocks")


def solution(mesh):
    sizes = dict(mesh.shape)
    grp, dp, mp = sizes["grp"], sizes["dp"], sizes["mp"]
    cores = 2 if dp % 2 == 0 else 1
    chips = dp // cores

    def swap(value, axis, step):
        return lax.ppermute(value, axis, [(i, i ^ step) for i in range(sizes[axis])])

    def per_device(
        teacher_hidden,
        teacher_gain,
        teacher_value,
        student_hidden,
        student_gain,
        student_value,
        segment_ids,
    ):
        f32, bf16, f16 = jnp.float32, jnp.bfloat16, jnp.float16
        tok, ds = student_hidden.shape
        kv_part = student_value.shape[1]
        rows = student_value.shape[0]
        dt_part = teacher_hidden.shape[1]
        dt, kv = dt_part * mp, kv_part * grp
        member = lax.axis_index("mp")
        place = lax.axis_index("dp")
        chip, core = place // cores, place % cores

        pieces = {0: student_value}
        step = mp // 2
        while step:
            pieces[step] = swap(student_value, "mp", step)
            step //= 2

        teacher_factor = half_scale(dt * HIDDEN_MAX * GAIN_MAX * TEACHER_VALUE_MAX)
        order = list(range(1, mp)) + [0]
        own, others, parts = prepare(
            jnp.stack([member ^ k for k in order] + [chip, core]),
            student_hidden,
            student_gain,
            teacher_hidden,
            teacher_gain,
            teacher_value,
            chips,
            cores,
            dt,
            teacher_factor,
        )
        others = [swap(part, "dp", cores * (j + 1)) for j, part in enumerate(others)]
        *parts, kept = parts
        parts = [part.astype(f16) for part in parts]
        parts, pieces = lax.optimization_barrier((parts, pieces))
        received = [swap(part, "mp", k) for k, part in zip(order, parts)]

        first = list(pieces)
        later = []
        step = mp // 4
        while step:
            for o in [o for o in pieces if o >= 2 * step and o % (2 * step) == 0]:
                if o ^ step not in pieces:
                    pieces[o ^ step] = swap(pieces[o], "mp", step)
                    later.append(o ^ step)
            step //= 2
        gathered = [jnp.concatenate([pieces[o] for o in first], axis=0)]
        gathered += [pieces[o] for o in later]
        gathered[-1], received[0] = lax.optimization_barrier((gathered[-1], received[0]))
        gathered = [gathered]
        if cores == 2:
            gathered.append([swap(v, "dp", 1) for v in gathered[0]])

        columns = jnp.stack([member ^ o for o in first + later])
        states_factor = half_scale(GAIN_MAX * ds * STUDENT_VALUE_MAX)
        returned = [
            states_part(columns, [part], gathered, rows, states_factor) for part in others
        ]
        second = [part[1] for part in returned]
        returned = [part[0].astype(f16) for part in returned]
        returned = [swap(part, "dp", cores * (j + 1)) for j, part in enumerate(returned)]
        states, _ = states_part(columns, own, gathered, rows, states_factor)

        held = [own[0], *others]
        if cores == 2:
            held += [swap(part, "dp", 1) for part in [own[1], *second]]
        turn_order = jnp.stack([member ^ k for k in order])
        if rows % 128 == 0:
            held = turned(turn_order, held, rows)

        summed = kept
        for part in received:
            summed = summed + part.astype(f32)
        pieces = summed[tok : tok + 3, :tok]
        squares = pieces[0] + (pieces[1] + pieces[2] * (1.0 / 256.0)) * (1.0 / 256.0)
        teacher_scale = lax.rsqrt(squares * (1.0 / SQUARE_FACTOR) + norm_eps)
        projected = summed[:tok] * (1.0 / teacher_factor)
        target = projected * teacher_scale[:, None]
        power_half = jnp.sum(target * target, axis=1)
        power = power_half
        for k in range(1, grp):
            power = power + swap(power_half, "grp", k)
        target_power = power / kv + power_eps

        for part in returned:
            states = states + part.astype(f32)
        states = states * (1.0 / states_factor)

        matches = segment_ids[:, :, None] == jnp.arange(NSEG, dtype=jnp.int32)[None, None, :]
        counts = jnp.sum(matches.astype(jnp.int32), axis=1)
        lengths = jnp.sum(jnp.where(matches, counts[:, None, :], 0), axis=2).reshape(-1)
        doc_length = lax.dynamic_slice_in_dim(lengths, member * tok, tok, 0).astype(f32)
        weighted = ((states - target) / (doc_length * target_power)[:, None]).astype(bf16)

        seen = [weighted] + [swap(weighted, "dp", cores * j) for j in range(1, chips)]
        if cores == 2:
            seen += [swap(part, "dp", 1) for part in seen]
        if rows % 128:
            held = jnp.concatenate([part[:tok] for part in held], axis=0)
            seen = jnp.concatenate(seen, axis=0)
            parts = [
                lax.dot_general(
                    lax.dynamic_slice_in_dim(held, turn_order[i] * rows, rows, 1),
                    seen,
                    (((0,), (0,)), ((), ())),
                    preferred_element_type=f32,
                ).astype(bf16 if order[i] else f32)
                for i in range(mp)
            ]
        else:
            parts = gradient_blocks(held, seen, mp)
        total = parts[-1]
        for i in range(mp - 1):
            total = total + swap(parts[i], "mp", order[i]).astype(f32)
        return total

    return jax.shard_map(
        per_device,
        mesh=mesh,
        in_specs=(
            P("dp", "mp"),
            P("mp"),
            P("mp", "grp"),
            P(("dp", "mp"), None),
            P(),
            P(("dp", "mp"), "grp"),
            P("dp", None),
        ),
        out_specs=P(("dp", "mp"), "grp"),
        check_vma=False,
    )
```

time: 118 us -> 93 us (0.79)
  the two profiles are of different devices: /device:TPU:0 before, /device:TPU:8 now
where the time goes in v2:
time: 93 us; the launch traced here: 92.7 us
  waiting for transfers between devices  53.3 us (57%)
  starting transfers between devices  17.9 us (19%)
  Pallas kernels  14.2 us (15%)
  other arithmetic  3.75 us (4%)
  local copies, waits for them, and re-layouts  3.29 us (4%)
    ppermute x19, waiting for transfers between devices, swap(): lax.ppermute(value, axis, [(i, i ^ step) for i in range(sizes[axis])])  53.3 us
    ppermute x19, starting transfers between devices, swap(): lax.ppermute(value, axis, [(i, i ^ step) for i in range(sizes[axis])])  17.9 us
    pallas_call x5, Pallas kernels, call(): pl.pallas_call(kernel, out_shape=[pltpu.VMEM(shape, dtype) for shape, dty...  14.2 us
  transfers between devices with their start and end apart: 19, of which 10 were waited for; matrix products, arithmetic and copies ran while one was open for 5% of the time, Pallas kernels for 14%

profile of v2, /device:TPU:8, one launch (start us, length us, event | category | flops | bytes accessed | tf_op | source)
XLA Modules:
  0.0 92.7 jit_solution(8108392152486246904)
XLA Ops:
  0.0 0.0 collective-permute-start.2
  0.0 3.0 %collective-permute-start.3 = (bf16[256,512]{1,0:T(8,128)(2,1)}, bf16[256,512]{1,0:T(8,128)(2,1)S(1)}, u32[]{:S(2)}, u32[]{:S(2)}) collective-permute-start(bf16[256,512]{1,0:T(8,128)(2,1)} %param.12), channel_id=1, source_target_pairs={{0,2},{1,3},{2,0},{3,1},{4,6},{5,7},{6,4},{7,5},{8,10},{9,11},{10,... | collective-permute-start | bytes 786440 | tf_op jit(solution)/shard_map/ppermute | solution.py:261
  3.0 0.7 reshape.139.gain_ref
  3.7 0.7 reshape.138.student_gain_ref
  4.5 0.1 stack.42.places_ref
  4.5 7.3 %prepare.1 = (bf16[256,1024]{1,0:T(8,128)(2,1)S(1)}, bf16[256,1024]{1,0:T(8,128)(2,1)}, bf16[512,1024]{1,0:T(8,128)(2,1)S(1)}, f32[272,512]{1,0:T(8,128)S(1)}, f...) custom-call(s32[6]{0:T(128)S(1)} %stack.42.places_ref, bf16[256,4096]{1,0:T(8,128)(2,1)} %student_ref.1, ...), custom_call_target="tpu_custom_call" | custom-call | flops 1 | bytes 1 | tf_op jit(solution)/shard_map/prepare/pallas_call | solution.py:35
  11.8 0.0 copy-start.5
  11.8 0.0 copy-start.6
  11.8 1.6 %collective-permute-start = (bf16[512,1024]{1,0:T(8,128)(2,1)S(1)}, bf16[512,1024]{1,0:T(8,128)(2,1)S(1)}, u32[]{:S(2)}, u32[]{:S(2)}) collective-permute-start(bf16[512,1024]{1,0:T(8,128)(2,1)S(1)} %get-tuple-element.27), channel_id=1, source_target_pairs={{0,8},{4,12},{8,0},{12,4},{1,9},{5,13},{9,1},{13,5},{2,10},{6,14},... | collective-permute-start | bytes 3145736 | tf_op jit(solution)/shard_map/ppermute | solution.py:261
  13.5 0.0 collective-permute-done.2
  13.5 1.4 %collective-permute-done.3 = bf16[256,512]{1,0:T(8,128)(2,1)S(1)} collective-permute-done((bf16[256,512]{1,0:T(8,128)(2,1)}, bf16[256,512]{1,0:T(8,128)(2,1)S(1)}, u32[]{:S(2)}, u32[]{:S(2)}) %collective-permute-start.3) | collective-permute-done | bytes 262176 | tf_op jit(solution)/shard_map/ppermute | solution.py:261
  15.0 1.6 %collective-permute-start.4 = (bf16[256,512]{1,0:T(8,128)(2,1)S(1)}, bf16[256,512]{1,0:T(8,128)(2,1)S(1)}, u32[]{:S(2)}, u32[]{:S(2)}) collective-permute-start(bf16[256,512]{1,0:T(8,128)(2,1)S(1)} %collective-permute-done.3), channel_id=1, source_target_pairs={{0,1},{1,0},{2,3},{3,2},{4,5},{5,4},{6,7},{7,6},{8,9},{9,8},{10,11... | collective-permute-start | bytes 786440 | tf_op jit(solution)/shard_map/ppermute | solution.py:261
  16.6 0.4 collective-permute-start.5
  17.0 2.7 %collective-permute-start.10 = (f16[272,512]{1,0:T(8,128)(2,1)S(1)}, f16[272,512]{1,0:T(8,128)(2,1)S(1)}, u32[]{:S(2)}, u32[]{:S(2)}) collective-permute-start(f16[272,512]{1,0:T(8,128)(2,1)S(1)} %convert_element_type.51), channel_id=1, source_target_pairs={{0,2},{1,3},{2,0},{3,1},{4,6},{5,7},{6,4},{7,5},{8,10},{9,11},{10,... | collective-permute-start | bytes 835592 | tf_op jit(solution)/shard_map/ppermute | solution.py:261
  19.7 0.4 collective-permute-start.11
  20.1 0.0 copy-done.5
  20.2 8.3 %collective-permute-done.4.refs_2_.refs_3_ = bf16[256,512]{1,0:T(8,128)(2,1)S(1)} collective-permute-done((bf16[256,512]{1,0:T(8,128)(2,1)S(1)}, bf16[256,512]{1,0:T(8,128)(2,1)S(1)}, u32[]{:S(2)}, u32[]{:S(2)}) %collective-permute-start.4) | collective-permute-done | bytes 262176 | tf_op jit(solution)/shard_map/ppermute | solution.py:261
  28.4 0.0 collective-permute-start.6
  28.4 0.1 pad_add_fusion.1.columns_ref
  28.5 0.1 convert_reduce_fusion
  28.6 4.8 %collective-permute-done.5 = f16[272,512]{1,0:T(8,128)(2,1)S(1)} collective-permute-done((f16[272,512]{1,0:T(8,128)(2,1)S(1)}, f16[272,512]{1,0:T(8,128)(2,1)S(1)}, u32[]{:S(2)}, u32[]{:S(2)}) %collective-permute-start.5) | collective-permute-done | bytes 278560 | tf_op jit(solution)/shard_map/ppermute | solution.py:261
  33.4 0.0 collective-permute-start.1
  33.4 3.5 %collective-permute-done.10 = f16[272,512]{1,0:T(8,128)(2,1)S(1)} collective-permute-done((f16[272,512]{1,0:T(8,128)(2,1)S(1)}, f16[272,512]{1,0:T(8,128)(2,1)S(1)}, u32[]{:S(2)}, u32[]{:S(2)}) %collective-permute-start.10) | collective-permute-done | bytes 278560 | tf_op jit(solution)/shard_map/ppermute | solution.py:261
  36.9 0.0 collective-permute-start.7
  36.9 4.7 %collective-permute-done.11 = f16[272,512]{1,0:T(8,128)(2,1)S(1)} collective-permute-done((f16[272,512]{1,0:T(8,128)(2,1)S(1)}, f16[272,512]{1,0:T(8,128)(2,1)S(1)}, u32[]{:S(2)}, u32[]{:S(2)}) %collective-permute-start.11) | collective-permute-done | bytes 278560 | tf_op jit(solution)/shard_map/ppermute | solution.py:261
  41.6 0.1 convert_add_fusion
  41.8 0.2 multiply_reduce_fusion
  42.0 1.6 %collective-permute-start.12 = (f32[256]{0:T(256)S(1)}, f32[256]{0:T(256)S(1)}, u32[]{:S(2)}, u32[]{:S(2)}) collective-permute-start(f32[256]{0:T(256)S(1)} %multiply_reduce_fusion), channel_id=1, source_target_pairs={{0,16},{16,0},{1,17},{17,1},{2,18},{18,2},{3,19},{19,3},{4,20},{20... | collective-permute-start | bytes 3080 | tf_op jit(solution)/shard_map/ppermute | solution.py:261
  43.6 0.0 collective-permute-done.7.refs_4_.refs_5_
  43.6 0.0 collective-permute-done.6.refs_3_.refs_4_
  43.6 0.0 copy-done.3
  43.6 0.0 collective-permute-done.refs_0_.refs_1_
  43.6 1.2 %states_part.2 = (f32[256,512]{1,0:T(8,128)S(1)}, bf16[256,1024]{1,0:T(8,128)(2,1)S(1)}) custom-call(s32[4]{0:T(128)S(1)} %pad_add_fusion.1.columns_ref, bf16[512,1024]{1,0:T(8,128)(2,1)S(1)} %collective-permute-done.refs_0_.refs_1_, bf16[768,512]{1,0:T(8,128)(2,1)S(1)} %constant_dynamic-update-slice_fusion.refs_1_.refs_2_, ...), custom_call_target="tpu_custom_call" | custom-call | flops 1 | bytes 1 | tf_op jit(solution)/shard_map/states_part/pallas_call | solution.py:35
  44.9 0.7 copy-done
  45.6 0.8 convert_element_type.53
  46.4 0.1 copy-done.2
  46.5 1.5 %collective-permute-start.9 = (f16[256,512]{1,0:T(8,128)(2,1)}, f16[256,512]{1,0:T(8,128)(2,1)}, u32[]{:S(2)}, u32[]{:S(2)}) collective-permute-start(f16[256,512]{1,0:T(8,128)(2,1)} %convert_element_type.53), channel_id=1, source_target_pairs={{0,8},{4,12},{8,0},{12,4},{1,9},{5,13},{9,1},{13,5},{2,10},{6,14},... | collective-permute-start | bytes 786440 | tf_op jit(solution)/shard_map/ppermute | solution.py:261
  48.0 0.1 select_reduce_fusion
  48.0 0.0 collective-permute-done.12
  48.1 0.1 add_multiply_fusion
  48.1 0.0 collective-permute-start.8
  48.2 0.9 %copy-done.1 = bf16[256,512]{1,0:T(8,128)(2,1)S(1)} copy-done((bf16[256,512]{1,0:T(8,128)(2,1)S(1)}, bf16[256,512]{1,0:T(8,128)(2,1)}, u32[]{:S(2)}) %copy-start.1) | copy-done | bytes 262168
  49.1 2.3 %states_part.3 = f32[256,512]{1,0:T(8,128)S(1)} custom-call(s32[4]{0:T(128)S(1)} %pad_add_fusion.1.columns_ref, bf16[256,1024]{1,0:T(8,128)(2,1)S(1)} %get-tuple-element.26.refs_0_, bf16[256,1024]{1,0:T(8,128)(2,1)} %get-tuple-element.28.refs_1_, bf16[768,512]{1,0:T(8,128)(2,1)S(1)} %constant_dynamic-update-slice_fusion.refs_1_.refs_2_, ...), custom_call_target="tpu_custom_call" | custom-call | flops 1 | bytes 1 | tf_op jit(solution)/shard_map/states_part/pallas_call | solution.py:35
  51.4 1.8 %collective-permute-done.9 = f16[256,512]{1,0:T(8,128)(2,1)} collective-permute-done((f16[256,512]{1,0:T(8,128)(2,1)}, f16[256,512]{1,0:T(8,128)(2,1)}, u32[]{:S(2)}, u32[]{:S(2)}) %collective-permute-start.9) | collective-permute-done | bytes 262176 | tf_op jit(solution)/shard_map/ppermute | solution.py:261
  53.2 0.0 copy-done.4
  53.2 1.1 %divide_convert_fusion.refs_0_ = bf16[256,512]{1,0:T(8,128)(2,1)S(1)} fusion(f32[256,512]{1,0:T(8,128)S(1)} %states_part.3, f16[256,512]{1,0:T(8,128)(2,1)} %collective-permute-done.9, f32[272,512]{1,0:T(8,128)S(1)} %copy-done.4, f32[256]{0:T(256)S(1)} %add_multiply_fusion, f32[256]{0:T(256)S(1)} %bitcast.11), kind=kLoop, calls=%fused_computation.3 | loop fusion | flops 917504 | bytes 1574912 | tf_op jit(solution)/shard_map/convert_element_type | solution.py:363
  54.3 1.6 %collective-permute-start.13 = (bf16[256,512]{1,0:T(8,128)(2,1)S(1)}, bf16[256,512]{1,0:T(8,128)(2,1)S(1)}, u32[]{:S(2)}, u32[]{:S(2)}) collective-permute-start(bf16[256,512]{1,0:T(8,128)(2,1)S(1)} %divide_convert_fusion.refs_0_), channel_id=1, source_target_pairs={{0,8},{4,12},{8,0},{12,4},{1,9},{5,13},{9,1},{13,5},{2,10},{6,14},... | collective-permute-start | bytes 786440 | tf_op jit(solution)/shard_map/ppermute | solution.py:261
  55.8 0.0 collective-permute-start.14
  55.8 5.5 %collective-permute-done.13.refs_1_ = bf16[256,512]{1,0:T(8,128)(2,1)S(1)} collective-permute-done((bf16[256,512]{1,0:T(8,128)(2,1)S(1)}, bf16[256,512]{1,0:T(8,128)(2,1)S(1)}, u32[]{:S(2)}, u32[]{:S(2)}) %collective-permute-start.13) | collective-permute-done | bytes 262176 | tf_op jit(solution)/shard_map/ppermute | solution.py:261
  61.3 0.0 collective-permute-start.15
  61.3 0.1 pad_add_fusion.columns_ref
  61.4 0.0 collective-permute-done.1.refs_2_
  61.4 0.0 collective-permute-done.8.refs_3_
  61.4 2.2 %turned.1.held_ref = bf16[1024,1024]{1,0:T(8,128)(2,1)S(1)} custom-call(s32[4]{0:T(128)S(1)} %pad_add_fusion.columns_ref, bf16[256,1024]{1,0:T(8,128)(2,1)S(1)} %get-tuple-element.26.refs_0_, bf16[512,1024]{1,0:T(8,128)(2,1)S(1)} %collective-permute-done.refs_0_.refs_1_, bf16[256,1024]{1,0:T(8,128)(2,1)} %collective-permute-done.1.refs_2_, ...), custom_call_target="tpu_custom_call" | custom-call | flops 1 | bytes 1 | tf_op jit(solution)/shard_map/turned/pallas_call | solution.py:35
  63.6 0.0 collective-permute-done.14.refs_2_
  63.6 0.0 collective-permute-done.15.refs_3_
  63.6 1.2 %gradient_blocks.1 = (bf16[256,512]{1,0:T(8,128)(2,1)S(1)}, bf16[256,512]{1,0:T(8,128)(2,1)S(1)}, bf16[256,512]{1,0:T(8,128)(2,1)S(1)}, f32[256,512]{1,0:T(8,128)S(1)}) custom-call(s32[1]{0:T(128)} %constant.22.clone.1._, bf16[1024,1024]{1,0:T(8,128)(2,1)S(1)} %turned.1.held_ref, bf16[256,512]{1,0:T(8,128)(2,1)S(1)} %divide_convert_fusion.refs_0_, ...), custom_call_target="tpu_custom_call" | custom-call | flops 1 | bytes 1 | tf_op jit(solution)/shard_map/gradient_blocks/pallas_call | solution.py:35
  64.9 0.1 collective-permute-start.16
  65.0 2.1 %collective-permute-start.17 = (bf16[256,512]{1,0:T(8,128)(2,1)S(1)}, bf16[256,512]{1,0:T(8,128)(2,1)S(1)}, u32[]{:S(2)}, u32[]{:S(2)}) collective-permute-start(bf16[256,512]{1,0:T(8,128)(2,1)S(1)} %get-tuple-element.45), channel_id=1, source_target_pairs={{0,2},{1,3},{2,0},{3,1},{4,6},{5,7},{6,4},{7,5},{8,10},{9,11},{10,... | collective-permute-start | bytes 786440 | tf_op jit(solution)/shard_map/ppermute | solution.py:261
  67.0 1.4 %collective-permute-start.18 = (bf16[256,512]{1,0:T(8,128)(2,1)S(1)}, bf16[256,512]{1,0:T(8,128)(2,1)S(1)}, u32[]{:S(2)}, u32[]{:S(2)}) collective-permute-start(bf16[256,512]{1,0:T(8,128)(2,1)S(1)} %get-tuple-element.46), channel_id=1, source_target_pairs={{0,3},{1,2},{2,1},{3,0},{4,7},{5,6},{6,5},{7,4},{8,11},{9,10},{10,... | collective-permute-start | bytes 786440 | tf_op jit(solution)/shard_map/ppermute | solution.py:261
  68.4 7.6 %collective-permute-done.16 = bf16[256,512]{1,0:T(8,128)(2,1)S(1)} collective-permute-done((bf16[256,512]{1,0:T(8,128)(2,1)S(1)}, bf16[256,512]{1,0:T(8,128)(2,1)S(1)}, u32[]{:S(2)}, u32[]{:S(2)}) %collective-permute-start.16) | collective-permute-done | bytes 262176 | tf_op jit(solution)/shard_map/ppermute | solution.py:261
  76.0 9.0 %collective-permute-done.17 = bf16[256,512]{1,0:T(8,128)(2,1)S(1)} collective-permute-done((bf16[256,512]{1,0:T(8,128)(2,1)S(1)}, bf16[256,512]{1,0:T(8,128)(2,1)S(1)}, u32[]{:S(2)}, u32[]{:S(2)}) %collective-permute-start.17) | collective-permute-done | bytes 262176 | tf_op jit(solution)/shard_map/ppermute | solution.py:261
  85.0 6.8 %collective-permute-done.18 = bf16[256,512]{1,0:T(8,128)(2,1)S(1)} collective-permute-done((bf16[256,512]{1,0:T(8,128)(2,1)S(1)}, bf16[256,512]{1,0:T(8,128)(2,1)S(1)}, u32[]{:S(2)}, u32[]{:S(2)}) %collective-permute-start.18) | collective-permute-done | bytes 262176 | tf_op jit(solution)/shard_map/ppermute | solution.py:261
  91.8 0.9 convert_add_fusion.1
  (13 shorter events, 0.2 us)
Async XLA Ops:
  0.0 13.5 %collective-permute-start.2 = (bf16[256,512]{1,0:T(8,128)(2,1)}, bf16[256,512]{1,0:T(8,128)(2,1)S(1)}, u32[]{:S(2)}, u32[]{:S(2)}) collective-permute-start(bf16[256,512]{1,0:T(8,128)(2,1)} %param.12), channel_id=1, source_target_pairs={{0,1},{1,0},{2,3},{3,2},{4,5},{5,4},{6,7},{7,6},{8,9},{9,8},{10,11... | collective-permute-start | bytes 786440 | tf_op jit(solution)/shard_map/ppermute | solution.py:261
  0.0 15.0 %collective-permute-start.3 = (bf16[256,512]{1,0:T(8,128)(2,1)}, bf16[256,512]{1,0:T(8,128)(2,1)S(1)}, u32[]{:S(2)}, u32[]{:S(2)}) collective-permute-start(bf16[256,512]{1,0:T(8,128)(2,1)} %param.12), channel_id=1, source_target_pairs={{0,2},{1,3},{2,0},{3,1},{4,6},{5,7},{6,4},{7,5},{8,10},{9,11},{10,... | collective-permute-start | bytes 786440 | tf_op jit(solution)/shard_map/ppermute | solution.py:261
  11.8 8.3 %copy-start.5 = (bf16[256,512]{1,0:T(8,128)(2,1)S(1)}, bf16[256,512]{1,0:T(8,128)(2,1)}, u32[]{:S(2)}) copy-start(bf16[256,512]{1,0:T(8,128)(2,1)} %param.12) | copy-start | bytes 786436
  11.8 16.7 %copy-start.6 = (s32[1,1024]{1,0:T(1,128)S(1)}, s32[1,1024]{1,0:T(1,128)}, u32[]{:S(2)}) copy-start(s32[1,1024]{1,0:T(1,128)} %param.13) | copy-start | bytes 12292
  11.8 31.8 %collective-permute-start = (bf16[512,1024]{1,0:T(8,128)(2,1)S(1)}, bf16[512,1024]{1,0:T(8,128)(2,1)S(1)}, u32[]{:S(2)}, u32[]{:S(2)}) collective-permute-start(bf16[512,1024]{1,0:T(8,128)(2,1)S(1)} %get-tuple-element.27), channel_id=1, source_target_pairs={{0,8},{4,12},{8,0},{12,4},{1,9},{5,13},{9,1},{13,5},{2,10},{6,14},... | collective-permute-start | bytes 3145736 | tf_op jit(solution)/shard_map/ppermute | solution.py:261
  15.0 13.4 %collective-permute-start.4 = (bf16[256,512]{1,0:T(8,128)(2,1)S(1)}, bf16[256,512]{1,0:T(8,128)(2,1)S(1)}, u32[]{:S(2)}, u32[]{:S(2)}) collective-permute-start(bf16[256,512]{1,0:T(8,128)(2,1)S(1)} %collective-permute-done.3), channel_id=1, source_target_pairs={{0,1},{1,0},{2,3},{3,2},{4,5},{5,4},{6,7},{7,6},{8,9},{9,8},{10,11... | collective-permute-start | bytes 786440 | tf_op jit(solution)/shard_map/ppermute | solution.py:261
  16.6 16.8 %collective-permute-start.5 = (f16[272,512]{1,0:T(8,128)(2,1)S(1)}, f16[272,512]{1,0:T(8,128)(2,1)S(1)}, u32[]{:S(2)}, u32[]{:S(2)}) collective-permute-start(f16[272,512]{1,0:T(8,128)(2,1)S(1)} %convert_element_type.50), channel_id=1, source_target_pairs={{0,1},{1,0},{2,3},{3,2},{4,5},{5,4},{6,7},{7,6},{8,9},{9,8},{10,11... | collective-permute-start | bytes 835592 | tf_op jit(solution)/shard_map/ppermute | solution.py:261
  17.0 19.9 %collective-permute-start.10 = (f16[272,512]{1,0:T(8,128)(2,1)S(1)}, f16[272,512]{1,0:T(8,128)(2,1)S(1)}, u32[]{:S(2)}, u32[]{:S(2)}) collective-permute-start(f16[272,512]{1,0:T(8,128)(2,1)S(1)} %convert_element_type.51), channel_id=1, source_target_pairs={{0,2},{1,3},{2,0},{3,1},{4,6},{5,7},{6,4},{7,5},{8,10},{9,11},{10,... | collective-permute-start | bytes 835592 | tf_op jit(solution)/shard_map/ppermute | solution.py:261
  19.7 21.9 %collective-permute-start.11 = (f16[272,512]{1,0:T(8,128)(2,1)S(1)}, f16[272,512]{1,0:T(8,128)(2,1)S(1)}, u32[]{:S(2)}, u32[]{:S(2)}) collective-permute-start(f16[272,512]{1,0:T(8,128)(2,1)S(1)} %convert_element_type.52), channel_id=1, source_target_pairs={{0,3},{1,2},{2,1},{3,0},{4,7},{5,6},{6,5},{7,4},{8,11},{9,10},{10,... | collective-permute-start | bytes 835592 | tf_op jit(solution)/shard_map/ppermute | solution.py:261
  28.4 15.2 %collective-permute-start.6 = (bf16[768,512]{1,0:T(8,128)(2,1)S(1)}, bf16[768,512]{1,0:T(8,128)(2,1)S(1)}, u32[]{:S(2)}, u32[]{:S(2)}) collective-permute-start(bf16[768,512]{1,0:T(8,128)(2,1)S(1)} %constant_dynamic-update-slice_fusion.refs_1_.refs_2_), channel_id=1, source_target_pairs={{0,4},{4,0},{8,12},{12,8},{1,5},{5,1},{9,13},{13,9},{2,6},{6,2},{1... | collective-permute-start | bytes 2359304 | tf_op jit(solution)/shard_map/ppermute | solution.py:261
  33.4 28.0 %collective-permute-start.1 = (bf16[256,1024]{1,0:T(8,128)(2,1)}, bf16[256,1024]{1,0:T(8,128)(2,1)}, u32[]{:S(2)}, u32[]{:S(2)}) collective-permute-start(bf16[256,1024]{1,0:T(8,128)(2,1)} %get-tuple-element.28.refs_1_), channel_id=1, source_target_pairs={{0,4},{4,0},{8,12},{12,8},{1,5},{5,1},{9,13},{13,9},{2,6},{6,2},{1... | collective-permute-start | bytes 1572872 | tf_op jit(solution)/shard_map/ppermute | solution.py:261
  36.9 6.7 %collective-permute-start.7 = (bf16[256,512]{1,0:T(8,128)(2,1)S(1)}, bf16[256,512]{1,0:T(8,128)(2,1)S(1)}, u32[]{:S(2)}, u32[]{:S(2)}) collective-permute-start(bf16[256,512]{1,0:T(8,128)(2,1)S(1)} %collective-permute-done.4.refs_2_.refs_3_), channel_id=1, source_target_pairs={{0,4},{4,0},{8,12},{12,8},{1,5},{5,1},{9,13},{13,9},{2,6},{6,2},{1... | collective-permute-start | bytes 786440 | tf_op jit(solution)/shard_map/ppermute | solution.py:261
  41.8 1.8 %copy-start.3 = (f32[272,512]{1,0:T(8,128)}, f32[272,512]{1,0:T(8,128)S(1)}, u32[]{:S(2)}) copy-start(f32[272,512]{1,0:T(8,128)S(1)} %convert_add_fusion) | copy-start | bytes 1671172
  42.0 6.0 %collective-permute-start.12 = (f32[256]{0:T(256)S(1)}, f32[256]{0:T(256)S(1)}, u32[]{:S(2)}, u32[]{:S(2)}) collective-permute-start(f32[256]{0:T(256)S(1)} %multiply_reduce_fusion), channel_id=1, source_target_pairs={{0,16},{16,0},{1,17},{17,1},{2,18},{18,2},{3,19},{19,3},{4,20},{20... | collective-permute-start | bytes 3080 | tf_op jit(solution)/shard_map/ppermute | solution.py:261
  44.9 0.7 copy-start
  45.6 0.9 copy-start.2
  46.5 6.7 %collective-permute-start.9 = (f16[256,512]{1,0:T(8,128)(2,1)}, f16[256,512]{1,0:T(8,128)(2,1)}, u32[]{:S(2)}, u32[]{:S(2)}) collective-permute-start(f16[256,512]{1,0:T(8,128)(2,1)} %convert_element_type.53), channel_id=1, source_target_pairs={{0,8},{4,12},{8,0},{12,4},{1,9},{5,13},{9,1},{13,5},{2,10},{6,14},... | collective-permute-start | bytes 786440 | tf_op jit(solution)/shard_map/ppermute | solution.py:261
  48.1 13.3 %collective-permute-start.8 = (bf16[256,1024]{1,0:T(8,128)(2,1)}, bf16[256,1024]{1,0:T(8,128)(2,1)S(1)}, u32[]{:S(2)}, u32[]{:S(2)}) collective-permute-start(bf16[256,1024]{1,0:T(8,128)(2,1)} %copy-done.2), channel_id=1, source_target_pairs={{0,4},{4,0},{8,12},{12,8},{1,5},{5,1},{9,13},{13,9},{2,6},{6,2},{1... | collective-permute-start | bytes 1572872 | tf_op jit(solution)/shard_map/ppermute | solution.py:261
  48.2 1.0 %copy-start.1 = (bf16[256,512]{1,0:T(8,128)(2,1)S(1)}, bf16[256,512]{1,0:T(8,128)(2,1)}, u32[]{:S(2)}) copy-start(bf16[256,512]{1,0:T(8,128)(2,1)} %copy-done) | copy-start | bytes 786436
  49.1 4.1 %copy-start.4 = (f32[272,512]{1,0:T(8,128)S(1)}, f32[272,512]{1,0:T(8,128)}, u32[]{:S(2)}) copy-start(f32[272,512]{1,0:T(8,128)} %copy-done.3) | copy-start | bytes 1671172
  54.3 7.0 %collective-permute-start.13 = (bf16[256,512]{1,0:T(8,128)(2,1)S(1)}, bf16[256,512]{1,0:T(8,128)(2,1)S(1)}, u32[]{:S(2)}, u32[]{:S(2)}) collective-permute-start(bf16[256,512]{1,0:T(8,128)(2,1)S(1)} %divide_convert_fusion.refs_0_), channel_id=1, source_target_pairs={{0,8},{4,12},{8,0},{12,4},{1,9},{5,13},{9,1},{13,5},{2,10},{6,14},... | collective-permute-start | bytes 786440 | tf_op jit(solution)/shard_map/ppermute | solution.py:261
  55.8 7.8 %collective-permute-start.14 = (bf16[256,512]{1,0:T(8,128)(2,1)S(1)}, bf16[256,512]{1,0:T(8,128)(2,1)S(1)}, u32[]{:S(2)}, u32[]{:S(2)}) collective-permute-start(bf16[256,512]{1,0:T(8,128)(2,1)S(1)} %divide_convert_fusion.refs_0_), channel_id=1, source_target_pairs={{0,4},{4,0},{8,12},{12,8},{1,5},{5,1},{9,13},{13,9},{2,6},{6,2},{1... | collective-permute-start | bytes 786440 | tf_op jit(solution)/shard_map/ppermute | solution.py:261
  61.3 2.3 %collective-permute-start.15 = (bf16[256,512]{1,0:T(8,128)(2,1)S(1)}, bf16[256,512]{1,0:T(8,128)(2,1)S(1)}, u32[]{:S(2)}, u32[]{:S(2)}) collective-permute-start(bf16[256,512]{1,0:T(8,128)(2,1)S(1)} %collective-permute-done.13.refs_1_), channel_id=1, source_target_pairs={{0,4},{4,0},{8,12},{12,8},{1,5},{5,1},{9,13},{13,9},{2,6},{6,2},{1... | collective-permute-start | bytes 786440 | tf_op jit(solution)/shard_map/ppermute | solution.py:261
  64.9 11.1 %collective-permute-start.16 = (bf16[256,512]{1,0:T(8,128)(2,1)S(1)}, bf16[256,512]{1,0:T(8,128)(2,1)S(1)}, u32[]{:S(2)}, u32[]{:S(2)}) collective-permute-start(bf16[256,512]{1,0:T(8,128)(2,1)S(1)} %get-tuple-element.44), channel_id=1, source_target_pairs={{0,1},{1,0},{2,3},{3,2},{4,5},{5,4},{6,7},{7,6},{8,9},{9,8},{10,11... | collective-permute-start | bytes 786440 | tf_op jit(solution)/shard_map/ppermute | solution.py:261
  65.0 20.0 %collective-permute-start.17 = (bf16[256,512]{1,0:T(8,128)(2,1)S(1)}, bf16[256,512]{1,0:T(8,128)(2,1)S(1)}, u32[]{:S(2)}, u32[]{:S(2)}) collective-permute-start(bf16[256,512]{1,0:T(8,128)(2,1)S(1)} %get-tuple-element.45), channel_id=1, source_target_pairs={{0,2},{1,3},{2,0},{3,1},{4,6},{5,7},{6,4},{7,5},{8,10},{9,11},{10,... | collective-permute-start | bytes 786440 | tf_op jit(solution)/shard_map/ppermute | solution.py:261
  67.0 24.7 %collective-permute-start.18 = (bf16[256,512]{1,0:T(8,128)(2,1)S(1)}, bf16[256,512]{1,0:T(8,128)(2,1)S(1)}, u32[]{:S(2)}, u32[]{:S(2)}) collective-permute-start(bf16[256,512]{1,0:T(8,128)(2,1)S(1)} %get-tuple-element.46), channel_id=1, source_target_pairs={{0,3},{1,2},{2,1},{3,0},{4,7},{5,6},{6,5},{7,4},{8,11},{9,10},{10,... | collective-permute-start | bytes 786440 | tf_op jit(solution)/shard_map/ppermute | solution.py:261

commit v3 on v2

--- a/solution.py
+++ b/solution.py
@@ -25,22 +25,27 @@
 
 VMEM_BYTES = 24 * 2**20
 SQUARE_FACTOR = 1024.0
-EXTRA_ROWS = 16
-
-
-def call(kernel, scalars, arrays, in_hbm, out, scratch, name):
+EXTRA_ROWS = 8
+
+
+def call(kernel, scalars, arrays, in_hbm, out, scratch, name, out_hbm=()):
     arrays = [pltpu.with_memory_space_constraint(a, pltpu.HBM) for a in arrays[:in_hbm]] + list(
         arrays[in_hbm:]
     )
     return pl.pallas_call(
         kernel,
-        out_shape=[pltpu.VMEM(shape, dtype) for shape, dtype in out],
+        out_shape=[
+            (pltpu.HBM if n in out_hbm else pltpu.VMEM)(*leaf) for n, leaf in enumerate(out)
+        ],
         grid_spec=pltpu.PrefetchScalarGridSpec(
             num_scalar_prefetch=1,
             grid=(),
             in_specs=[pl.BlockSpec(memory_space=pltpu.HBM)] * in_hbm
             + [pl.BlockSpec(memory_space=pltpu.VMEM)] * (len(arrays) - in_hbm),
-            out_specs=[pl.BlockSpec(memory_space=pltpu.VMEM)] * len(out),
+            out_specs=[
+                pl.BlockSpec(memory_space=pltpu.HBM if n in out_hbm else pltpu.VMEM)
+                for n in range(len(out))
+            ],
             scratch_shapes=scratch,
         ),
         compiler_params=pltpu.CompilerParams(vmem_limit_bytes=VMEM_BYTES),
@@ -171,9 +176,9 @@
     return results[:cores], results[cores:shared], results[shared:]
 
 
-def states_part(columns, features, values, rows, factor):
-    cores = len(values)
-    tok, wide = features[0].shape[0] * len(features) // cores, features[0].shape[1]
+def states_parts(columns, features, values, rows, factor):
+    cores, chips = len(values), len(features)
+    tok, wide = features[0][0].shape
     kv = values[0][0].shape[1]
     flat = [v for of_core in values for v in of_core]
     spots = [
@@ -184,36 +189,59 @@
     ]
     each = len(values[0])
     per_core = len(spots) // cores
-    place = [(h, 0) if len(features) == cores else (0, h * tok) for h in range(cores)]
-    alone = len(features) < cores
+    arrays = [part for of_chip in features for part in of_chip]
+    place, first = [], 0
+    for of_chip in features:
+        split = len(of_chip) == cores
+        place.append([(first + h, 0) if split else (first, h * tok) for h in range(cores)])
+        first += len(of_chip)
+    alone = [first for first, of_chip in enumerate(features) if len(of_chip) < cores]
     if rows % 128:
-        total = jnp.zeros((tok, kv), jnp.float32)
-        for i, (h, n, b) in enumerate(spots):
-            at = (place[h][1], columns[i % per_core] * rows)
-            part = lax.dynamic_slice(features[place[h][0]], at, (tok, rows))
-            block = lax.slice_in_dim(values[h][n], b * rows, (b + 1) * rows)
-            total += jnp.dot(part, block, preferred_element_type=jnp.float32)
-        return total * factor, features[-1][-tok:]
+        totals = []
+        for j in range(chips):
+            total = jnp.zeros((tok, kv), jnp.float32)
+            for i, (h, n, b) in enumerate(spots):
+                array, above = place[j][h]
+                at = (above, columns[i % per_core] * rows)
+                part = lax.dynamic_slice(arrays[array], at, (tok, rows))
+                block = lax.slice_in_dim(values[h][n], b * rows, (b + 1) * rows)
+                total += jnp.dot(part, block, preferred_element_type=jnp.float32)
+            totals.append(total * factor)
+        return totals, [features[j][-1][-tok:] for j in alone]
 
     def kernel(columns_ref, *refs):
-        feature_refs, refs = refs[: len(features)], refs[len(features) :]
-        value_refs, out_refs = refs[: len(flat)], refs[len(flat) :]
-        total = jnp.zeros((tok, kv), jnp.float32)
-        for i, (h, n, b) in enumerate(spots):
-            start = pl.multiple_of(columns_ref[i % per_core] * rows, rows)
-            array, above = place[h]
-            total += jnp.dot(
-                feature_refs[array][above : above + tok, pl.ds(start, rows)],
-                value_refs[h * each + n][b * rows : (b + 1) * rows, :],
-                preferred_element_type=jnp.float32,
-            )
-        out_refs[0][...] = total * factor
-        if alone:
-            out_refs[1][...] = feature_refs[-1][-tok:, :]
-
-    out = [((tok, kv), jnp.float32)] + [((tok, wide), jnp.bfloat16)] * alone
-    results = call(kernel, columns, [*features, *flat], 0, out, [], "states_part")
-    return results[0], results[1] if alone else features[-1]
+        feature_refs, refs = refs[: len(arrays)], refs[len(arrays) :]
+        value_refs, refs = refs[: len(flat)], refs[len(flat) :]
+        out_refs, (own_ref, sems) = refs[:-2], refs[-2:]
+        copies = []
+        for n, j in enumerate(alone):
+            src = feature_refs[place[j][0][0]].at[pl.ds((cores - 1) * tok, tok)]
+            copies.append(pltpu.make_async_copy(src, out_refs[chips + n], sems.at[1 + n]))
+            copies[-1].start()
+        for j in range(chips):
+            total = jnp.zeros((tok, kv), jnp.float32)
+            for i, (h, n, b) in enumerate(spots):
+                start = pl.multiple_of(columns_ref[i % per_core] * rows, rows)
+                array, above = place[j][h]
+                total += jnp.dot(
+                    feature_refs[array][above : above + tok, pl.ds(start, rows)],
+                    value_refs[h * each + n][b * rows : (b + 1) * rows, :],
+                    preferred_element_type=jnp.float32,
+                )
+            if j:
+                out_refs[j][...] = total * factor
+            else:
+                own_ref[...] = total * factor
+                copies.append(pltpu.make_async_copy(own_ref, out_refs[0], sems.at[0]))
+                copies[-1].start()
+        for copy in copies:
+            copy.wait()
+
+    out = [((tok, kv), jnp.float32)] * chips + [((tok, wide), jnp.bfloat16)] * len(alone)
+    scratch = [pltpu.VMEM((tok, kv), jnp.float32), pltpu.SemaphoreType.DMA((1 + len(alone),))]
+    out_hbm = (0, *range(chips, len(out)))
+    results = call(kernel, columns, [*arrays, *flat], 0, out, scratch, "states_parts", out_hbm)
+    return results[:chips], results[chips:]
 
 
 def turned(columns, blocks, rows):
@@ -231,7 +259,7 @@
     return call(kernel, columns, blocks, 0, out, [], "turned")[0]
 
 
-def gradient_blocks(held, seen, number):
+def gradient_blocks(held, seen, number, rounded):
     rows, tok = held.shape[0] // number, seen[0].shape[0]
     kv = seen[0].shape[1]
 
@@ -247,7 +275,7 @@
                 )
             out_ref[...] = total.astype(out_ref.dtype)
 
-    out = [((rows, kv), jnp.bfloat16)] * (number - 1) + [((rows, kv), jnp.float32)]
+    out = [((rows, kv), jnp.bfloat16)] * rounded + [((rows, kv), jnp.float32)] * (number - rounded)
     return call(kernel, jnp.zeros(1), [held, *seen], 0, out, [], "gradient_blocks")
 
 
@@ -323,18 +351,25 @@
 
         columns = jnp.stack([member ^ o for o in first + later])
         states_factor = half_scale(GAIN_MAX * ds * STUDENT_VALUE_MAX)
-        returned = [
-            states_part(columns, [part], gathered, rows, states_factor) for part in others
-        ]
-        second = [part[1] for part in returned]
-        returned = [part[0].astype(f16) for part in returned]
+        (states, *returned), second = states_parts(
+            columns, [own] + [[part] for part in others], gathered, rows, states_factor
+        )
+        if cores == 1:
+            second = others
+        returned = payload = [part.astype(f16) for part in returned]
         returned = [swap(part, "dp", cores * (j + 1)) for j, part in enumerate(returned)]
-        states, _ = states_part(columns, own, gathered, rows, states_factor)
 
         held = [own[0], *others]
         if cores == 2:
             held += [swap(part, "dp", 1) for part in [own[1], *second]]
-        turn_order = jnp.stack([member ^ k for k in order])
+        line = mp == 4
+        if line:
+            inner = (member == 1) | (member == 2)
+            turn_order = [(1, 3), (3, 2), (2, 1), (0, 0)]
+            turn_order = [member ^ jnp.where(inner, i, o) for i, o in turn_order]
+        else:
+            turn_order = [member ^ k for k in order]
+        turn_order = jnp.stack(turn_order)
         if rows % 128 == 0:
             held = turned(turn_order, held, rows)
 
@@ -347,6 +382,7 @@
         projected = summed[:tok] * (1.0 / teacher_factor)
         target = projected * teacher_scale[:, None]
         power_half = jnp.sum(target * target, axis=1)
+        power_half, payload = lax.optimization_barrier((power_half, payload))
         power = power_half
         for k in range(1, grp):
             power = power + swap(power_half, "grp", k)
@@ -362,9 +398,12 @@
         doc_length = lax.dynamic_slice_in_dim(lengths, member * tok, tok, 0).astype(f32)
         weighted = ((states - target) / (doc_length * target_power)[:, None]).astype(bf16)
 
-        seen = [weighted] + [swap(weighted, "dp", cores * j) for j in range(1, chips)]
+        seen = [swap(weighted, "dp", cores * j) for j in range(1, chips)]
+        held, seen = lax.optimization_barrier((held, seen))
+        seen = [weighted] + seen
         if cores == 2:
             seen += [swap(part, "dp", 1) for part in seen]
+        rounded = 2 if line else mp - 1
         if rows % 128:
             held = jnp.concatenate([part[:tok] for part in held], axis=0)
             seen = jnp.concatenate(seen, axis=0)
@@ -374,14 +413,24 @@
                     seen,
                     (((0,), (0,)), ((), ())),
                     preferred_element_type=f32,
-                ).astype(bf16 if order[i] else f32)
+                )
                 for i in range(mp)
             ]
+            parts = [p.astype(bf16) for p in parts[:rounded]] + parts[rounded:]
         else:
-            parts = gradient_blocks(held, seen, mp)
-        total = parts[-1]
-        for i in range(mp - 1):
-            total = total + swap(parts[i], "mp", order[i]).astype(f32)
+            parts = gradient_blocks(held, seen, mp, rounded)
+        if line:
+            near = swap(parts[0], "mp", 1).astype(f32)
+            across = lax.ppermute(parts[1], "mp", [(1, 2), (2, 1)])
+            past = lax.ppermute(parts[1], "mp", [(0, 2), (3, 1)])
+            last = (parts[2] + jnp.where(inner, near, 0.0)).astype(bf16)
+            last = lax.ppermute(last, "mp", [(1, 3), (2, 0), (0, 1), (3, 2)])
+            total = parts[3] + jnp.where(inner, 0.0, near)
+            total = total + across.astype(f32) + past.astype(f32) + last.astype(f32)
+        else:
+            total = parts[-1]
+            for i in range(mp - 1):
+                total = total + swap(parts[i], "mp", order[i]).astype(f32)
         return total
 
     return jax.shard_map(

time: 93 us -> 87.9 us (0.945)
  the two profiles are of different devices: /device:TPU:8 before, /device:TPU:0 now
where the time goes in v3:
time: 87.9 us; the launch traced here: 87.7 us
  waiting for transfers between devices  42 us (48%)
  starting transfers between devices  27.1 us (31%)
  Pallas kernels  12.9 us (15%)
  other arithmetic  3.46 us (4%)
  local copies, waits for them, and re-layouts  2.1 us (2%)
    ppermute x17, waiting for transfers between devices, swap(): lax.ppermute(value, axis, [(i, i ^ step) for i in range(sizes[axis])])  30 us
    ppermute x17, starting transfers between devices, swap(): lax.ppermute(value, axis, [(i, i ^ step) for i in range(sizes[axis])])  19.4 us
    pallas_call x4, Pallas kernels, call(): pl.pallas_call(kernel, out_shape=[(pltpu.HBM if n in out_hbm else pltpu.V...  12.9 us
    ppermute x1, waiting for transfers between devices, per_device(): last = lax.ppermute(last, 'mp', [(1, 3), (2, 0), (0, 1), (3, 2)])  8.85 us
    ppermute x1, starting transfers between devices, per_device(): past = lax.ppermute(parts[1], 'mp', [(0, 2), (3, 1)])  4.64 us
    ppermute x1, waiting for transfers between devices, per_device(): past = lax.ppermute(parts[1], 'mp', [(0, 2), (3, 1)])  3.05 us
    ppermute x1, starting transfers between devices, per_device(): last = lax.ppermute(last, 'mp', [(1, 3), (2, 0), (0, 1), (3, 2)])  2.34 us
  transfers between devices with their start and end apart: 20, of which 10 were waited for; matrix products, arithmetic and copies ran while one was open for 5% of the time, Pallas kernels for 12%

profile of v3, /device:TPU:0, one launch (start us, length us, event | category | flops | bytes accessed | tf_op | source)
XLA Modules:
  0.0 87.7 jit_solution(12922782954470436276)
XLA Ops:
  0.0 3.0 %collective-permute-start.2 = (bf16[256,512]{1,0:T(8,128)(2,1)}, bf16[256,512]{1,0:T(8,128)(2,1)S(1)}, u32[]{:S(2)}, u32[]{:S(2)}) collective-permute-start(bf16[256,512]{1,0:T(8,128)(2,1)} %param.12), channel_id=1, source_target_pairs={{0,1},{1,0},{2,3},{3,2},{4,5},{5,4},{6,7},{7,6},{8,9},{9,8},{10,11... | collective-permute-start | bytes 786440 | tf_op jit(solution)/shard_map/ppermute | solution.py:289
  3.0 2.6 %collective-permute-start.3 = (bf16[256,512]{1,0:T(8,128)(2,1)}, bf16[256,512]{1,0:T(8,128)(2,1)S(1)}, u32[]{:S(2)}, u32[]{:S(2)}) collective-permute-start(bf16[256,512]{1,0:T(8,128)(2,1)} %param.12), channel_id=1, source_target_pairs={{0,2},{1,3},{2,0},{3,1},{4,6},{5,7},{6,4},{7,5},{8,10},{9,11},{10,... | collective-permute-start | bytes 786440 | tf_op jit(solution)/shard_map/ppermute | solution.py:289
  5.6 0.7 reshape.138.student_gain_ref
  6.3 0.7 reshape.139.gain_ref
  7.0 0.1 stack.51.places_ref
  7.1 7.3 %prepare.1 = (bf16[256,1024]{1,0:T(8,128)(2,1)S(1)}, bf16[256,1024]{1,0:T(8,128)(2,1)S(1)}, bf16[512,1024]{1,0:T(8,128)(2,1)S(1)}, f32[264,512]{1,0:T(8,128)S(1)...) custom-call(s32[6]{0:T(128)S(1)} %stack.51.places_ref, bf16[256,4096]{1,0:T(8,128)(2,1)} %student_ref.1, ...), custom_call_target="tpu_custom_call" | custom-call | flops 1 | bytes 1 | tf_op jit(solution)/shard_map/prepare/pallas_call | solution.py:35
  14.4 0.0 copy-start.1
  14.4 0.0 copy-start.2
  14.4 1.6 %collective-permute-start = (bf16[512,1024]{1,0:T(8,128)(2,1)S(1)}, bf16[512,1024]{1,0:T(8,128)(2,1)S(1)}, u32[]{:S(2)}, u32[]{:S(2)}) collective-permute-start(bf16[512,1024]{1,0:T(8,128)(2,1)S(1)} %get-tuple-element.31), channel_id=1, source_target_pairs={{0,8},{4,12},{8,0},{12,4},{1,9},{5,13},{9,1},{13,5},{2,10},{6,14},... | collective-permute-start | bytes 3145736 | tf_op jit(solution)/shard_map/ppermute | solution.py:289
  16.1 0.0 collective-permute-done.2
  16.1 1.5 %collective-permute-done.3 = bf16[256,512]{1,0:T(8,128)(2,1)S(1)} collective-permute-done((bf16[256,512]{1,0:T(8,128)(2,1)}, bf16[256,512]{1,0:T(8,128)(2,1)S(1)}, u32[]{:S(2)}, u32[]{:S(2)}) %collective-permute-start.3) | collective-permute-done | bytes 262176 | tf_op jit(solution)/shard_map/ppermute | solution.py:289
  17.6 0.4 collective-permute-start.5
  18.0 1.6 %collective-permute-start.4 = (bf16[256,512]{1,0:T(8,128)(2,1)S(1)}, bf16[256,512]{1,0:T(8,128)(2,1)S(1)}, u32[]{:S(2)}, u32[]{:S(2)}) collective-permute-start(bf16[256,512]{1,0:T(8,128)(2,1)S(1)} %collective-permute-done.3), channel_id=1, source_target_pairs={{0,1},{1,0},{2,3},{3,2},{4,5},{5,4},{6,7},{7,6},{8,9},{9,8},{10,11... | collective-permute-start | bytes 786440 | tf_op jit(solution)/shard_map/ppermute | solution.py:289
  19.6 1.1 %collective-permute-start.10 = (f16[264,512]{1,0:T(8,128)(2,1)S(1)}, f16[264,512]{1,0:T(8,128)(2,1)S(1)}, u32[]{:S(2)}, u32[]{:S(2)}) collective-permute-start(f16[264,512]{1,0:T(8,128)(2,1)S(1)} %convert_element_type.57), channel_id=1, source_target_pairs={{0,2},{1,3},{2,0},{3,1},{4,6},{5,7},{6,4},{7,5},{8,10},{9,11},{10,... | collective-permute-start | bytes 811016 | tf_op jit(solution)/shard_map/ppermute | solution.py:289
  20.7 1.7 %collective-permute-start.11 = (f16[264,512]{1,0:T(8,128)(2,1)S(1)}, f16[264,512]{1,0:T(8,128)(2,1)S(1)}, u32[]{:S(2)}, u32[]{:S(2)}) collective-permute-start(f16[264,512]{1,0:T(8,128)(2,1)S(1)} %convert_element_type.58), channel_id=1, source_target_pairs={{0,3},{1,2},{2,1},{3,0},{4,7},{5,6},{6,5},{7,4},{8,11},{9,10},{10,... | collective-permute-start | bytes 811016 | tf_op jit(solution)/shard_map/ppermute | solution.py:289
  22.4 0.0 copy-done.1
  22.5 14.2 %collective-permute-done.4.refs_4_ = bf16[256,512]{1,0:T(8,128)(2,1)S(1)} collective-permute-done((bf16[256,512]{1,0:T(8,128)(2,1)S(1)}, bf16[256,512]{1,0:T(8,128)(2,1)S(1)}, u32[]{:S(2)}, u32[]{:S(2)}) %collective-permute-start.4) | collective-permute-done | bytes 262176 | tf_op jit(solution)/shard_map/ppermute | solution.py:289
  36.7 0.0 collective-permute-start.6
  36.7 0.1 pad_add_fusion.1.columns_ref
  36.8 0.0 copy-done.2
  36.8 0.1 convert_reduce_fusion
  36.9 0.0 collective-permute-done.5
  36.9 0.6 collective-permute-start.1
  37.5 0.0 collective-permute-done.10
  37.5 0.1 collective-permute-start.7
  37.6 4.4 %collective-permute-done.11 = f16[264,512]{1,0:T(8,128)(2,1)S(1)} collective-permute-done((f16[264,512]{1,0:T(8,128)(2,1)S(1)}, f16[264,512]{1,0:T(8,128)(2,1)S(1)}, u32[]{:S(2)}, u32[]{:S(2)}) %collective-permute-start.11) | collective-permute-done | bytes 270368 | tf_op jit(solution)/shard_map/ppermute | solution.py:289
  41.9 0.2 convert_add_fusion
  42.1 0.0 copy-start
  42.1 0.2 multiply_reduce_fusion
  42.4 0.0 collective-permute-done.7.refs_6_
  42.4 0.0 collective-permute-done.6.refs_5_
  42.4 0.0 collective-permute-done.refs_2_.refs_1_
  42.4 0.5 copy-done
  42.9 2.2 %states_parts.1 = (f32[256,512]{1,0:T(8,128)}, f32[256,512]{1,0:T(8,128)S(1)}, bf16[256,1024]{1,0:T(8,128)(2,1)}) custom-call(s32[4]{0:T(128)S(1)} %pad_add_fusion.1.columns_ref, bf16[256,1024]{1,0:T(8,128)(2,1)S(1)} %get-tuple-element.30.refs_0_, bf16[256,1024]{1,0:T(8,128)(2,1)S(1)} %get-tuple-element.32.refs_1_, ...), custom_call_target="tpu_custom_call" | custom-call | flops 1 | bytes 1 | tf_op jit(solution)/shard_map/states_parts/pallas_call | solution.py:35
  45.2 1.6 %collective-permute-start.9 = (f16[256,512]{1,0:T(8,128)(2,1)S(1)}, f16[256,512]{1,0:T(8,128)(2,1)}, u32[]{:S(2)}, u32[]{:S(2)}) collective-permute-start(f16[256,512]{1,0:T(8,128)(2,1)S(1)} %convert_element_type.59), channel_id=1, source_target_pairs={{0,8},{4,12},{8,0},{12,4},{1,9},{5,13},{9,1},{13,5},{2,10},{6,14},... | collective-permute-start | bytes 786440 | tf_op jit(solution)/shard_map/ppermute | solution.py:289
  46.8 1.5 %collective-permute-start.12 = (f32[256]{0:T(256)S(1)}, f32[256]{0:T(256)S(1)}, u32[]{:S(2)}, u32[]{:S(2)}) collective-permute-start(f32[256]{0:T(256)S(1)} %multiply_reduce_fusion), channel_id=1, source_target_pairs={{0,16},{16,0},{1,17},{17,1},{2,18},{18,2},{3,19},{19,3},{4,20},{20... | collective-permute-start | bytes 3080 | tf_op jit(solution)/shard_map/ppermute | solution.py:289
  48.3 0.1 select_reduce_fusion
  48.4 0.1 collective-permute-start.8
  48.5 1.9 %collective-permute-done.12 = f32[256]{0:T(256)S(1)} collective-permute-done((f32[256]{0:T(256)S(1)}, f32[256]{0:T(256)S(1)}, u32[]{:S(2)}, u32[]{:S(2)}) %collective-permute-start.12) | collective-permute-done | bytes 1056 | tf_op jit(solution)/shard_map/ppermute | solution.py:289
  50.4 0.1 add_multiply_fusion
  50.4 1.3 %collective-permute-done.9 = f16[256,512]{1,0:T(8,128)(2,1)} collective-permute-done((f16[256,512]{1,0:T(8,128)(2,1)S(1)}, f16[256,512]{1,0:T(8,128)(2,1)}, u32[]{:S(2)}, u32[]{:S(2)}) %collective-permute-start.9) | collective-permute-done | bytes 262176 | tf_op jit(solution)/shard_map/ppermute | solution.py:289
  51.8 1.4 %divide_convert_fusion.refs_0_ = bf16[256,512]{1,0:T(8,128)(2,1)S(1)} fusion(f32[256,512]{1,0:T(8,128)} %get-tuple-element.42, f16[256,512]{1,0:T(8,128)(2,1)} %collective-permute-done.9, f32[264,512]{1,0:T(8,128)} %copy-done, f32[256]{0:T(256)S(1)} %add_multiply_fusion, f32[256]{0:T(256)S(1)} %bitcast.14), kind=kLoop, calls=%fused_computation.10 | loop fusion | flops 917504 | bytes 1574912 | tf_op jit(solution)/shard_map/convert_element_type | solution.py:399
  53.2 1.6 %collective-permute-start.13 = (bf16[256,512]{1,0:T(8,128)(2,1)S(1)}, bf16[256,512]{1,0:T(8,128)(2,1)}, u32[]{:S(2)}, u32[]{:S(2)}) collective-permute-start(bf16[256,512]{1,0:T(8,128)(2,1)S(1)} %divide_convert_fusion.refs_0_), channel_id=1, source_target_pairs={{0,8},{4,12},{8,0},{12,4},{1,9},{5,13},{9,1},{13,5},{2,10},{6,14},... | collective-permute-start | bytes 786440 | tf_op jit(solution)/shard_map/ppermute | solution.py:289
  54.8 0.1 pad_add_fusion.columns_ref
  54.9 0.0 collective-permute-start.14
  54.9 0.0 collective-permute-done.1.refs_2_
  54.9 0.0 collective-permute-done.8.refs_3_
  54.9 1.2 %turned.1.held_ref = bf16[1024,1024]{1,0:T(8,128)(2,1)S(1)} custom-call(s32[4]{0:T(128)S(1)} %pad_add_fusion.columns_ref, bf16[256,1024]{1,0:T(8,128)(2,1)S(1)} %get-tuple-element.30.refs_0_, bf16[512,1024]{1,0:T(8,128)(2,1)S(1)} %collective-permute-done.refs_2_.refs_1_, bf16[256,1024]{1,0:T(8,128)(2,1)S(1)} %collective-permute-done.1.refs_2_, ...), custom_call_target="tpu_custom_call" | custom-call | flops 1 | bytes 1 | tf_op jit(solution)/shard_map/turned/pallas_call | solution.py:35
  56.1 3.7 %collective-permute-done.13.refs_1_ = bf16[256,512]{1,0:T(8,128)(2,1)} collective-permute-done((bf16[256,512]{1,0:T(8,128)(2,1)S(1)}, bf16[256,512]{1,0:T(8,128)(2,1)}, u32[]{:S(2)}, u32[]{:S(2)}) %collective-permute-start.13) | collective-permute-done | bytes 262176 | tf_op jit(solution)/shard_map/ppermute | solution.py:289
  59.8 0.0 collective-permute-start.15
  59.8 0.0 collective-permute-done.14.refs_2_
  59.8 1.7 %collective-permute-done.15.refs_3_ = bf16[256,512]{1,0:T(8,128)(2,1)S(1)} collective-permute-done((bf16[256,512]{1,0:T(8,128)(2,1)}, bf16[256,512]{1,0:T(8,128)(2,1)S(1)}, u32[]{:S(2)}, u32[]{:S(2)}) %collective-permute-start.15) | collective-permute-done | bytes 262176 | tf_op jit(solution)/shard_map/ppermute | solution.py:289
  61.5 2.2 %gradient_blocks.1 = (bf16[256,512]{1,0:T(8,128)(2,1)S(1)}, bf16[256,512]{1,0:T(8,128)(2,1)S(1)}, f32[256,512]{1,0:T(8,128)S(1)}, f32[256,512]{1,0:T(8,128)S(1)}) custom-call(s32[1]{0:T(128)} %constant.22.clone.1._, bf16[1024,1024]{1,0:T(8,128)(2,1)S(1)} %turned.1.held_ref, bf16[256,512]{1,0:T(8,128)(2,1)S(1)} %divide_convert_fusion.refs_0_, ...), custom_call_target="tpu_custom_call" | custom-call | flops 1 | bytes 1 | tf_op jit(solution)/shard_map/gradient_blocks/pallas_call | solution.py:35
  63.7 2.1 %collective-permute-start.16 = (bf16[256,512]{1,0:T(8,128)(2,1)S(1)}, bf16[256,512]{1,0:T(8,128)(2,1)S(1)}, u32[]{:S(2)}, u32[]{:S(2)}) collective-permute-start(bf16[256,512]{1,0:T(8,128)(2,1)S(1)} %get-tuple-element.52), channel_id=1, source_target_pairs={{0,1},{1,0},{2,3},{3,2},{4,5},{5,4},{6,7},{7,6},{8,9},{9,8},{10,11... | collective-permute-start | bytes 786440 | tf_op jit(solution)/shard_map/ppermute | solution.py:289
  65.8 0.7 collective-permute-start.17
  66.5 4.6 %collective-permute-start.18 = (bf16[256,512]{1,0:T(8,128)(2,1)S(1)}, bf16[256,512]{1,0:T(8,128)(2,1)S(1)}, u32[]{:S(2)}, u32[]{:S(2)}) collective-permute-start(bf16[256,512]{1,0:T(8,128)(2,1)S(1)} %get-tuple-element.53), channel_id=1, source_target_pairs={{0,2},{3,1},{4,6},{7,5},{8,10},{11,9},{12,14},{15,13},{16,18},{19,... | collective-permute-start | bytes 786440 | tf_op jit(solution)/shard_map/ppermute | solution.py:425
  71.1 1.3 %collective-permute-done.16 = bf16[256,512]{1,0:T(8,128)(2,1)S(1)} collective-permute-done((bf16[256,512]{1,0:T(8,128)(2,1)S(1)}, bf16[256,512]{1,0:T(8,128)(2,1)S(1)}, u32[]{:S(2)}, u32[]{:S(2)}) %collective-permute-start.16) | collective-permute-done | bytes 262176 | tf_op jit(solution)/shard_map/ppermute | solution.py:289
  72.4 0.1 fusion.5
  72.5 2.3 %collective-permute-start.19 = (bf16[256,512]{1,0:T(8,128)(2,1)S(1)}, bf16[256,512]{1,0:T(8,128)(2,1)S(1)}, u32[]{:S(2)}, u32[]{:S(2)}) collective-permute-start(bf16[256,512]{1,0:T(8,128)(2,1)S(1)} %fusion.5), channel_id=1, source_target_pairs={{1,3},{2,0},{0,1},{3,2},{5,7},{6,4},{4,5},{7,6},{9,11},{10,8},{8,9... | collective-permute-start | bytes 786440 | tf_op jit(solution)/shard_map/ppermute | solution.py:427
  74.8 0.0 collective-permute-done.17
  74.8 3.1 %collective-permute-done.18 = bf16[256,512]{1,0:T(8,128)(2,1)S(1)} collective-permute-done((bf16[256,512]{1,0:T(8,128)(2,1)S(1)}, bf16[256,512]{1,0:T(8,128)(2,1)S(1)}, u32[]{:S(2)}, u32[]{:S(2)}) %collective-permute-start.18) | collective-permute-done | bytes 262176 | tf_op jit(solution)/shard_map/ppermute | solution.py:425
  77.9 8.9 %collective-permute-done.19 = bf16[256,512]{1,0:T(8,128)(2,1)S(1)} collective-permute-done((bf16[256,512]{1,0:T(8,128)(2,1)S(1)}, bf16[256,512]{1,0:T(8,128)(2,1)S(1)}, u32[]{:S(2)}, u32[]{:S(2)}) %collective-permute-start.19) | collective-permute-done | bytes 262176 | tf_op jit(solution)/shard_map/ppermute | solution.py:427
  86.7 1.0 %fusion.3 = f32[256,512]{1,0:T(8,128)} fusion(f32[256,512]{1,0:T(8,128)S(1)} %get-tuple-element.51, bf16[256,512]{1,0:T(8,128)(2,1)S(1)} %collective-permute-done.16, bf16[256,512]{1,0:T(8,128)(2,1)S(1)} %collective-permute-done.19, bf16[256,512]{1,0:T(8,128)(2,1)S(1)} %collective-permute-done.18, bf16[256,512]{1,0:T(8,128)(2,1)S(1)} %collective-permute-done.17, ...), kind=kLoop, calls=%fused_computation.6 | loop fusion | flops 1179648 | bytes 2097153 | tf_op jit(solution)/shard_map/add | solution.py:429
  (8 shorter events, 0.2 us)
Async XLA Ops:
  0.0 16.1 %collective-permute-start.2 = (bf16[256,512]{1,0:T(8,128)(2,1)}, bf16[256,512]{1,0:T(8,128)(2,1)S(1)}, u32[]{:S(2)}, u32[]{:S(2)}) collective-permute-start(bf16[256,512]{1,0:T(8,128)(2,1)} %param.12), channel_id=1, source_target_pairs={{0,1},{1,0},{2,3},{3,2},{4,5},{5,4},{6,7},{7,6},{8,9},{9,8},{10,11... | collective-permute-start | bytes 786440 | tf_op jit(solution)/shard_map/ppermute | solution.py:289
  3.0 14.6 %collective-permute-start.3 = (bf16[256,512]{1,0:T(8,128)(2,1)}, bf16[256,512]{1,0:T(8,128)(2,1)S(1)}, u32[]{:S(2)}, u32[]{:S(2)}) collective-permute-start(bf16[256,512]{1,0:T(8,128)(2,1)} %param.12), channel_id=1, source_target_pairs={{0,2},{1,3},{2,0},{3,1},{4,6},{5,7},{6,4},{7,5},{8,10},{9,11},{10,... | collective-permute-start | bytes 786440 | tf_op jit(solution)/shard_map/ppermute | solution.py:289
  14.4 8.0 %copy-start.1 = (bf16[256,512]{1,0:T(8,128)(2,1)S(1)}, bf16[256,512]{1,0:T(8,128)(2,1)}, u32[]{:S(2)}) copy-start(bf16[256,512]{1,0:T(8,128)(2,1)} %param.12) | copy-start | bytes 786436
  14.4 22.4 %copy-start.2 = (s32[1,1024]{1,0:T(1,128)S(1)}, s32[1,1024]{1,0:T(1,128)}, u32[]{:S(2)}) copy-start(s32[1,1024]{1,0:T(1,128)} %param.13) | copy-start | bytes 12292
  14.4 28.0 %collective-permute-start = (bf16[512,1024]{1,0:T(8,128)(2,1)S(1)}, bf16[512,1024]{1,0:T(8,128)(2,1)S(1)}, u32[]{:S(2)}, u32[]{:S(2)}) collective-permute-start(bf16[512,1024]{1,0:T(8,128)(2,1)S(1)} %get-tuple-element.31), channel_id=1, source_target_pairs={{0,8},{4,12},{8,0},{12,4},{1,9},{5,13},{9,1},{13,5},{2,10},{6,14},... | collective-permute-start | bytes 3145736 | tf_op jit(solution)/shard_map/ppermute | solution.py:289
  17.6 19.3 %collective-permute-start.5 = (f16[264,512]{1,0:T(8,128)(2,1)S(1)}, f16[264,512]{1,0:T(8,128)(2,1)S(1)}, u32[]{:S(2)}, u32[]{:S(2)}) collective-permute-start(f16[264,512]{1,0:T(8,128)(2,1)S(1)} %convert_element_type.56), channel_id=1, source_target_pairs={{0,1},{1,0},{2,3},{3,2},{4,5},{5,4},{6,7},{7,6},{8,9},{9,8},{10,11... | collective-permute-start | bytes 811016 | tf_op jit(solution)/shard_map/ppermute | solution.py:289
  18.0 18.7 %collective-permute-start.4 = (bf16[256,512]{1,0:T(8,128)(2,1)S(1)}, bf16[256,512]{1,0:T(8,128)(2,1)S(1)}, u32[]{:S(2)}, u32[]{:S(2)}) collective-permute-start(bf16[256,512]{1,0:T(8,128)(2,1)S(1)} %collective-permute-done.3), channel_id=1, source_target_pairs={{0,1},{1,0},{2,3},{3,2},{4,5},{5,4},{6,7},{7,6},{8,9},{9,8},{10,11... | collective-permute-start | bytes 786440 | tf_op jit(solution)/shard_map/ppermute | solution.py:289
  19.6 17.9 %collective-permute-start.10 = (f16[264,512]{1,0:T(8,128)(2,1)S(1)}, f16[264,512]{1,0:T(8,128)(2,1)S(1)}, u32[]{:S(2)}, u32[]{:S(2)}) collective-permute-start(f16[264,512]{1,0:T(8,128)(2,1)S(1)} %convert_element_type.57), channel_id=1, source_target_pairs={{0,2},{1,3},{2,0},{3,1},{4,6},{5,7},{6,4},{7,5},{8,10},{9,11},{10,... | collective-permute-start | bytes 811016 | tf_op jit(solution)/shard_map/ppermute | solution.py:289
  20.7 21.2 %collective-permute-start.11 = (f16[264,512]{1,0:T(8,128)(2,1)S(1)}, f16[264,512]{1,0:T(8,128)(2,1)S(1)}, u32[]{:S(2)}, u32[]{:S(2)}) collective-permute-start(f16[264,512]{1,0:T(8,128)(2,1)S(1)} %convert_element_type.58), channel_id=1, source_target_pairs={{0,3},{1,2},{2,1},{3,0},{4,7},{5,6},{6,5},{7,4},{8,11},{9,10},{10,... | collective-permute-start | bytes 811016 | tf_op jit(solution)/shard_map/ppermute | solution.py:289
  36.7 5.7 %collective-permute-start.6 = (bf16[768,512]{1,0:T(8,128)(2,1)S(1)}, bf16[768,512]{1,0:T(8,128)(2,1)S(1)}, u32[]{:S(2)}, u32[]{:S(2)}) collective-permute-start(bf16[768,512]{1,0:T(8,128)(2,1)S(1)} %constant_dynamic-update-slice_fusion.refs_3_), channel_id=1, source_target_pairs={{0,4},{4,0},{8,12},{12,8},{1,5},{5,1},{9,13},{13,9},{2,6},{6,2},{1... | collective-permute-start | bytes 2359304 | tf_op jit(solution)/shard_map/ppermute | solution.py:289
  36.9 18.0 %collective-permute-start.1 = (bf16[256,1024]{1,0:T(8,128)(2,1)S(1)}, bf16[256,1024]{1,0:T(8,128)(2,1)S(1)}, u32[]{:S(2)}, u32[]{:S(2)}) collective-permute-start(bf16[256,1024]{1,0:T(8,128)(2,1)S(1)} %get-tuple-element.32.refs_1_), channel_id=1, source_target_pairs={{0,4},{4,0},{8,12},{12,8},{1,5},{5,1},{9,13},{13,9},{2,6},{6,2},{1... | collective-permute-start | bytes 1572872 | tf_op jit(solution)/shard_map/ppermute | solution.py:289
  37.5 4.9 %collective-permute-start.7 = (bf16[256,512]{1,0:T(8,128)(2,1)S(1)}, bf16[256,512]{1,0:T(8,128)(2,1)S(1)}, u32[]{:S(2)}, u32[]{:S(2)}) collective-permute-start(bf16[256,512]{1,0:T(8,128)(2,1)S(1)} %collective-permute-done.4.refs_4_), channel_id=1, source_target_pairs={{0,4},{4,0},{8,12},{12,8},{1,5},{5,1},{9,13},{13,9},{2,6},{6,2},{1... | collective-permute-start | bytes 786440 | tf_op jit(solution)/shard_map/ppermute | solution.py:289
  42.1 0.8 copy-start
  45.2 6.5 %collective-permute-start.9 = (f16[256,512]{1,0:T(8,128)(2,1)S(1)}, f16[256,512]{1,0:T(8,128)(2,1)}, u32[]{:S(2)}, u32[]{:S(2)}) collective-permute-start(f16[256,512]{1,0:T(8,128)(2,1)S(1)} %convert_element_type.59), channel_id=1, source_target_pairs={{0,8},{4,12},{8,0},{12,4},{1,9},{5,13},{9,1},{13,5},{2,10},{6,14},... | collective-permute-start | bytes 786440 | tf_op jit(solution)/shard_map/ppermute | solution.py:289
  46.8 3.6 %collective-permute-start.12 = (f32[256]{0:T(256)S(1)}, f32[256]{0:T(256)S(1)}, u32[]{:S(2)}, u32[]{:S(2)}) collective-permute-start(f32[256]{0:T(256)S(1)} %multiply_reduce_fusion), channel_id=1, source_target_pairs={{0,16},{16,0},{1,17},{17,1},{2,18},{18,2},{3,19},{19,3},{4,20},{20... | collective-permute-start | bytes 3080 | tf_op jit(solution)/shard_map/ppermute | solution.py:289
  48.4 6.5 %collective-permute-start.8 = (bf16[256,1024]{1,0:T(8,128)(2,1)}, bf16[256,1024]{1,0:T(8,128)(2,1)S(1)}, u32[]{:S(2)}, u32[]{:S(2)}) collective-permute-start(bf16[256,1024]{1,0:T(8,128)(2,1)} %get-tuple-element.41), channel_id=1, source_target_pairs={{0,4},{4,0},{8,12},{12,8},{1,5},{5,1},{9,13},{13,9},{2,6},{6,2},{1... | collective-permute-start | bytes 1572872 | tf_op jit(solution)/shard_map/ppermute | solution.py:289
  53.2 6.5 %collective-permute-start.13 = (bf16[256,512]{1,0:T(8,128)(2,1)S(1)}, bf16[256,512]{1,0:T(8,128)(2,1)}, u32[]{:S(2)}, u32[]{:S(2)}) collective-permute-start(bf16[256,512]{1,0:T(8,128)(2,1)S(1)} %divide_convert_fusion.refs_0_), channel_id=1, source_target_pairs={{0,8},{4,12},{8,0},{12,4},{1,9},{5,13},{9,1},{13,5},{2,10},{6,14},... | collective-permute-start | bytes 786440 | tf_op jit(solution)/shard_map/ppermute | solution.py:289
  54.9 4.9 %collective-permute-start.14 = (bf16[256,512]{1,0:T(8,128)(2,1)S(1)}, bf16[256,512]{1,0:T(8,128)(2,1)S(1)}, u32[]{:S(2)}, u32[]{:S(2)}) collective-permute-start(bf16[256,512]{1,0:T(8,128)(2,1)S(1)} %divide_convert_fusion.refs_0_), channel_id=1, source_target_pairs={{0,4},{4,0},{8,12},{12,8},{1,5},{5,1},{9,13},{13,9},{2,6},{6,2},{1... | collective-permute-start | bytes 786440 | tf_op jit(solution)/shard_map/ppermute | solution.py:289
  59.8 1.7 %collective-permute-start.15 = (bf16[256,512]{1,0:T(8,128)(2,1)}, bf16[256,512]{1,0:T(8,128)(2,1)S(1)}, u32[]{:S(2)}, u32[]{:S(2)}) collective-permute-start(bf16[256,512]{1,0:T(8,128)(2,1)} %collective-permute-done.13.refs_1_), channel_id=1, source_target_pairs={{0,4},{4,0},{8,12},{12,8},{1,5},{5,1},{9,13},{13,9},{2,6},{6,2},{1... | collective-permute-start | bytes 786440 | tf_op jit(solution)/shard_map/ppermute | solution.py:289
  63.7 8.7 %collective-permute-start.16 = (bf16[256,512]{1,0:T(8,128)(2,1)S(1)}, bf16[256,512]{1,0:T(8,128)(2,1)S(1)}, u32[]{:S(2)}, u32[]{:S(2)}) collective-permute-start(bf16[256,512]{1,0:T(8,128)(2,1)S(1)} %get-tuple-element.52), channel_id=1, source_target_pairs={{0,1},{1,0},{2,3},{3,2},{4,5},{5,4},{6,7},{7,6},{8,9},{9,8},{10,11... | collective-permute-start | bytes 786440 | tf_op jit(solution)/shard_map/ppermute | solution.py:289
  65.8 9.0 %collective-permute-start.17 = (bf16[256,512]{1,0:T(8,128)(2,1)S(1)}, bf16[256,512]{1,0:T(8,128)(2,1)S(1)}, u32[]{:S(2)}, u32[]{:S(2)}) collective-permute-start(bf16[256,512]{1,0:T(8,128)(2,1)S(1)} %get-tuple-element.53), channel_id=1, source_target_pairs={{1,2},{2,1},{5,6},{6,5},{9,10},{10,9},{13,14},{14,13},{17,18},{18,... | collective-permute-start | bytes 786440 | tf_op jit(solution)/shard_map/ppermute | solution.py:424
  66.5 11.4 %collective-permute-start.18 = (bf16[256,512]{1,0:T(8,128)(2,1)S(1)}, bf16[256,512]{1,0:T(8,128)(2,1)S(1)}, u32[]{:S(2)}, u32[]{:S(2)}) collective-permute-start(bf16[256,512]{1,0:T(8,128)(2,1)S(1)} %get-tuple-element.53), channel_id=1, source_target_pairs={{0,2},{3,1},{4,6},{7,5},{8,10},{11,9},{12,14},{15,13},{16,18},{19,... | collective-permute-start | bytes 786440 | tf_op jit(solution)/shard_map/ppermute | solution.py:425
  72.5 14.2 %collective-permute-start.19 = (bf16[256,512]{1,0:T(8,128)(2,1)S(1)}, bf16[256,512]{1,0:T(8,128)(2,1)S(1)}, u32[]{:S(2)}, u32[]{:S(2)}) collective-permute-start(bf16[256,512]{1,0:T(8,128)(2,1)S(1)} %fusion.5), channel_id=1, source_target_pairs={{1,3},{2,0},{0,1},{3,2},{5,7},{6,4},{4,5},{7,6},{9,11},{10,8},{8,9... | collective-permute-start | bytes 786440 | tf_op jit(solution)/shard_map/ppermute | solution.py:427

commit v4 on v3

--- a/solution.py
+++ b/solution.py
@@ -72,8 +72,10 @@
     shared = cores + chips - 1
 
     def kernel(places_ref, student_ref, hidden_ref, value_ref, student_gain_ref, gain_ref, *refs):
-        feature_refs, out_refs = refs[:shared], refs[shared : shared + number]
-        student_held, held, value_held, scaled, square_ref, sems = refs[shared + number :]
+        feature_outs, out_refs = refs[:shared], list(refs[shared : shared + number])
+        student_held, held, value_held, scaled, square_ref, kept_ref, sems = refs[-7:]
+        feature_refs = refs[shared + number : -7]
+        kept_out, out_refs[-1] = out_refs[-1], kept_ref
         student_copies = []
         for p in range(pieces):
             at = pl.ds(p * rows, rows)
@@ -116,6 +118,13 @@
         for p, copy in enumerate(student_copies):
             copy.wait()
             lax.fori_loop(p * rows // 16, (p + 1) * rows // 16, normalise_rows, 0, unroll=2)
+        last = pieces + number + 1
+        out_copies = []
+        for n in range(shared):
+            out_copies.append(
+                pltpu.make_async_copy(feature_refs[n], feature_outs[n], sems.at[last + n])
+            )
+            out_copies[-1].start()
 
         for i in range(number):
             copies[i].wait()
@@ -154,24 +163,31 @@
             out_ref[:tok, :] = product[i * tok : (i + 1) * tok, :] * factor
             out_ref[tok:, :] = jnp.zeros((EXTRA_ROWS, kv), jnp.float32)
             out_ref[tok : tok + 8, :tok] = split[:, i * tok : (i + 1) * tok]
-
+        out_copies.append(pltpu.make_async_copy(kept_ref, kept_out, sems.at[last + shared]))
+        out_copies[-1].start()
+        for copy in out_copies:
+            copy.wait()
+
+    feature_shapes = [((tok, wide), jnp.bfloat16)] * cores
+    feature_shapes += [((cores * tok, wide), jnp.bfloat16)] * (chips - 1)
     results = call(
         kernel,
         places,
         [student, hidden, value, student_gain.reshape(1, ds), gain.reshape(1, depth)],
         3,
-        [((tok, wide), jnp.bfloat16)] * cores
-        + [((cores * tok, wide), jnp.bfloat16)] * (chips - 1)
-        + [((tok + EXTRA_ROWS, kv), jnp.float32)] * number,
-        [
+        feature_shapes + [((tok + EXTRA_ROWS, kv), jnp.float32)] * number,
+        [pltpu.VMEM(shape, dtype) for shape, dtype in feature_shapes]
+        + [
             pltpu.VMEM((tok, ds), jnp.bfloat16),
             pltpu.VMEM((number, tok, depth), jnp.bfloat16),
             pltpu.VMEM((depth, kv), jnp.bfloat16),
             pltpu.VMEM((number * tok, depth), jnp.bfloat16),
             pltpu.VMEM((number * tok, 128), jnp.float32),
-            pltpu.SemaphoreType.DMA((pieces + number + 1,)),
+            pltpu.VMEM((tok + EXTRA_ROWS, kv), jnp.float32),
+            pltpu.SemaphoreType.DMA((pieces + number + 2 + shared,)),
         ],
         "prepare",
+        [*range(shared), shared + number - 1],
     )
     return results[:cores], results[cores:shared], results[shared:]
 
@@ -209,16 +225,26 @@
             totals.append(total * factor)
         return totals, [features[j][-1][-tok:] for j in alone]
 
+    early = len(features[0])
+
     def kernel(columns_ref, *refs):
-        feature_refs, refs = refs[: len(arrays)], refs[len(arrays) :]
+        own_refs, rest, refs = refs[:early], refs[early : len(arrays)], refs[len(arrays) :]
         value_refs, refs = refs[: len(flat)], refs[len(flat) :]
-        out_refs, (own_ref, sems) = refs[:-2], refs[-2:]
+        out_refs, own_held, (own_ref, sems) = refs[: -2 - early], refs[-2 - early : -2], refs[-2:]
+        own_copies = []
+        for n in range(early):
+            own_copies.append(pltpu.make_async_copy(own_refs[n], own_held[n], sems.at[n]))
+            own_copies[-1].start()
+        feature_refs = [*own_held, *rest]
         copies = []
         for n, j in enumerate(alone):
             src = feature_refs[place[j][0][0]].at[pl.ds((cores - 1) * tok, tok)]
-            copies.append(pltpu.make_async_copy(src, out_refs[chips + n], sems.at[1 + n]))
+            copies.append(pltpu.make_async_copy(src, out_refs[chips + n], sems.at[early + 1 + n]))
             copies[-1].start()
-        for j in range(chips):
+        for j in [*range(1, chips), 0]:
+            if j == 0:
+                for copy in own_copies:
+                    copy.wait()
             total = jnp.zeros((tok, kv), jnp.float32)
             for i, (h, n, b) in enumerate(spots):
                 start = pl.multiple_of(columns_ref[i % per_core] * rows, rows)
@@ -231,16 +257,18 @@
             if j:
                 out_refs[j][...] = total * factor
             else:
-                own_ref[...] = total * factor
-                copies.append(pltpu.make_async_copy(own_ref, out_refs[0], sems.at[0]))
-                copies[-1].start()
+                out_refs[0][...] = total * factor
         for copy in copies:
             copy.wait()
 
     out = [((tok, kv), jnp.float32)] * chips + [((tok, wide), jnp.bfloat16)] * len(alone)
-    scratch = [pltpu.VMEM((tok, kv), jnp.float32), pltpu.SemaphoreType.DMA((1 + len(alone),))]
-    out_hbm = (0, *range(chips, len(out)))
-    results = call(kernel, columns, [*arrays, *flat], 0, out, scratch, "states_parts", out_hbm)
+    scratch = [pltpu.VMEM(part.shape, part.dtype) for part in features[0]]
+    scratch += [pltpu.VMEM((tok, kv), jnp.float32)]
+    scratch += [pltpu.SemaphoreType.DMA((early + 1 + len(alone),))]
+    out_hbm = range(chips, len(out))
+    results = call(
+        kernel, columns, [*arrays, *flat], early, out, scratch, "states_parts", out_hbm
+    )
     return results[:chips], results[chips:]
 
 
@@ -248,15 +276,20 @@
     number = columns.shape[0]
     tok = blocks[0].shape[0]
 
-    def kernel(columns_ref, *refs):
-        block_refs, out_ref = refs[:-1], refs[-1]
-        for i in range(number):
-            src = pl.ds(pl.multiple_of(columns_ref[i] * rows, rows), rows)
-            for b, block_ref in enumerate(block_refs):
+    def kernel(columns_ref, first_ref, *refs):
+        block_refs, (out_ref, first_held, sem) = refs[:-3], refs[-3:]
+        copy = pltpu.make_async_copy(first_ref, first_held, sem.at[0])
+        copy.start()
+        for b, block_ref in [*enumerate(block_refs, 1), (0, first_held)]:
+            if b == 0:
+                copy.wait()
+            for i in range(number):
+                src = pl.ds(pl.multiple_of(columns_ref[i] * rows, rows), rows)
                 out_ref[i * rows : (i + 1) * rows, b * tok : (b + 1) * tok] = block_ref[:tok, src].T
 
     out = [((number * rows, len(blocks) * tok), jnp.bfloat16)]
-    return call(kernel, columns, blocks, 0, out, [], "turned")[0]
+    scratch = [pltpu.VMEM(blocks[0].shape, blocks[0].dtype), pltpu.SemaphoreType.DMA((1,))]
+    return call(kernel, columns, blocks, 1, out, scratch, "turned")[0]
 
 
 def gradient_blocks(held, seen, number, rounded):
@@ -314,7 +347,7 @@
             step //= 2
 
         teacher_factor = half_scale(dt * HIDDEN_MAX * GAIN_MAX * TEACHER_VALUE_MAX)
-        order = list(range(1, mp)) + [0]
+        order = [2, 3, 1] + [0] if mp == 4 else list(range(1, mp)) + [0]
         own, others, parts = prepare(
             jnp.stack([member ^ k for k in order] + [chip, core]),
             student_hidden,
@@ -344,7 +377,7 @@
             step //= 2
         gathered = [jnp.concatenate([pieces[o] for o in first], axis=0)]
         gathered += [pieces[o] for o in later]
-        gathered[-1], received[0] = lax.optimization_barrier((gathered[-1], received[0]))
+        gathered[-1], received[2] = lax.optimization_barrier((gathered[-1], received[2]))
         gathered = [gathered]
         if cores == 2:
             gathered.append([swap(v, "dp", 1) for v in gathered[0]])
@@ -421,8 +454,8 @@
             parts = gradient_blocks(held, seen, mp, rounded)
         if line:
             near = swap(parts[0], "mp", 1).astype(f32)
+            past = lax.ppermute(parts[1], "mp", [(0, 2), (3, 1)])
             across = lax.ppermute(parts[1], "mp", [(1, 2), (2, 1)])
-            past = lax.ppermute(parts[1], "mp", [(0, 2), (3, 1)])
             last = (parts[2] + jnp.where(inner, near, 0.0)).astype(bf16)
             last = lax.ppermute(last, "mp", [(1, 3), (2, 0), (0, 1), (3, 2)])
             total = parts[3] + jnp.where(inner, 0.0, near)

time: 87.9 us -> 87.6 us (level)
  Pallas kernels: 12.9 us -> 14.7 us
  starting transfers between devices: 27.1 us -> 26 us
    pallas_call x4, Pallas kernels: 12.9 us -> 14.7 us  [call(): pl.pallas_call(kernel, out_shape=[(pltpu.HBM if n in out_hbm else pltpu.V...]
    ppermute x17, starting transfers between devices: 19.4 us -> 18.1 us  [swap(): lax.ppermute(value, axis, [(i, i ^ step) for i in range(sizes[axis])])]
  transfers between devices with their start and end apart: 20 -> 20, of which waited for: 10 -> 10; matrix products, arithmetic and copies ran while one was open for 5% -> 4% of each run, Pallas kernels for 12% -> 15%
where the time goes in v4:
time: 87.6 us; the launch traced here: 87.3 us
  waiting for transfers between devices  41.6 us (47%)
  starting transfers between devices  26 us (30%)
  Pallas kernels  14.7 us (17%)
  other arithmetic  3.15 us (4%)
  local copies, waits for them, and re-layouts  1.56 us (2%)
    ppermute x17, waiting for transfers between devices, swap(): lax.ppermute(value, axis, [(i, i ^ step) for i in range(sizes[axis])])  29.7 us
    ppermute x17, starting transfers between devices, swap(): lax.ppermute(value, axis, [(i, i ^ step) for i in range(sizes[axis])])  18.1 us
    pallas_call x4, Pallas kernels, call(): pl.pallas_call(kernel, out_shape=[(pltpu.HBM if n in out_hbm else pltpu.V...  14.7 us
    ppermute x1, waiting for transfers between devices, per_device(): last = lax.ppermute(last, 'mp', [(1, 3), (2, 0), (0, 1), (3, 2)])  8.58 us
    ppermute x1, starting transfers between devices, per_device(): past = lax.ppermute(parts[1], 'mp', [(0, 2), (3, 1)])  4.91 us
    ppermute x1, waiting for transfers between devices, per_device(): past = lax.ppermute(parts[1], 'mp', [(0, 2), (3, 1)])  3.32 us
    ppermute x1, starting transfers between devices, per_device(): last = lax.ppermute(last, 'mp', [(1, 3), (2, 0), (0, 1), (3, 2)])  2.33 us
  transfers between devices with their start and end apart: 20, of which 10 were waited for; matrix products, arithmetic and copies ran while one was open for 4% of the time, Pallas kernels for 15%

profile of v4, /device:TPU:0, one launch (start us, length us, event | category | flops | bytes accessed | tf_op | source)
XLA Modules:
  0.0 87.3 jit_solution(8839627255673563526)
XLA Ops:
  0.0 3.0 %collective-permute-start.2 = (bf16[256,512]{1,0:T(8,128)(2,1)}, bf16[256,512]{1,0:T(8,128)(2,1)S(1)}, u32[]{:S(2)}, u32[]{:S(2)}) collective-permute-start(bf16[256,512]{1,0:T(8,128)(2,1)} %param.12), channel_id=1, source_target_pairs={{0,1},{1,0},{2,3},{3,2},{4,5},{5,4},{6,7},{7,6},{8,9},{9,8},{10,11... | collective-permute-start | bytes 786440 | tf_op jit(solution)/shard_map/ppermute | solution.py:322
  3.0 2.6 %collective-permute-start.3 = (bf16[256,512]{1,0:T(8,128)(2,1)}, bf16[256,512]{1,0:T(8,128)(2,1)S(1)}, u32[]{:S(2)}, u32[]{:S(2)}) collective-permute-start(bf16[256,512]{1,0:T(8,128)(2,1)} %param.12), channel_id=1, source_target_pairs={{0,2},{1,3},{2,0},{3,1},{4,6},{5,7},{6,4},{7,5},{8,10},{9,11},{10,... | collective-permute-start | bytes 786440 | tf_op jit(solution)/shard_map/ppermute | solution.py:322
  5.6 0.7 reshape.138.student_gain_ref
  6.3 0.7 reshape.139.gain_ref
  7.0 0.1 stack.51.places_ref
  7.1 8.1 %prepare.1 = (bf16[256,1024]{1,0:T(8,128)(2,1)}, bf16[256,1024]{1,0:T(8,128)(2,1)}, bf16[512,1024]{1,0:T(8,128)(2,1)}, f32[264,512]{1,0:T(8,128)S(1)}, f32[264,5...) custom-call(s32[6]{0:T(128)S(1)} %stack.51.places_ref, bf16[256,4096]{1,0:T(8,128)(2,1)} %student_ref.1, ...), custom_call_target="tpu_custom_call" | custom-call | flops 1 | bytes 1 | tf_op jit(solution)/shard_map/prepare/pallas_call | solution.py:35
  15.2 0.0 copy-start.1
  15.2 0.0 copy-start.2
  15.2 0.0 copy-start
  15.3 1.6 %collective-permute-start = (bf16[512,1024]{1,0:T(8,128)(2,1)}, bf16[512,1024]{1,0:T(8,128)(2,1)S(1)}, u32[]{:S(2)}, u32[]{:S(2)}) collective-permute-start(bf16[512,1024]{1,0:T(8,128)(2,1)} %get-tuple-element.31), channel_id=1, source_target_pairs={{0,8},{4,12},{8,0},{12,4},{1,9},{5,13},{9,1},{13,5},{2,10},{6,14},... | collective-permute-start | bytes 3145736 | tf_op jit(solution)/shard_map/ppermute | solution.py:322
  16.9 0.0 collective-permute-done.2
  17.0 0.6 collective-permute-done.3
  17.6 0.4 collective-permute-start.5
  18.0 1.6 %collective-permute-start.4 = (bf16[256,512]{1,0:T(8,128)(2,1)S(1)}, bf16[256,512]{1,0:T(8,128)(2,1)S(1)}, u32[]{:S(2)}, u32[]{:S(2)}) collective-permute-start(bf16[256,512]{1,0:T(8,128)(2,1)S(1)} %collective-permute-done.3), channel_id=1, source_target_pairs={{0,1},{1,0},{2,3},{3,2},{4,5},{5,4},{6,7},{7,6},{8,9},{9,8},{10,11... | collective-permute-start | bytes 786440 | tf_op jit(solution)/shard_map/ppermute | solution.py:322
  19.6 1.1 %collective-permute-start.10 = (f16[264,512]{1,0:T(8,128)(2,1)S(1)}, f16[264,512]{1,0:T(8,128)(2,1)S(1)}, u32[]{:S(2)}, u32[]{:S(2)}) collective-permute-start(f16[264,512]{1,0:T(8,128)(2,1)S(1)} %convert_element_type.56), channel_id=1, source_target_pairs={{0,2},{1,3},{2,0},{3,1},{4,6},{5,7},{6,4},{7,5},{8,10},{9,11},{10,... | collective-permute-start | bytes 811016 | tf_op jit(solution)/shard_map/ppermute | solution.py:322
  20.7 1.7 %collective-permute-start.11 = (f16[264,512]{1,0:T(8,128)(2,1)S(1)}, f16[264,512]{1,0:T(8,128)(2,1)S(1)}, u32[]{:S(2)}, u32[]{:S(2)}) collective-permute-start(f16[264,512]{1,0:T(8,128)(2,1)S(1)} %convert_element_type.57), channel_id=1, source_target_pairs={{0,3},{1,2},{2,1},{3,0},{4,7},{5,6},{6,5},{7,4},{8,11},{9,10},{10,... | collective-permute-start | bytes 811016 | tf_op jit(solution)/shard_map/ppermute | solution.py:322
  22.4 0.0 copy-done.1
  22.5 15.9 %collective-permute-done.4.refs_4_ = bf16[256,512]{1,0:T(8,128)(2,1)S(1)} collective-permute-done((bf16[256,512]{1,0:T(8,128)(2,1)S(1)}, bf16[256,512]{1,0:T(8,128)(2,1)S(1)}, u32[]{:S(2)}, u32[]{:S(2)}) %collective-permute-start.4) | collective-permute-done | bytes 262176 | tf_op jit(solution)/shard_map/ppermute | solution.py:322
  38.4 0.0 collective-permute-start.6
  38.4 0.1 pad_add_fusion.1.columns_ref
  38.5 0.0 copy-done.2
  38.5 0.1 convert_reduce_fusion
  38.6 0.0 collective-permute-done.5
  38.6 0.6 collective-permute-start.1
  39.2 0.0 collective-permute-done.10
  39.2 0.1 collective-permute-start.7
  39.3 2.7 %collective-permute-done.11 = f16[264,512]{1,0:T(8,128)(2,1)S(1)} collective-permute-done((f16[264,512]{1,0:T(8,128)(2,1)S(1)}, f16[264,512]{1,0:T(8,128)(2,1)S(1)}, u32[]{:S(2)}, u32[]{:S(2)}) %collective-permute-start.11) | collective-permute-done | bytes 270368 | tf_op jit(solution)/shard_map/ppermute | solution.py:322
  41.9 0.0 copy-done
  41.9 0.2 convert_add_fusion
  42.1 0.2 multiply_reduce_fusion
  42.3 0.0 collective-permute-done.7.refs_6_
  42.4 0.0 collective-permute-done.6.refs_5_
  42.4 0.0 collective-permute-done.refs_2_.refs_0_
  42.4 3.2 %states_parts.1 = (f32[256,512]{1,0:T(8,128)S(1)}, f32[256,512]{1,0:T(8,128)S(1)}, bf16[256,1024]{1,0:T(8,128)(2,1)}) custom-call(s32[4]{0:T(128)S(1)} %pad_add_fusion.1.columns_ref, bf16[256,1024]{1,0:T(8,128)(2,1)} %get-tuple-element.30.refs_0_.first_ref, bf16[256,1024]{1,0:T(8,128)(2,1)} %get-tuple-element.32.refs_1_, ...), custom_call_target="tpu_custom_call" | custom-call | flops 1 | bytes 1 | tf_op jit(solution)/shard_map/states_parts/pallas_call | solution.py:35
  45.6 1.6 %collective-permute-start.9 = (f16[256,512]{1,0:T(8,128)(2,1)S(1)}, f16[256,512]{1,0:T(8,128)(2,1)}, u32[]{:S(2)}, u32[]{:S(2)}) collective-permute-start(f16[256,512]{1,0:T(8,128)(2,1)S(1)} %convert_element_type.59), channel_id=1, source_target_pairs={{0,8},{4,12},{8,0},{12,4},{1,9},{5,13},{9,1},{13,5},{2,10},{6,14},... | collective-permute-start | bytes 786440 | tf_op jit(solution)/shard_map/ppermute | solution.py:322
  47.1 1.5 %collective-permute-start.12 = (f32[256]{0:T(256)S(1)}, f32[256]{0:T(256)S(1)}, u32[]{:S(2)}, u32[]{:S(2)}) collective-permute-start(f32[256]{0:T(256)S(1)} %multiply_reduce_fusion), channel_id=1, source_target_pairs={{0,16},{16,0},{1,17},{17,1},{2,18},{18,2},{3,19},{19,3},{4,20},{20... | collective-permute-start | bytes 3080 | tf_op jit(solution)/shard_map/ppermute | solution.py:322
  48.7 0.1 select_reduce_fusion
  48.7 0.1 collective-permute-start.8
  48.8 1.9 %collective-permute-done.12 = f32[256]{0:T(256)S(1)} collective-permute-done((f32[256]{0:T(256)S(1)}, f32[256]{0:T(256)S(1)}, u32[]{:S(2)}, u32[]{:S(2)}) %collective-permute-start.12) | collective-permute-done | bytes 1056 | tf_op jit(solution)/shard_map/ppermute | solution.py:322
  50.7 0.1 add_multiply_fusion
  50.8 2.4 %collective-permute-done.9 = f16[256,512]{1,0:T(8,128)(2,1)} collective-permute-done((f16[256,512]{1,0:T(8,128)(2,1)S(1)}, f16[256,512]{1,0:T(8,128)(2,1)}, u32[]{:S(2)}, u32[]{:S(2)}) %collective-permute-start.9) | collective-permute-done | bytes 262176 | tf_op jit(solution)/shard_map/ppermute | solution.py:322
  53.1 1.1 %divide_convert_fusion.refs_0_ = bf16[256,512]{1,0:T(8,128)(2,1)S(1)} fusion(f32[256,512]{1,0:T(8,128)S(1)} %get-tuple-element.42, f16[256,512]{1,0:T(8,128)(2,1)} %collective-permute-done.9, f32[264,512]{1,0:T(8,128)S(1)} %convert_add_fusion, f32[256]{0:T(256)S(1)} %add_multiply_fusion, f32[256]{0:T(256)S(1)} %bitcast.14), kind=kLoop, calls=%fused_computation.10 | loop fusion | flops 917504 | bytes 1574912 | tf_op jit(solution)/shard_map/convert_element_type | solution.py:432
  54.3 0.5 collective-permute-start.13
  54.8 0.1 pad_add_fusion.columns_ref
  54.9 0.0 collective-permute-start.14
  54.9 0.0 collective-permute-done.1.refs_1_
  54.9 0.0 collective-permute-done.8.refs_2_
  54.9 2.2 %turned.1.held_ref = bf16[1024,1024]{1,0:T(8,128)(2,1)S(1)} custom-call(s32[4]{0:T(128)S(1)} %pad_add_fusion.columns_ref, bf16[256,1024]{1,0:T(8,128)(2,1)} %get-tuple-element.30.refs_0_.first_ref, bf16[512,1024]{1,0:T(8,128)(2,1)S(1)} %collective-permute-done.refs_2_.refs_0_, bf16[256,1024]{1,0:T(8,128)(2,1)S(1)} %collective-permute-done.1.refs_1_, ...), custom_call_target="tpu_custom_call" | custom-call | flops 1 | bytes 1 | tf_op jit(solution)/shard_map/turned/pallas_call | solution.py:35
  57.1 3.7 %collective-permute-done.13.refs_1_ = bf16[256,512]{1,0:T(8,128)(2,1)S(1)} collective-permute-done((bf16[256,512]{1,0:T(8,128)(2,1)S(1)}, bf16[256,512]{1,0:T(8,128)(2,1)S(1)}, u32[]{:S(2)}, u32[]{:S(2)}) %collective-permute-start.13) | collective-permute-done | bytes 262176 | tf_op jit(solution)/shard_map/ppermute | solution.py:322
  60.8 0.0 collective-permute-start.15
  60.8 0.0 collective-permute-done.14.refs_2_
  60.8 1.5 %collective-permute-done.15.refs_3_ = bf16[256,512]{1,0:T(8,128)(2,1)S(1)} collective-permute-done((bf16[256,512]{1,0:T(8,128)(2,1)S(1)}, bf16[256,512]{1,0:T(8,128)(2,1)S(1)}, u32[]{:S(2)}, u32[]{:S(2)}) %collective-permute-start.15) | collective-permute-done | bytes 262176 | tf_op jit(solution)/shard_map/ppermute | solution.py:322
  62.3 1.3 %gradient_blocks.1 = (bf16[256,512]{1,0:T(8,128)(2,1)S(1)}, bf16[256,512]{1,0:T(8,128)(2,1)S(1)}, f32[256,512]{1,0:T(8,128)S(1)}, f32[256,512]{1,0:T(8,128)S(1)}) custom-call(s32[1]{0:T(128)} %constant.22.clone.1._, bf16[1024,1024]{1,0:T(8,128)(2,1)S(1)} %turned.1.held_ref, bf16[256,512]{1,0:T(8,128)(2,1)S(1)} %divide_convert_fusion.refs_0_, ...), custom_call_target="tpu_custom_call" | custom-call | flops 1 | bytes 1 | tf_op jit(solution)/shard_map/gradient_blocks/pallas_call | solution.py:35
  63.6 1.8 %collective-permute-start.16 = (bf16[256,512]{1,0:T(8,128)(2,1)S(1)}, bf16[256,512]{1,0:T(8,128)(2,1)S(1)}, u32[]{:S(2)}, u32[]{:S(2)}) collective-permute-start(bf16[256,512]{1,0:T(8,128)(2,1)S(1)} %get-tuple-element.52), channel_id=1, source_target_pairs={{0,1},{1,0},{2,3},{3,2},{4,5},{5,4},{6,7},{7,6},{8,9},{9,8},{10,11... | collective-permute-start | bytes 786440 | tf_op jit(solution)/shard_map/ppermute | solution.py:322
  65.4 0.7 collective-permute-start.17
  66.1 4.9 %collective-permute-start.18 = (bf16[256,512]{1,0:T(8,128)(2,1)S(1)}, bf16[256,512]{1,0:T(8,128)(2,1)S(1)}, u32[]{:S(2)}, u32[]{:S(2)}) collective-permute-start(bf16[256,512]{1,0:T(8,128)(2,1)S(1)} %get-tuple-element.53), channel_id=1, source_target_pairs={{0,2},{3,1},{4,6},{7,5},{8,10},{11,9},{12,14},{15,13},{16,18},{19,... | collective-permute-start | bytes 786440 | tf_op jit(solution)/shard_map/ppermute | solution.py:457
  71.0 1.0 %collective-permute-done.16 = bf16[256,512]{1,0:T(8,128)(2,1)S(1)} collective-permute-done((bf16[256,512]{1,0:T(8,128)(2,1)S(1)}, bf16[256,512]{1,0:T(8,128)(2,1)S(1)}, u32[]{:S(2)}, u32[]{:S(2)}) %collective-permute-start.16) | collective-permute-done | bytes 262176 | tf_op jit(solution)/shard_map/ppermute | solution.py:322
  72.0 0.1 fusion.5
  72.1 2.3 %collective-permute-start.19 = (bf16[256,512]{1,0:T(8,128)(2,1)S(1)}, bf16[256,512]{1,0:T(8,128)(2,1)S(1)}, u32[]{:S(2)}, u32[]{:S(2)}) collective-permute-start(bf16[256,512]{1,0:T(8,128)(2,1)S(1)} %fusion.5), channel_id=1, source_target_pairs={{1,3},{2,0},{0,1},{3,2},{5,7},{6,4},{4,5},{7,6},{9,11},{10,8},{8,9... | collective-permute-start | bytes 786440 | tf_op jit(solution)/shard_map/ppermute | solution.py:460
  74.4 0.0 collective-permute-done.17
  74.4 3.3 %collective-permute-done.18 = bf16[256,512]{1,0:T(8,128)(2,1)S(1)} collective-permute-done((bf16[256,512]{1,0:T(8,128)(2,1)S(1)}, bf16[256,512]{1,0:T(8,128)(2,1)S(1)}, u32[]{:S(2)}, u32[]{:S(2)}) %collective-permute-start.18) | collective-permute-done | bytes 262176 | tf_op jit(solution)/shard_map/ppermute | solution.py:457
  77.8 8.6 %collective-permute-done.19 = bf16[256,512]{1,0:T(8,128)(2,1)S(1)} collective-permute-done((bf16[256,512]{1,0:T(8,128)(2,1)S(1)}, bf16[256,512]{1,0:T(8,128)(2,1)S(1)}, u32[]{:S(2)}, u32[]{:S(2)}) %collective-permute-start.19) | collective-permute-done | bytes 262176 | tf_op jit(solution)/shard_map/ppermute | solution.py:460
  86.3 1.0 %fusion.3 = f32[256,512]{1,0:T(8,128)} fusion(f32[256,512]{1,0:T(8,128)S(1)} %get-tuple-element.51, bf16[256,512]{1,0:T(8,128)(2,1)S(1)} %collective-permute-done.16, bf16[256,512]{1,0:T(8,128)(2,1)S(1)} %collective-permute-done.19, bf16[256,512]{1,0:T(8,128)(2,1)S(1)} %collective-permute-done.18, bf16[256,512]{1,0:T(8,128)(2,1)S(1)} %collective-permute-done.17, ...), kind=kLoop, calls=%fused_computation.6 | loop fusion | flops 1179648 | bytes 2097153 | tf_op jit(solution)/shard_map/add | solution.py:462
  (8 shorter events, 0.2 us)
Async XLA Ops:
  0.0 16.9 %collective-permute-start.2 = (bf16[256,512]{1,0:T(8,128)(2,1)}, bf16[256,512]{1,0:T(8,128)(2,1)S(1)}, u32[]{:S(2)}, u32[]{:S(2)}) collective-permute-start(bf16[256,512]{1,0:T(8,128)(2,1)} %param.12), channel_id=1, source_target_pairs={{0,1},{1,0},{2,3},{3,2},{4,5},{5,4},{6,7},{7,6},{8,9},{9,8},{10,11... | collective-permute-start | bytes 786440 | tf_op jit(solution)/shard_map/ppermute | solution.py:322
  3.0 14.6 %collective-permute-start.3 = (bf16[256,512]{1,0:T(8,128)(2,1)}, bf16[256,512]{1,0:T(8,128)(2,1)S(1)}, u32[]{:S(2)}, u32[]{:S(2)}) collective-permute-start(bf16[256,512]{1,0:T(8,128)(2,1)} %param.12), channel_id=1, source_target_pairs={{0,2},{1,3},{2,0},{3,1},{4,6},{5,7},{6,4},{7,5},{8,10},{9,11},{10,... | collective-permute-start | bytes 786440 | tf_op jit(solution)/shard_map/ppermute | solution.py:322
  15.2 7.2 %copy-start.1 = (bf16[256,512]{1,0:T(8,128)(2,1)S(1)}, bf16[256,512]{1,0:T(8,128)(2,1)}, u32[]{:S(2)}) copy-start(bf16[256,512]{1,0:T(8,128)(2,1)} %param.12) | copy-start | bytes 786436
  15.2 23.2 %copy-start.2 = (s32[1,1024]{1,0:T(1,128)S(1)}, s32[1,1024]{1,0:T(1,128)}, u32[]{:S(2)}) copy-start(s32[1,1024]{1,0:T(1,128)} %param.13) | copy-start | bytes 12292
  15.2 26.7 %copy-start = (f32[264,512]{1,0:T(8,128)S(1)}, f32[264,512]{1,0:T(8,128)}, u32[]{:S(2)}) copy-start(f32[264,512]{1,0:T(8,128)} %get-tuple-element.44) | copy-start | bytes 1622020
  15.3 27.1 %collective-permute-start = (bf16[512,1024]{1,0:T(8,128)(2,1)}, bf16[512,1024]{1,0:T(8,128)(2,1)S(1)}, u32[]{:S(2)}, u32[]{:S(2)}) collective-permute-start(bf16[512,1024]{1,0:T(8,128)(2,1)} %get-tuple-element.31), channel_id=1, source_target_pairs={{0,8},{4,12},{8,0},{12,4},{1,9},{5,13},{9,1},{13,5},{2,10},{6,14},... | collective-permute-start | bytes 3145736 | tf_op jit(solution)/shard_map/ppermute | solution.py:322
  17.6 21.0 %collective-permute-start.5 = (f16[264,512]{1,0:T(8,128)(2,1)S(1)}, f16[264,512]{1,0:T(8,128)(2,1)S(1)}, u32[]{:S(2)}, u32[]{:S(2)}) collective-permute-start(f16[264,512]{1,0:T(8,128)(2,1)S(1)} %convert_element_type.58), channel_id=1, source_target_pairs={{0,1},{1,0},{2,3},{3,2},{4,5},{5,4},{6,7},{7,6},{8,9},{9,8},{10,11... | collective-permute-start | bytes 811016 | tf_op jit(solution)/shard_map/ppermute | solution.py:322
  18.0 20.4 %collective-permute-start.4 = (bf16[256,512]{1,0:T(8,128)(2,1)S(1)}, bf16[256,512]{1,0:T(8,128)(2,1)S(1)}, u32[]{:S(2)}, u32[]{:S(2)}) collective-permute-start(bf16[256,512]{1,0:T(8,128)(2,1)S(1)} %collective-permute-done.3), channel_id=1, source_target_pairs={{0,1},{1,0},{2,3},{3,2},{4,5},{5,4},{6,7},{7,6},{8,9},{9,8},{10,11... | collective-permute-start | bytes 786440 | tf_op jit(solution)/shard_map/ppermute | solution.py:322
  19.6 19.6 %collective-permute-start.10 = (f16[264,512]{1,0:T(8,128)(2,1)S(1)}, f16[264,512]{1,0:T(8,128)(2,1)S(1)}, u32[]{:S(2)}, u32[]{:S(2)}) collective-permute-start(f16[264,512]{1,0:T(8,128)(2,1)S(1)} %convert_element_type.56), channel_id=1, source_target_pairs={{0,2},{1,3},{2,0},{3,1},{4,6},{5,7},{6,4},{7,5},{8,10},{9,11},{10,... | collective-permute-start | bytes 811016 | tf_op jit(solution)/shard_map/ppermute | solution.py:322
  20.7 21.2 %collective-permute-start.11 = (f16[264,512]{1,0:T(8,128)(2,1)S(1)}, f16[264,512]{1,0:T(8,128)(2,1)S(1)}, u32[]{:S(2)}, u32[]{:S(2)}) collective-permute-start(f16[264,512]{1,0:T(8,128)(2,1)S(1)} %convert_element_type.57), channel_id=1, source_target_pairs={{0,3},{1,2},{2,1},{3,0},{4,7},{5,6},{6,5},{7,4},{8,11},{9,10},{10,... | collective-permute-start | bytes 811016 | tf_op jit(solution)/shard_map/ppermute | solution.py:322
  38.4 4.0 %collective-permute-start.6 = (bf16[768,512]{1,0:T(8,128)(2,1)S(1)}, bf16[768,512]{1,0:T(8,128)(2,1)S(1)}, u32[]{:S(2)}, u32[]{:S(2)}) collective-permute-start(bf16[768,512]{1,0:T(8,128)(2,1)S(1)} %constant_dynamic-update-slice_fusion.refs_3_), channel_id=1, source_target_pairs={{0,4},{4,0},{8,12},{12,8},{1,5},{5,1},{9,13},{13,9},{2,6},{6,2},{1... | collective-permute-start | bytes 2359304 | tf_op jit(solution)/shard_map/ppermute | solution.py:322
  38.6 16.3 %collective-permute-start.1 = (bf16[256,1024]{1,0:T(8,128)(2,1)}, bf16[256,1024]{1,0:T(8,128)(2,1)S(1)}, u32[]{:S(2)}, u32[]{:S(2)}) collective-permute-start(bf16[256,1024]{1,0:T(8,128)(2,1)} %get-tuple-element.32.refs_1_), channel_id=1, source_target_pairs={{0,4},{4,0},{8,12},{12,8},{1,5},{5,1},{9,13},{13,9},{2,6},{6,2},{1... | collective-permute-start | bytes 1572872 | tf_op jit(solution)/shard_map/ppermute | solution.py:322
  39.2 3.2 %collective-permute-start.7 = (bf16[256,512]{1,0:T(8,128)(2,1)S(1)}, bf16[256,512]{1,0:T(8,128)(2,1)S(1)}, u32[]{:S(2)}, u32[]{:S(2)}) collective-permute-start(bf16[256,512]{1,0:T(8,128)(2,1)S(1)} %collective-permute-done.4.refs_4_), channel_id=1, source_target_pairs={{0,4},{4,0},{8,12},{12,8},{1,5},{5,1},{9,13},{13,9},{2,6},{6,2},{1... | collective-permute-start | bytes 786440 | tf_op jit(solution)/shard_map/ppermute | solution.py:322
  45.6 7.6 %collective-permute-start.9 = (f16[256,512]{1,0:T(8,128)(2,1)S(1)}, f16[256,512]{1,0:T(8,128)(2,1)}, u32[]{:S(2)}, u32[]{:S(2)}) collective-permute-start(f16[256,512]{1,0:T(8,128)(2,1)S(1)} %convert_element_type.59), channel_id=1, source_target_pairs={{0,8},{4,12},{8,0},{12,4},{1,9},{5,13},{9,1},{13,5},{2,10},{6,14},... | collective-permute-start | bytes 786440 | tf_op jit(solution)/shard_map/ppermute | solution.py:322
  47.1 3.6 %collective-permute-start.12 = (f32[256]{0:T(256)S(1)}, f32[256]{0:T(256)S(1)}, u32[]{:S(2)}, u32[]{:S(2)}) collective-permute-start(f32[256]{0:T(256)S(1)} %multiply_reduce_fusion), channel_id=1, source_target_pairs={{0,16},{16,0},{1,17},{17,1},{2,18},{18,2},{3,19},{19,3},{4,20},{20... | collective-permute-start | bytes 3080 | tf_op jit(solution)/shard_map/ppermute | solution.py:322
  48.7 6.2 %collective-permute-start.8 = (bf16[256,1024]{1,0:T(8,128)(2,1)}, bf16[256,1024]{1,0:T(8,128)(2,1)S(1)}, u32[]{:S(2)}, u32[]{:S(2)}) collective-permute-start(bf16[256,1024]{1,0:T(8,128)(2,1)} %get-tuple-element.41), channel_id=1, source_target_pairs={{0,4},{4,0},{8,12},{12,8},{1,5},{5,1},{9,13},{13,9},{2,6},{6,2},{1... | collective-permute-start | bytes 1572872 | tf_op jit(solution)/shard_map/ppermute | solution.py:322
  54.3 6.5 %collective-permute-start.13 = (bf16[256,512]{1,0:T(8,128)(2,1)S(1)}, bf16[256,512]{1,0:T(8,128)(2,1)S(1)}, u32[]{:S(2)}, u32[]{:S(2)}) collective-permute-start(bf16[256,512]{1,0:T(8,128)(2,1)S(1)} %divide_convert_fusion.refs_0_), channel_id=1, source_target_pairs={{0,8},{4,12},{8,0},{12,4},{1,9},{5,13},{9,1},{13,5},{2,10},{6,14},... | collective-permute-start | bytes 786440 | tf_op jit(solution)/shard_map/ppermute | solution.py:322
  54.9 5.9 %collective-permute-start.14 = (bf16[256,512]{1,0:T(8,128)(2,1)S(1)}, bf16[256,512]{1,0:T(8,128)(2,1)S(1)}, u32[]{:S(2)}, u32[]{:S(2)}) collective-permute-start(bf16[256,512]{1,0:T(8,128)(2,1)S(1)} %divide_convert_fusion.refs_0_), channel_id=1, source_target_pairs={{0,4},{4,0},{8,12},{12,8},{1,5},{5,1},{9,13},{13,9},{2,6},{6,2},{1... | collective-permute-start | bytes 786440 | tf_op jit(solution)/shard_map/ppermute | solution.py:322
  60.8 1.5 %collective-permute-start.15 = (bf16[256,512]{1,0:T(8,128)(2,1)S(1)}, bf16[256,512]{1,0:T(8,128)(2,1)S(1)}, u32[]{:S(2)}, u32[]{:S(2)}) collective-permute-start(bf16[256,512]{1,0:T(8,128)(2,1)S(1)} %collective-permute-done.13.refs_1_), channel_id=1, source_target_pairs={{0,4},{4,0},{8,12},{12,8},{1,5},{5,1},{9,13},{13,9},{2,6},{6,2},{1... | collective-permute-start | bytes 786440 | tf_op jit(solution)/shard_map/ppermute | solution.py:322
  63.6 8.4 %collective-permute-start.16 = (bf16[256,512]{1,0:T(8,128)(2,1)S(1)}, bf16[256,512]{1,0:T(8,128)(2,1)S(1)}, u32[]{:S(2)}, u32[]{:S(2)}) collective-permute-start(bf16[256,512]{1,0:T(8,128)(2,1)S(1)} %get-tuple-element.52), channel_id=1, source_target_pairs={{0,1},{1,0},{2,3},{3,2},{4,5},{5,4},{6,7},{7,6},{8,9},{9,8},{10,11... | collective-permute-start | bytes 786440 | tf_op jit(solution)/shard_map/ppermute | solution.py:322
  65.4 9.0 %collective-permute-start.17 = (bf16[256,512]{1,0:T(8,128)(2,1)S(1)}, bf16[256,512]{1,0:T(8,128)(2,1)S(1)}, u32[]{:S(2)}, u32[]{:S(2)}) collective-permute-start(bf16[256,512]{1,0:T(8,128)(2,1)S(1)} %get-tuple-element.53), channel_id=1, source_target_pairs={{1,2},{2,1},{5,6},{6,5},{9,10},{10,9},{13,14},{14,13},{17,18},{18,... | collective-permute-start | bytes 786440 | tf_op jit(solution)/shard_map/ppermute | solution.py:458
  66.1 11.7 %collective-permute-start.18 = (bf16[256,512]{1,0:T(8,128)(2,1)S(1)}, bf16[256,512]{1,0:T(8,128)(2,1)S(1)}, u32[]{:S(2)}, u32[]{:S(2)}) collective-permute-start(bf16[256,512]{1,0:T(8,128)(2,1)S(1)} %get-tuple-element.53), channel_id=1, source_target_pairs={{0,2},{3,1},{4,6},{7,5},{8,10},{11,9},{12,14},{15,13},{16,18},{19,... | collective-permute-start | bytes 786440 | tf_op jit(solution)/shard_map/ppermute | solution.py:457
  72.1 14.2 %collective-permute-start.19 = (bf16[256,512]{1,0:T(8,128)(2,1)S(1)}, bf16[256,512]{1,0:T(8,128)(2,1)S(1)}, u32[]{:S(2)}, u32[]{:S(2)}) collective-permute-start(bf16[256,512]{1,0:T(8,128)(2,1)S(1)} %fusion.5), channel_id=1, source_target_pairs={{1,3},{2,0},{0,1},{3,2},{5,7},{6,4},{4,5},{7,6},{9,11},{10,8},{8,9... | collective-permute-start | bytes 786440 | tf_op jit(solution)/shard_map/ppermute | solution.py:460

commit v5 on v4

--- a/solution.py
+++ b/solution.py
@@ -192,9 +192,10 @@
     return results[:cores], results[cores:shared], results[shared:]
 
 
-def states_parts(columns, features, values, rows, factor):
+def states_parts(columns, features, values, rows, factor, early):
     cores, chips = len(values), len(features)
     tok, wide = features[0][0].shape
+    tok = tok * len(features[0]) // cores
     kv = values[0][0].shape[1]
     flat = [v for of_core in values for v in of_core]
     spots = [
@@ -225,7 +226,6 @@
             totals.append(total * factor)
         return totals, [features[j][-1][-tok:] for j in alone]
 
-    early = len(features[0])
 
     def kernel(columns_ref, *refs):
         own_refs, rest, refs = refs[:early], refs[early : len(arrays)], refs[len(arrays) :]
@@ -241,7 +241,7 @@
             src = feature_refs[place[j][0][0]].at[pl.ds((cores - 1) * tok, tok)]
             copies.append(pltpu.make_async_copy(src, out_refs[chips + n], sems.at[early + 1 + n]))
             copies[-1].start()
-        for j in [*range(1, chips), 0]:
+        for j in range(chips):
             if j == 0:
                 for copy in own_copies:
                     copy.wait()
@@ -254,15 +254,12 @@
                     value_refs[h * each + n][b * rows : (b + 1) * rows, :],
                     preferred_element_type=jnp.float32,
                 )
-            if j:
-                out_refs[j][...] = total * factor
-            else:
-                out_refs[0][...] = total * factor
+            out_refs[j][...] = total * factor
         for copy in copies:
             copy.wait()
 
     out = [((tok, kv), jnp.float32)] * chips + [((tok, wide), jnp.bfloat16)] * len(alone)
-    scratch = [pltpu.VMEM(part.shape, part.dtype) for part in features[0]]
+    scratch = [pltpu.VMEM(part.shape, part.dtype) for part in arrays[:early]]
     scratch += [pltpu.VMEM((tok, kv), jnp.float32)]
     scratch += [pltpu.SemaphoreType.DMA((early + 1 + len(alone),))]
     out_hbm = range(chips, len(out))
@@ -292,13 +289,13 @@
     return call(kernel, columns, blocks, 1, out, scratch, "turned")[0]
 
 
-def gradient_blocks(held, seen, number, rounded):
+def gradient_blocks(held, seen, number, blocks, dtype):
     rows, tok = held.shape[0] // number, seen[0].shape[0]
     kv = seen[0].shape[1]
 
     def kernel(_, held_ref, *refs):
         seen_refs, out_refs = refs[: len(seen)], refs[len(seen) :]
-        for i, out_ref in enumerate(out_refs):
+        for i, out_ref in zip(blocks, out_refs):
             total = jnp.zeros((rows, kv), jnp.float32)
             for b, seen_ref in enumerate(seen_refs):
                 total += jnp.dot(
@@ -308,7 +305,7 @@
                 )
             out_ref[...] = total.astype(out_ref.dtype)
 
-    out = [((rows, kv), jnp.bfloat16)] * rounded + [((rows, kv), jnp.float32)] * (number - rounded)
+    out = [((rows, kv), dtype)] * len(blocks)
     return call(kernel, jnp.zeros(1), [held, *seen], 0, out, [], "gradient_blocks")
 
 
@@ -384,9 +381,10 @@
 
         columns = jnp.stack([member ^ o for o in first + later])
         states_factor = half_scale(GAIN_MAX * ds * STUDENT_VALUE_MAX)
-        (states, *returned), second = states_parts(
-            columns, [own] + [[part] for part in others], gathered, rows, states_factor
+        returned, second = states_parts(
+            columns, [[part] for part in others], gathered, rows, states_factor, 0
         )
+        (states,), _ = states_parts(columns, [own], gathered, rows, states_factor, len(own))
         if cores == 1:
             second = others
         returned = payload = [part.astype(f16) for part in returned]
@@ -451,7 +449,10 @@
             ]
             parts = [p.astype(bf16) for p in parts[:rounded]] + parts[rounded:]
         else:
-            parts = gradient_blocks(held, seen, mp, rounded)
+            parts = [
+                *gradient_blocks(held, seen, mp, range(rounded), bf16),
+                *gradient_blocks(held, seen, mp, range(rounded, mp), f32),
+            ]
         if line:
             near = swap(parts[0], "mp", 1).astype(f32)
             past = lax.ppermute(parts[1], "mp", [(0, 2), (3, 1)])

time: 87.6 us -> 87.1 us (level)
  waiting for transfers between devices: 41.6 us -> 37.4 us
  Pallas kernels: 14.7 us -> 17.1 us
    ppermute x17, waiting for transfers between devices: 29.7 us -> 25.5 us  [swap(): lax.ppermute(value, axis, [(i, i ^ step) for i in range(sizes[axis])])]
    pallas_call x4 -> x6, Pallas kernels: 14.7 us -> 17.1 us  [call(): pl.pallas_call(kernel, out_shape=[(pltpu.HBM if n in out_hbm else pltpu.V...]
  transfers between devices with their start and end apart: 20 -> 20, of which waited for: 10 -> 9; matrix products, arithmetic and copies ran while one was open for 4% -> 4% of each run, Pallas kernels for 15% -> 19%
where the time goes in v5:
time: 87.1 us; the launch traced here: 86.7 us
  waiting for transfers between devices  37.4 us (43%)
  starting transfers between devices  26.6 us (31%)
  Pallas kernels  17.1 us (20%)
  other arithmetic  3.18 us (4%)
  local copies, waits for them, and re-layouts  2.13 us (2%)
    ppermute x17, waiting for transfers between devices, swap(): lax.ppermute(value, axis, [(i, i ^ step) for i in range(sizes[axis])])  25.5 us
    ppermute x17, starting transfers between devices, swap(): lax.ppermute(value, axis, [(i, i ^ step) for i in range(sizes[axis])])  19 us
    pallas_call x6, Pallas kernels, call(): pl.pallas_call(kernel, out_shape=[(pltpu.HBM if n in out_hbm else pltpu.V...  17.1 us
    ppermute x1, waiting for transfers between devices, per_device(): last = lax.ppermute(last, 'mp', [(1, 3), (2, 0), (0, 1), (3, 2)])  8.85 us
    ppermute x1, starting transfers between devices, per_device(): past = lax.ppermute(parts[1], 'mp', [(0, 2), (3, 1)])  4.64 us
    ppermute x1, waiting for transfers between devices, per_device(): past = lax.ppermute(parts[1], 'mp', [(0, 2), (3, 1)])  3.05 us
    ppermute x1, starting transfers between devices, per_device(): last = lax.ppermute(last, 'mp', [(1, 3), (2, 0), (0, 1), (3, 2)])  2.34 us
  transfers between devices with their start and end apart: 20, of which 9 were waited for; matrix products, arithmetic and copies ran while one was open for 4% of the time, Pallas kernels for 19%

profile of v5, /device:TPU:0, one launch (start us, length us, event | category | flops | bytes accessed | tf_op | source)
XLA Modules:
  0.0 86.7 jit_solution(15850916897587353074)
XLA Ops:
  0.0 3.0 %collective-permute-start.2 = (bf16[256,512]{1,0:T(8,128)(2,1)}, bf16[256,512]{1,0:T(8,128)(2,1)S(1)}, u32[]{:S(2)}, u32[]{:S(2)}) collective-permute-start(bf16[256,512]{1,0:T(8,128)(2,1)} %param.12), channel_id=1, source_target_pairs={{0,1},{1,0},{2,3},{3,2},{4,5},{5,4},{6,7},{7,6},{8,9},{9,8},{10,11... | collective-permute-start | bytes 786440 | tf_op jit(solution)/shard_map/ppermute | solution.py:319
  3.0 2.6 %collective-permute-start.3 = (bf16[256,512]{1,0:T(8,128)(2,1)}, bf16[256,512]{1,0:T(8,128)(2,1)S(1)}, u32[]{:S(2)}, u32[]{:S(2)}) collective-permute-start(bf16[256,512]{1,0:T(8,128)(2,1)} %param.12), channel_id=1, source_target_pairs={{0,2},{1,3},{2,0},{3,1},{4,6},{5,7},{6,4},{7,5},{8,10},{9,11},{10,... | collective-permute-start | bytes 786440 | tf_op jit(solution)/shard_map/ppermute | solution.py:319
  5.6 0.7 reshape.138.student_gain_ref
  6.3 0.7 reshape.139.gain_ref
  7.0 0.1 stack.51.places_ref
  7.1 8.1 %prepare.1 = (bf16[256,1024]{1,0:T(8,128)(2,1)}, bf16[256,1024]{1,0:T(8,128)(2,1)}, bf16[512,1024]{1,0:T(8,128)(2,1)}, f32[264,512]{1,0:T(8,128)S(1)}, f32[264,5...) custom-call(s32[6]{0:T(128)S(1)} %stack.51.places_ref, bf16[256,4096]{1,0:T(8,128)(2,1)} %student_ref.1, ...), custom_call_target="tpu_custom_call" | custom-call | flops 1 | bytes 1 | tf_op jit(solution)/shard_map/prepare/pallas_call | solution.py:35
  15.2 0.0 copy-start.3
  15.2 0.0 copy-start.4
  15.2 1.6 %collective-permute-start = (bf16[512,1024]{1,0:T(8,128)(2,1)}, bf16[512,1024]{1,0:T(8,128)(2,1)S(1)}, u32[]{:S(2)}, u32[]{:S(2)}) collective-permute-start(bf16[512,1024]{1,0:T(8,128)(2,1)} %get-tuple-element.30), channel_id=1, source_target_pairs={{0,8},{4,12},{8,0},{12,4},{1,9},{5,13},{9,1},{13,5},{2,10},{6,14},... | collective-permute-start | bytes 3145736 | tf_op jit(solution)/shard_map/ppermute | solution.py:319
  16.9 0.0 collective-permute-done.2
  16.9 0.6 collective-permute-done.3
  17.6 0.4 collective-permute-start.5
  18.0 1.6 %collective-permute-start.4 = (bf16[256,512]{1,0:T(8,128)(2,1)S(1)}, bf16[256,512]{1,0:T(8,128)(2,1)S(1)}, u32[]{:S(2)}, u32[]{:S(2)}) collective-permute-start(bf16[256,512]{1,0:T(8,128)(2,1)S(1)} %collective-permute-done.3), channel_id=1, source_target_pairs={{0,1},{1,0},{2,3},{3,2},{4,5},{5,4},{6,7},{7,6},{8,9},{9,8},{10,11... | collective-permute-start | bytes 786440 | tf_op jit(solution)/shard_map/ppermute | solution.py:319
  19.6 1.1 %collective-permute-start.10 = (f16[264,512]{1,0:T(8,128)(2,1)S(1)}, f16[264,512]{1,0:T(8,128)(2,1)S(1)}, u32[]{:S(2)}, u32[]{:S(2)}) collective-permute-start(f16[264,512]{1,0:T(8,128)(2,1)S(1)} %convert_element_type.56), channel_id=1, source_target_pairs={{0,2},{1,3},{2,0},{3,1},{4,6},{5,7},{6,4},{7,5},{8,10},{9,11},{10,... | collective-permute-start | bytes 811016 | tf_op jit(solution)/shard_map/ppermute | solution.py:319
  20.7 1.7 %collective-permute-start.11 = (f16[264,512]{1,0:T(8,128)(2,1)S(1)}, f16[264,512]{1,0:T(8,128)(2,1)S(1)}, u32[]{:S(2)}, u32[]{:S(2)}) collective-permute-start(f16[264,512]{1,0:T(8,128)(2,1)S(1)} %convert_element_type.57), channel_id=1, source_target_pairs={{0,3},{1,2},{2,1},{3,0},{4,7},{5,6},{6,5},{7,4},{8,11},{9,10},{10,... | collective-permute-start | bytes 811016 | tf_op jit(solution)/shard_map/ppermute | solution.py:319
  22.4 0.0 copy-done.3
  22.5 15.9 %collective-permute-done.4.refs_2_.refs_3_ = bf16[256,512]{1,0:T(8,128)(2,1)S(1)} collective-permute-done((bf16[256,512]{1,0:T(8,128)(2,1)S(1)}, bf16[256,512]{1,0:T(8,128)(2,1)S(1)}, u32[]{:S(2)}, u32[]{:S(2)}) %collective-permute-start.4) | collective-permute-done | bytes 262176 | tf_op jit(solution)/shard_map/ppermute | solution.py:319
  38.4 0.0 collective-permute-start.6
  38.4 0.1 pad_add_fusion.1.columns_ref
  38.4 0.1 convert_reduce_fusion
  38.6 0.0 collective-permute-done.5
  38.6 0.6 collective-permute-start.1
  39.1 0.0 collective-permute-done.10
  39.1 0.1 collective-permute-start.7
  39.2 2.7 %collective-permute-done.11 = f16[264,512]{1,0:T(8,128)(2,1)S(1)} collective-permute-done((f16[264,512]{1,0:T(8,128)(2,1)S(1)}, f16[264,512]{1,0:T(8,128)(2,1)S(1)}, u32[]{:S(2)}, u32[]{:S(2)}) %collective-permute-start.11) | collective-permute-done | bytes 270368 | tf_op jit(solution)/shard_map/ppermute | solution.py:319
  41.9 0.2 convert_add_fusion
  42.1 0.0 copy-start
  42.1 0.2 multiply_reduce_fusion
  42.4 0.0 collective-permute-done.7.refs_4_.refs_5_
  42.4 0.0 collective-permute-done.6.refs_3_.refs_4_
  42.4 0.6 copy-done
  42.9 0.0 collective-permute-done.refs_0_
  42.9 1.8 %states_parts.2 = (f32[256,512]{1,0:T(8,128)S(1)}, bf16[256,1024]{1,0:T(8,128)(2,1)}) custom-call(s32[4]{0:T(128)S(1)} %pad_add_fusion.1.columns_ref, bf16[512,1024]{1,0:T(8,128)(2,1)S(1)} %collective-permute-done.refs_0_, bf16[768,512]{1,0:T(8,128)(2,1)S(1)} %constant_dynamic-update-slice_fusion.refs_1_.refs_2_, ...), custom_call_target="tpu_custom_call" | custom-call | flops 1 | bytes 1 | tf_op jit(solution)/shard_map/states_parts/pallas_call | solution.py:35
  44.8 1.6 %collective-permute-start.9 = (f16[256,512]{1,0:T(8,128)(2,1)S(1)}, f16[256,512]{1,0:T(8,128)(2,1)}, u32[]{:S(2)}, u32[]{:S(2)}) collective-permute-start(f16[256,512]{1,0:T(8,128)(2,1)S(1)} %convert_element_type.59), channel_id=1, source_target_pairs={{0,8},{4,12},{8,0},{12,4},{1,9},{5,13},{9,1},{13,5},{2,10},{6,14},... | collective-permute-start | bytes 786440 | tf_op jit(solution)/shard_map/ppermute | solution.py:319
  46.3 1.5 %collective-permute-start.12 = (f32[256]{0:T(256)S(1)}, f32[256]{0:T(256)S(1)}, u32[]{:S(2)}, u32[]{:S(2)}) collective-permute-start(f32[256]{0:T(256)S(1)} %multiply_reduce_fusion), channel_id=1, source_target_pairs={{0,16},{16,0},{1,17},{17,1},{2,18},{18,2},{3,19},{19,3},{4,20},{20... | collective-permute-start | bytes 3080 | tf_op jit(solution)/shard_map/ppermute | solution.py:319
  47.8 0.1 select_reduce_fusion
  47.9 0.1 collective-permute-start.8
  48.0 2.5 %states_parts.3 = f32[256,512]{1,0:T(8,128)S(1)} custom-call(s32[4]{0:T(128)S(1)} %pad_add_fusion.1.columns_ref, bf16[256,1024]{1,0:T(8,128)(2,1)} %get-tuple-element.29.first_ref.refs_0_, bf16[256,1024]{1,0:T(8,128)(2,1)} %get-tuple-element.31.refs_1_, bf16[768,512]{1,0:T(8,128)(2,1)S(1)} %constant_dynamic-update-slice_fusion.refs_1_.refs_2_, ...), custom_call_target="tpu_custom_call" | custom-call | flops 1 | bytes 1 | tf_op jit(solution)/shard_map/states_parts/pallas_call | solution.py:35
  50.5 0.0 collective-permute-done.12
  50.5 0.1 add_multiply_fusion
  50.6 1.1 %collective-permute-done.9 = f16[256,512]{1,0:T(8,128)(2,1)} collective-permute-done((f16[256,512]{1,0:T(8,128)(2,1)S(1)}, f16[256,512]{1,0:T(8,128)(2,1)}, u32[]{:S(2)}, u32[]{:S(2)}) %collective-permute-start.9) | collective-permute-done | bytes 262176 | tf_op jit(solution)/shard_map/ppermute | solution.py:319
  51.7 1.1 %divide_convert_fusion.refs_0_ = bf16[256,512]{1,0:T(8,128)(2,1)S(1)} fusion(f32[256,512]{1,0:T(8,128)S(1)} %states_parts.3, f16[256,512]{1,0:T(8,128)(2,1)} %collective-permute-done.9, f32[264,512]{1,0:T(8,128)S(1)} %copy-done.1, f32[256]{0:T(256)S(1)} %add_multiply_fusion, f32[256]{0:T(256)S(1)} %bitcast.14), kind=kLoop, calls=%fused_computation.10 | loop fusion | flops 917504 | bytes 1574912 | tf_op jit(solution)/shard_map/convert_element_type | solution.py:430
  52.9 1.1 %collective-permute-start.13 = (bf16[256,512]{1,0:T(8,128)(2,1)S(1)}, bf16[256,512]{1,0:T(8,128)(2,1)S(1)}, u32[]{:S(2)}, u32[]{:S(2)}) collective-permute-start(bf16[256,512]{1,0:T(8,128)(2,1)S(1)} %divide_convert_fusion.refs_0_), channel_id=1, source_target_pairs={{0,8},{4,12},{8,0},{12,4},{1,9},{5,13},{9,1},{13,5},{2,10},{6,14},... | collective-permute-start | bytes 786440 | tf_op jit(solution)/shard_map/ppermute | solution.py:319
  54.0 0.1 pad_add_fusion.columns_ref
  54.1 0.0 collective-permute-start.14
  54.1 0.0 collective-permute-done.1.refs_1_
  54.1 0.0 collective-permute-done.8.refs_2_
  54.1 3.4 %turned.1.held_ref = bf16[1024,1024]{1,0:T(8,128)(2,1)S(1)} custom-call(s32[4]{0:T(128)S(1)} %pad_add_fusion.columns_ref, bf16[256,1024]{1,0:T(8,128)(2,1)} %get-tuple-element.29.first_ref.refs_0_, bf16[512,1024]{1,0:T(8,128)(2,1)S(1)} %collective-permute-done.refs_0_, bf16[256,1024]{1,0:T(8,128)(2,1)} %collective-permute-done.1.refs_1_, ...), custom_call_target="tpu_custom_call" | custom-call | flops 1 | bytes 1 | tf_op jit(solution)/shard_map/turned/pallas_call | solution.py:35
  57.5 3.0 %collective-permute-done.13.refs_1_ = bf16[256,512]{1,0:T(8,128)(2,1)S(1)} collective-permute-done((bf16[256,512]{1,0:T(8,128)(2,1)S(1)}, bf16[256,512]{1,0:T(8,128)(2,1)S(1)}, u32[]{:S(2)}, u32[]{:S(2)}) %collective-permute-start.13) | collective-permute-done | bytes 262176 | tf_op jit(solution)/shard_map/ppermute | solution.py:319
  60.5 0.0 collective-permute-start.15
  60.5 0.0 collective-permute-done.14.refs_2_
  60.5 1.5 %collective-permute-done.15.refs_3_ = bf16[256,512]{1,0:T(8,128)(2,1)S(1)} collective-permute-done((bf16[256,512]{1,0:T(8,128)(2,1)S(1)}, bf16[256,512]{1,0:T(8,128)(2,1)S(1)}, u32[]{:S(2)}, u32[]{:S(2)}) %collective-permute-start.15) | collective-permute-done | bytes 262176 | tf_op jit(solution)/shard_map/ppermute | solution.py:319
  62.0 0.7 gradient_blocks.3
  62.8 2.1 %collective-permute-start.16 = (bf16[256,512]{1,0:T(8,128)(2,1)S(1)}, bf16[256,512]{1,0:T(8,128)(2,1)S(1)}, u32[]{:S(2)}, u32[]{:S(2)}) collective-permute-start(bf16[256,512]{1,0:T(8,128)(2,1)S(1)} %get-tuple-element.50), channel_id=1, source_target_pairs={{0,1},{1,0},{2,3},{3,2},{4,5},{5,4},{6,7},{7,6},{8,9},{9,8},{10,11... | collective-permute-start | bytes 786440 | tf_op jit(solution)/shard_map/ppermute | solution.py:319
  64.8 0.7 collective-permute-start.17
  65.5 4.6 %collective-permute-start.18 = (bf16[256,512]{1,0:T(8,128)(2,1)S(1)}, bf16[256,512]{1,0:T(8,128)(2,1)S(1)}, u32[]{:S(2)}, u32[]{:S(2)}) collective-permute-start(bf16[256,512]{1,0:T(8,128)(2,1)S(1)} %get-tuple-element.51), channel_id=1, source_target_pairs={{0,2},{3,1},{4,6},{7,5},{8,10},{11,9},{12,14},{15,13},{16,18},{19,... | collective-permute-start | bytes 786440 | tf_op jit(solution)/shard_map/ppermute | solution.py:458
  70.1 0.7 gradient_blocks.2
  70.9 0.6 collective-permute-done.16
  71.4 0.1 fusion.5
  71.5 2.3 %collective-permute-start.19 = (bf16[256,512]{1,0:T(8,128)(2,1)S(1)}, bf16[256,512]{1,0:T(8,128)(2,1)S(1)}, u32[]{:S(2)}, u32[]{:S(2)}) collective-permute-start(bf16[256,512]{1,0:T(8,128)(2,1)S(1)} %fusion.5), channel_id=1, source_target_pairs={{1,3},{2,0},{0,1},{3,2},{5,7},{6,4},{4,5},{7,6},{9,11},{10,8},{8,9... | collective-permute-start | bytes 786440 | tf_op jit(solution)/shard_map/ppermute | solution.py:461
  73.8 0.0 collective-permute-done.17
  73.8 3.0 %collective-permute-done.18 = bf16[256,512]{1,0:T(8,128)(2,1)S(1)} collective-permute-done((bf16[256,512]{1,0:T(8,128)(2,1)S(1)}, bf16[256,512]{1,0:T(8,128)(2,1)S(1)}, u32[]{:S(2)}, u32[]{:S(2)}) %collective-permute-start.18) | collective-permute-done | bytes 262176 | tf_op jit(solution)/shard_map/ppermute | solution.py:458
  76.9 8.9 %collective-permute-done.19 = bf16[256,512]{1,0:T(8,128)(2,1)S(1)} collective-permute-done((bf16[256,512]{1,0:T(8,128)(2,1)S(1)}, bf16[256,512]{1,0:T(8,128)(2,1)S(1)}, u32[]{:S(2)}, u32[]{:S(2)}) %collective-permute-start.19) | collective-permute-done | bytes 262176 | tf_op jit(solution)/shard_map/ppermute | solution.py:461
  85.7 1.0 %fusion.3 = f32[256,512]{1,0:T(8,128)} fusion(f32[256,512]{1,0:T(8,128)S(1)} %get-tuple-element.49, bf16[256,512]{1,0:T(8,128)(2,1)S(1)} %collective-permute-done.16, bf16[256,512]{1,0:T(8,128)(2,1)S(1)} %collective-permute-done.19, bf16[256,512]{1,0:T(8,128)(2,1)S(1)} %collective-permute-done.18, bf16[256,512]{1,0:T(8,128)(2,1)S(1)} %collective-permute-done.17, ...), kind=kLoop, calls=%fused_computation.6 | loop fusion | flops 1179648 | bytes 2097153 | tf_op jit(solution)/shard_map/add | solution.py:463
  (13 shorter events, 0.2 us)
Async XLA Ops:
  0.0 16.9 %collective-permute-start.2 = (bf16[256,512]{1,0:T(8,128)(2,1)}, bf16[256,512]{1,0:T(8,128)(2,1)S(1)}, u32[]{:S(2)}, u32[]{:S(2)}) collective-permute-start(bf16[256,512]{1,0:T(8,128)(2,1)} %param.12), channel_id=1, source_target_pairs={{0,1},{1,0},{2,3},{3,2},{4,5},{5,4},{6,7},{7,6},{8,9},{9,8},{10,11... | collective-permute-start | bytes 786440 | tf_op jit(solution)/shard_map/ppermute | solution.py:319
  3.0 14.6 %collective-permute-start.3 = (bf16[256,512]{1,0:T(8,128)(2,1)}, bf16[256,512]{1,0:T(8,128)(2,1)S(1)}, u32[]{:S(2)}, u32[]{:S(2)}) collective-permute-start(bf16[256,512]{1,0:T(8,128)(2,1)} %param.12), channel_id=1, source_target_pairs={{0,2},{1,3},{2,0},{3,1},{4,6},{5,7},{6,4},{7,5},{8,10},{9,11},{10,... | collective-permute-start | bytes 786440 | tf_op jit(solution)/shard_map/ppermute | solution.py:319
  15.2 7.2 %copy-start.3 = (bf16[256,512]{1,0:T(8,128)(2,1)S(1)}, bf16[256,512]{1,0:T(8,128)(2,1)}, u32[]{:S(2)}) copy-start(bf16[256,512]{1,0:T(8,128)(2,1)} %param.12) | copy-start | bytes 786436
  15.2 23.2 %copy-start.4 = (s32[1,1024]{1,0:T(1,128)S(1)}, s32[1,1024]{1,0:T(1,128)}, u32[]{:S(2)}) copy-start(s32[1,1024]{1,0:T(1,128)} %param.13) | copy-start | bytes 12292
  15.2 26.7 %copy-start.2 = (f32[264,512]{1,0:T(8,128)S(1)}, f32[264,512]{1,0:T(8,128)}, u32[]{:S(2)}) copy-start(f32[264,512]{1,0:T(8,128)} %get-tuple-element.42) | copy-start | bytes 1622020
  15.2 27.7 %collective-permute-start = (bf16[512,1024]{1,0:T(8,128)(2,1)}, bf16[512,1024]{1,0:T(8,128)(2,1)S(1)}, u32[]{:S(2)}, u32[]{:S(2)}) collective-permute-start(bf16[512,1024]{1,0:T(8,128)(2,1)} %get-tuple-element.30), channel_id=1, source_target_pairs={{0,8},{4,12},{8,0},{12,4},{1,9},{5,13},{9,1},{13,5},{2,10},{6,14},... | collective-permute-start | bytes 3145736 | tf_op jit(solution)/shard_map/ppermute | solution.py:319
  17.6 21.0 %collective-permute-start.5 = (f16[264,512]{1,0:T(8,128)(2,1)S(1)}, f16[264,512]{1,0:T(8,128)(2,1)S(1)}, u32[]{:S(2)}, u32[]{:S(2)}) collective-permute-start(f16[264,512]{1,0:T(8,128)(2,1)S(1)} %convert_element_type.58), channel_id=1, source_target_pairs={{0,1},{1,0},{2,3},{3,2},{4,5},{5,4},{6,7},{7,6},{8,9},{9,8},{10,11... | collective-permute-start | bytes 811016 | tf_op jit(solution)/shard_map/ppermute | solution.py:319
  18.0 20.3 %collective-permute-start.4 = (bf16[256,512]{1,0:T(8,128)(2,1)S(1)}, bf16[256,512]{1,0:T(8,128)(2,1)S(1)}, u32[]{:S(2)}, u32[]{:S(2)}) collective-permute-start(bf16[256,512]{1,0:T(8,128)(2,1)S(1)} %collective-permute-done.3), channel_id=1, source_target_pairs={{0,1},{1,0},{2,3},{3,2},{4,5},{5,4},{6,7},{7,6},{8,9},{9,8},{10,11... | collective-permute-start | bytes 786440 | tf_op jit(solution)/shard_map/ppermute | solution.py:319
  19.6 19.5 %collective-permute-start.10 = (f16[264,512]{1,0:T(8,128)(2,1)S(1)}, f16[264,512]{1,0:T(8,128)(2,1)S(1)}, u32[]{:S(2)}, u32[]{:S(2)}) collective-permute-start(f16[264,512]{1,0:T(8,128)(2,1)S(1)} %convert_element_type.56), channel_id=1, source_target_pairs={{0,2},{1,3},{2,0},{3,1},{4,6},{5,7},{6,4},{7,5},{8,10},{9,11},{10,... | collective-permute-start | bytes 811016 | tf_op jit(solution)/shard_map/ppermute | solution.py:319
  20.7 21.2 %collective-permute-start.11 = (f16[264,512]{1,0:T(8,128)(2,1)S(1)}, f16[264,512]{1,0:T(8,128)(2,1)S(1)}, u32[]{:S(2)}, u32[]{:S(2)}) collective-permute-start(f16[264,512]{1,0:T(8,128)(2,1)S(1)} %convert_element_type.57), channel_id=1, source_target_pairs={{0,3},{1,2},{2,1},{3,0},{4,7},{5,6},{6,5},{7,4},{8,11},{9,10},{10,... | collective-permute-start | bytes 811016 | tf_op jit(solution)/shard_map/ppermute | solution.py:319
  38.4 4.0 %collective-permute-start.6 = (bf16[768,512]{1,0:T(8,128)(2,1)S(1)}, bf16[768,512]{1,0:T(8,128)(2,1)S(1)}, u32[]{:S(2)}, u32[]{:S(2)}) collective-permute-start(bf16[768,512]{1,0:T(8,128)(2,1)S(1)} %constant_dynamic-update-slice_fusion.refs_1_.refs_2_), channel_id=1, source_target_pairs={{0,4},{4,0},{8,12},{12,8},{1,5},{5,1},{9,13},{13,9},{2,6},{6,2},{1... | collective-permute-start | bytes 2359304 | tf_op jit(solution)/shard_map/ppermute | solution.py:319
  38.6 15.5 %collective-permute-start.1 = (bf16[256,1024]{1,0:T(8,128)(2,1)}, bf16[256,1024]{1,0:T(8,128)(2,1)}, u32[]{:S(2)}, u32[]{:S(2)}) collective-permute-start(bf16[256,1024]{1,0:T(8,128)(2,1)} %get-tuple-element.31.refs_1_), channel_id=1, source_target_pairs={{0,4},{4,0},{8,12},{12,8},{1,5},{5,1},{9,13},{13,9},{2,6},{6,2},{1... | collective-permute-start | bytes 1572872 | tf_op jit(solution)/shard_map/ppermute | solution.py:319
  39.1 3.2 %collective-permute-start.7 = (bf16[256,512]{1,0:T(8,128)(2,1)S(1)}, bf16[256,512]{1,0:T(8,128)(2,1)S(1)}, u32[]{:S(2)}, u32[]{:S(2)}) collective-permute-start(bf16[256,512]{1,0:T(8,128)(2,1)S(1)} %collective-permute-done.4.refs_2_.refs_3_), channel_id=1, source_target_pairs={{0,4},{4,0},{8,12},{12,8},{1,5},{5,1},{9,13},{13,9},{2,6},{6,2},{1... | collective-permute-start | bytes 786440 | tf_op jit(solution)/shard_map/ppermute | solution.py:319
  42.1 0.8 copy-start
  44.8 7.0 %collective-permute-start.9 = (f16[256,512]{1,0:T(8,128)(2,1)S(1)}, f16[256,512]{1,0:T(8,128)(2,1)}, u32[]{:S(2)}, u32[]{:S(2)}) collective-permute-start(f16[256,512]{1,0:T(8,128)(2,1)S(1)} %convert_element_type.59), channel_id=1, source_target_pairs={{0,8},{4,12},{8,0},{12,4},{1,9},{5,13},{9,1},{13,5},{2,10},{6,14},... | collective-permute-start | bytes 786440 | tf_op jit(solution)/shard_map/ppermute | solution.py:319
  46.3 4.2 %collective-permute-start.12 = (f32[256]{0:T(256)S(1)}, f32[256]{0:T(256)S(1)}, u32[]{:S(2)}, u32[]{:S(2)}) collective-permute-start(f32[256]{0:T(256)S(1)} %multiply_reduce_fusion), channel_id=1, source_target_pairs={{0,16},{16,0},{1,17},{17,1},{2,18},{18,2},{3,19},{19,3},{4,20},{20... | collective-permute-start | bytes 3080 | tf_op jit(solution)/shard_map/ppermute | solution.py:319
  47.9 3.8 %copy-start.1 = (f32[264,512]{1,0:T(8,128)S(1)}, f32[264,512]{1,0:T(8,128)}, u32[]{:S(2)}) copy-start(f32[264,512]{1,0:T(8,128)} %copy-done) | copy-start | bytes 1622020
  47.9 6.2 %collective-permute-start.8 = (bf16[256,1024]{1,0:T(8,128)(2,1)}, bf16[256,1024]{1,0:T(8,128)(2,1)}, u32[]{:S(2)}, u32[]{:S(2)}) collective-permute-start(bf16[256,1024]{1,0:T(8,128)(2,1)} %get-tuple-element.40), channel_id=1, source_target_pairs={{0,4},{4,0},{8,12},{12,8},{1,5},{5,1},{9,13},{13,9},{2,6},{6,2},{1... | collective-permute-start | bytes 1572872 | tf_op jit(solution)/shard_map/ppermute | solution.py:319
  52.9 7.6 %collective-permute-start.13 = (bf16[256,512]{1,0:T(8,128)(2,1)S(1)}, bf16[256,512]{1,0:T(8,128)(2,1)S(1)}, u32[]{:S(2)}, u32[]{:S(2)}) collective-permute-start(bf16[256,512]{1,0:T(8,128)(2,1)S(1)} %divide_convert_fusion.refs_0_), channel_id=1, source_target_pairs={{0,8},{4,12},{8,0},{12,4},{1,9},{5,13},{9,1},{13,5},{2,10},{6,14},... | collective-permute-start | bytes 786440 | tf_op jit(solution)/shard_map/ppermute | solution.py:319
  54.1 6.4 %collective-permute-start.14 = (bf16[256,512]{1,0:T(8,128)(2,1)S(1)}, bf16[256,512]{1,0:T(8,128)(2,1)S(1)}, u32[]{:S(2)}, u32[]{:S(2)}) collective-permute-start(bf16[256,512]{1,0:T(8,128)(2,1)S(1)} %divide_convert_fusion.refs_0_), channel_id=1, source_target_pairs={{0,4},{4,0},{8,12},{12,8},{1,5},{5,1},{9,13},{13,9},{2,6},{6,2},{1... | collective-permute-start | bytes 786440 | tf_op jit(solution)/shard_map/ppermute | solution.py:319
  60.5 1.5 %collective-permute-start.15 = (bf16[256,512]{1,0:T(8,128)(2,1)S(1)}, bf16[256,512]{1,0:T(8,128)(2,1)S(1)}, u32[]{:S(2)}, u32[]{:S(2)}) collective-permute-start(bf16[256,512]{1,0:T(8,128)(2,1)S(1)} %collective-permute-done.13.refs_1_), channel_id=1, source_target_pairs={{0,4},{4,0},{8,12},{12,8},{1,5},{5,1},{9,13},{13,9},{2,6},{6,2},{1... | collective-permute-start | bytes 786440 | tf_op jit(solution)/shard_map/ppermute | solution.py:319
  62.8 8.7 %collective-permute-start.16 = (bf16[256,512]{1,0:T(8,128)(2,1)S(1)}, bf16[256,512]{1,0:T(8,128)(2,1)S(1)}, u32[]{:S(2)}, u32[]{:S(2)}) collective-permute-start(bf16[256,512]{1,0:T(8,128)(2,1)S(1)} %get-tuple-element.50), channel_id=1, source_target_pairs={{0,1},{1,0},{2,3},{3,2},{4,5},{5,4},{6,7},{7,6},{8,9},{9,8},{10,11... | collective-permute-start | bytes 786440 | tf_op jit(solution)/shard_map/ppermute | solution.py:319
  64.8 9.0 %collective-permute-start.17 = (bf16[256,512]{1,0:T(8,128)(2,1)S(1)}, bf16[256,512]{1,0:T(8,128)(2,1)S(1)}, u32[]{:S(2)}, u32[]{:S(2)}) collective-permute-start(bf16[256,512]{1,0:T(8,128)(2,1)S(1)} %get-tuple-element.51), channel_id=1, source_target_pairs={{1,2},{2,1},{5,6},{6,5},{9,10},{10,9},{13,14},{14,13},{17,18},{18,... | collective-permute-start | bytes 786440 | tf_op jit(solution)/shard_map/ppermute | solution.py:459
  65.5 11.4 %collective-permute-start.18 = (bf16[256,512]{1,0:T(8,128)(2,1)S(1)}, bf16[256,512]{1,0:T(8,128)(2,1)S(1)}, u32[]{:S(2)}, u32[]{:S(2)}) collective-permute-start(bf16[256,512]{1,0:T(8,128)(2,1)S(1)} %get-tuple-element.51), channel_id=1, source_target_pairs={{0,2},{3,1},{4,6},{7,5},{8,10},{11,9},{12,14},{15,13},{16,18},{19,... | collective-permute-start | bytes 786440 | tf_op jit(solution)/shard_map/ppermute | solution.py:458
  71.5 14.2 %collective-permute-start.19 = (bf16[256,512]{1,0:T(8,128)(2,1)S(1)}, bf16[256,512]{1,0:T(8,128)(2,1)S(1)}, u32[]{:S(2)}, u32[]{:S(2)}) collective-permute-start(bf16[256,512]{1,0:T(8,128)(2,1)S(1)} %fusion.5), channel_id=1, source_target_pairs={{1,3},{2,0},{0,1},{3,2},{5,7},{6,4},{4,5},{7,6},{9,11},{10,8},{8,9... | collective-permute-start | bytes 786440 | tf_op jit(solution)/shard_map/ppermute | solution.py:461

commit v6 on v5

--- a/solution.py
+++ b/solution.py
@@ -71,7 +71,7 @@
     rows = tok // pieces
     shared = cores + chips - 1
 
-    def kernel(places_ref, student_ref, hidden_ref, value_ref, student_gain_ref, gain_ref, *refs):
+    def kernel(places_ref, student_ref, hidden_ref, value_ref, gains_ref, *refs):
         feature_outs, out_refs = refs[:shared], list(refs[shared : shared + number])
         student_held, held, value_held, scaled, square_ref, kept_ref, sems = refs[-7:]
         feature_refs = refs[shared + number : -7]
@@ -111,7 +111,7 @@
                 for c in range(0, wide, chunk):
                     src = pl.ds(pl.multiple_of(base + c, chunk), chunk)
                     part = student_held[at, src].astype(jnp.float32) * scale
-                    part = part * student_gain_ref[:, src].astype(jnp.float32)
+                    part = part * gains_ref[:, src].astype(jnp.float32)
                     feature_ref[to, c : c + chunk] = part.astype(jnp.bfloat16)
             return 0
 
@@ -136,7 +136,7 @@
                 for c in range(0, depth, deep):
                     part = held[i, at, c : c + deep].astype(jnp.float32)
                     lanes = lane_sum(part * part, lanes)
-                    part = part * gain_ref[:, c : c + deep].astype(jnp.float32)
+                    part = part * gains_ref[:, ds + c : ds + c + deep].astype(jnp.float32)
                     scaled[to, c : c + deep] = part.astype(jnp.bfloat16)
                 square_ref[to, :] = lanes
                 return 0
@@ -173,7 +173,7 @@
     results = call(
         kernel,
         places,
-        [student, hidden, value, student_gain.reshape(1, ds), gain.reshape(1, depth)],
+        [student, hidden, value, jnp.concatenate([student_gain, gain]).reshape(1, ds + depth)],
         3,
         feature_shapes + [((tok + EXTRA_ROWS, kv), jnp.float32)] * number,
         [pltpu.VMEM(shape, dtype) for shape, dtype in feature_shapes]

time: 87.1 us -> 87 us (level)
  local copies, waits for them, and re-layouts: 2.13 us -> 0.75 us
    reshape x2 -> x1, local copies, waits for them, and re-layouts: 1.4 us -> 0.02 us  [prepare(): jnp.concatenate([student_gain, gain]).reshape(1, ds + depth)]
where the time goes in v6:
time: 87 us; the launch traced here: 86.7 us
  waiting for transfers between devices  37.6 us (43%)
  starting transfers between devices  27.1 us (31%)
  Pallas kernels  17.1 us (20%)
  other arithmetic  3.89 us (4%)
    ppermute x17, waiting for transfers between devices, swap(): lax.ppermute(value, axis, [(i, i ^ step) for i in range(sizes[axis])])  25.7 us
    ppermute x17, starting transfers between devices, swap(): lax.ppermute(value, axis, [(i, i ^ step) for i in range(sizes[axis])])  19.4 us
    pallas_call x6, Pallas kernels, call(): pl.pallas_call(kernel, out_shape=[(pltpu.HBM if n in out_hbm else pltpu.V...  17.1 us
    ppermute x1, waiting for transfers between devices, per_device(): last = lax.ppermute(last, 'mp', [(1, 3), (2, 0), (0, 1), (3, 2)])  8.85 us
    ppermute x1, starting transfers between devices, per_device(): past = lax.ppermute(parts[1], 'mp', [(0, 2), (3, 1)])  4.64 us
    ppermute x1, waiting for transfers between devices, per_device(): past = lax.ppermute(parts[1], 'mp', [(0, 2), (3, 1)])  3.05 us
    ppermute x1, starting transfers between devices, per_device(): last = lax.ppermute(last, 'mp', [(1, 3), (2, 0), (0, 1), (3, 2)])  2.34 us
  transfers between devices with their start and end apart: 20, of which 9 were waited for; matrix products, arithmetic and copies ran while one was open for 4% of the time, Pallas kernels for 19%

profile of v6, /device:TPU:0, one launch (start us, length us, event | category | flops | bytes accessed | tf_op | source)
XLA Modules:
  0.0 86.7 jit_solution(949551234775537073)
XLA Ops:
  0.0 3.0 %collective-permute-start.2 = (bf16[256,512]{1,0:T(8,128)(2,1)}, bf16[256,512]{1,0:T(8,128)(2,1)S(1)}, u32[]{:S(2)}, u32[]{:S(2)}) collective-permute-start(bf16[256,512]{1,0:T(8,128)(2,1)} %param.12), channel_id=1, source_target_pairs={{0,1},{1,0},{2,3},{3,2},{4,5},{5,4},{6,7},{7,6},{8,9},{9,8},{10,11... | collective-permute-start | bytes 786440 | tf_op jit(solution)/shard_map/ppermute | solution.py:319
  3.0 2.6 %collective-permute-start.3 = (bf16[256,512]{1,0:T(8,128)(2,1)}, bf16[256,512]{1,0:T(8,128)(2,1)S(1)}, u32[]{:S(2)}, u32[]{:S(2)}) collective-permute-start(bf16[256,512]{1,0:T(8,128)(2,1)} %param.12), channel_id=1, source_target_pairs={{0,2},{1,3},{2,0},{3,1},{4,6},{5,7},{6,4},{7,5},{8,10},{9,11},{10,... | collective-permute-start | bytes 786440 | tf_op jit(solution)/shard_map/ppermute | solution.py:319
  5.6 0.7 pad_maximum_fusion
  6.4 0.1 stack.51.places_ref
  6.5 8.1 %prepare.1 = (bf16[256,1024]{1,0:T(8,128)(2,1)}, bf16[256,1024]{1,0:T(8,128)(2,1)}, bf16[512,1024]{1,0:T(8,128)(2,1)}, f32[264,512]{1,0:T(8,128)S(1)}, f32[264,5...) custom-call(s32[6]{0:T(128)S(1)} %stack.51.places_ref, bf16[256,4096]{1,0:T(8,128)(2,1)} %student_ref.1, ...), custom_call_target="tpu_custom_call" | custom-call | flops 1 | bytes 1 | tf_op jit(solution)/shard_map/prepare/pallas_call | solution.py:35
  14.6 0.0 copy-start.3
  14.6 0.0 copy-start.4
  14.6 0.0 copy-start.2
  14.6 1.6 %collective-permute-start = (bf16[512,1024]{1,0:T(8,128)(2,1)}, bf16[512,1024]{1,0:T(8,128)(2,1)S(1)}, u32[]{:S(2)}, u32[]{:S(2)}) collective-permute-start(bf16[512,1024]{1,0:T(8,128)(2,1)} %get-tuple-element.30), channel_id=1, source_target_pairs={{0,8},{4,12},{8,0},{12,4},{1,9},{5,13},{9,1},{13,5},{2,10},{6,14},... | collective-permute-start | bytes 3145736 | tf_op jit(solution)/shard_map/ppermute | solution.py:319
  16.3 0.0 collective-permute-done.2
  16.3 1.3 %collective-permute-done.3 = bf16[256,512]{1,0:T(8,128)(2,1)S(1)} collective-permute-done((bf16[256,512]{1,0:T(8,128)(2,1)}, bf16[256,512]{1,0:T(8,128)(2,1)S(1)}, u32[]{:S(2)}, u32[]{:S(2)}) %collective-permute-start.3) | collective-permute-done | bytes 262176 | tf_op jit(solution)/shard_map/ppermute | solution.py:319
  17.6 0.4 collective-permute-start.5
  18.0 1.6 %collective-permute-start.4 = (bf16[256,512]{1,0:T(8,128)(2,1)S(1)}, bf16[256,512]{1,0:T(8,128)(2,1)S(1)}, u32[]{:S(2)}, u32[]{:S(2)}) collective-permute-start(bf16[256,512]{1,0:T(8,128)(2,1)S(1)} %collective-permute-done.3), channel_id=1, source_target_pairs={{0,1},{1,0},{2,3},{3,2},{4,5},{5,4},{6,7},{7,6},{8,9},{9,8},{10,11... | collective-permute-start | bytes 786440 | tf_op jit(solution)/shard_map/ppermute | solution.py:319
  19.6 1.1 %collective-permute-start.10 = (f16[264,512]{1,0:T(8,128)(2,1)S(1)}, f16[264,512]{1,0:T(8,128)(2,1)S(1)}, u32[]{:S(2)}, u32[]{:S(2)}) collective-permute-start(f16[264,512]{1,0:T(8,128)(2,1)S(1)} %convert_element_type.56), channel_id=1, source_target_pairs={{0,2},{1,3},{2,0},{3,1},{4,6},{5,7},{6,4},{7,5},{8,10},{9,11},{10,... | collective-permute-start | bytes 811016 | tf_op jit(solution)/shard_map/ppermute | solution.py:319
  20.7 1.7 %collective-permute-start.11 = (f16[264,512]{1,0:T(8,128)(2,1)S(1)}, f16[264,512]{1,0:T(8,128)(2,1)S(1)}, u32[]{:S(2)}, u32[]{:S(2)}) collective-permute-start(f16[264,512]{1,0:T(8,128)(2,1)S(1)} %convert_element_type.57), channel_id=1, source_target_pairs={{0,3},{1,2},{2,1},{3,0},{4,7},{5,6},{6,5},{7,4},{8,11},{9,10},{10,... | collective-permute-start | bytes 811016 | tf_op jit(solution)/shard_map/ppermute | solution.py:319
  22.5 14.6 %collective-permute-done.4.refs_2_.refs_3_ = bf16[256,512]{1,0:T(8,128)(2,1)S(1)} collective-permute-done((bf16[256,512]{1,0:T(8,128)(2,1)S(1)}, bf16[256,512]{1,0:T(8,128)(2,1)S(1)}, u32[]{:S(2)}, u32[]{:S(2)}) %collective-permute-start.4) | collective-permute-done | bytes 262176 | tf_op jit(solution)/shard_map/ppermute | solution.py:319
  37.1 0.0 collective-permute-start.6
  37.1 0.1 pad_add_fusion.1.columns_ref
  37.1 0.1 convert_reduce_fusion
  37.3 0.0 collective-permute-done.5
  37.3 0.6 collective-permute-start.1
  37.8 0.0 collective-permute-done.10
  37.8 0.1 collective-permute-start.7
  37.9 4.0 %collective-permute-done.11 = f16[264,512]{1,0:T(8,128)(2,1)S(1)} collective-permute-done((f16[264,512]{1,0:T(8,128)(2,1)S(1)}, f16[264,512]{1,0:T(8,128)(2,1)S(1)}, u32[]{:S(2)}, u32[]{:S(2)}) %collective-permute-start.11) | collective-permute-done | bytes 270368 | tf_op jit(solution)/shard_map/ppermute | solution.py:319
  41.9 0.2 convert_add_fusion
  42.1 0.0 copy-start
  42.1 0.2 multiply_reduce_fusion
  42.4 0.0 collective-permute-done.7.refs_4_.refs_5_
  42.4 0.0 collective-permute-done.6.refs_3_.refs_4_
  42.4 0.6 copy-done
  42.9 0.0 collective-permute-done.refs_0_
  42.9 1.8 %states_parts.2 = (f32[256,512]{1,0:T(8,128)S(1)}, bf16[256,1024]{1,0:T(8,128)(2,1)}) custom-call(s32[4]{0:T(128)S(1)} %pad_add_fusion.1.columns_ref, bf16[512,1024]{1,0:T(8,128)(2,1)S(1)} %collective-permute-done.refs_0_, bf16[768,512]{1,0:T(8,128)(2,1)S(1)} %constant_dynamic-update-slice_fusion.refs_1_.refs_2_, ...), custom_call_target="tpu_custom_call" | custom-call | flops 1 | bytes 1 | tf_op jit(solution)/shard_map/states_parts/pallas_call | solution.py:35
  44.8 1.6 %collective-permute-start.9 = (f16[256,512]{1,0:T(8,128)(2,1)S(1)}, f16[256,512]{1,0:T(8,128)(2,1)}, u32[]{:S(2)}, u32[]{:S(2)}) collective-permute-start(f16[256,512]{1,0:T(8,128)(2,1)S(1)} %convert_element_type.59), channel_id=1, source_target_pairs={{0,8},{4,12},{8,0},{12,4},{1,9},{5,13},{9,1},{13,5},{2,10},{6,14},... | collective-permute-start | bytes 786440 | tf_op jit(solution)/shard_map/ppermute | solution.py:319
  46.3 1.5 %collective-permute-start.12 = (f32[256]{0:T(256)S(1)}, f32[256]{0:T(256)S(1)}, u32[]{:S(2)}, u32[]{:S(2)}) collective-permute-start(f32[256]{0:T(256)S(1)} %multiply_reduce_fusion), channel_id=1, source_target_pairs={{0,16},{16,0},{1,17},{17,1},{2,18},{18,2},{3,19},{19,3},{4,20},{20... | collective-permute-start | bytes 3080 | tf_op jit(solution)/shard_map/ppermute | solution.py:319
  47.8 0.1 select_reduce_fusion
  47.9 0.1 collective-permute-start.8
  48.0 2.5 %states_parts.3 = f32[256,512]{1,0:T(8,128)S(1)} custom-call(s32[4]{0:T(128)S(1)} %pad_add_fusion.1.columns_ref, bf16[256,1024]{1,0:T(8,128)(2,1)} %get-tuple-element.29.first_ref.refs_0_, bf16[256,1024]{1,0:T(8,128)(2,1)} %get-tuple-element.31.refs_1_, bf16[768,512]{1,0:T(8,128)(2,1)S(1)} %constant_dynamic-update-slice_fusion.refs_1_.refs_2_, ...), custom_call_target="tpu_custom_call" | custom-call | flops 1 | bytes 1 | tf_op jit(solution)/shard_map/states_parts/pallas_call | solution.py:35
  50.5 0.0 collective-permute-done.12
  50.5 0.1 add_multiply_fusion
  50.6 0.7 collective-permute-done.9
  51.3 0.0 copy-done.1
  51.3 1.1 %divide_convert_fusion.refs_0_ = bf16[256,512]{1,0:T(8,128)(2,1)S(1)} fusion(f32[256,512]{1,0:T(8,128)S(1)} %states_parts.3, f16[256,512]{1,0:T(8,128)(2,1)} %collective-permute-done.9, f32[264,512]{1,0:T(8,128)S(1)} %copy-done.1, f32[256]{0:T(256)S(1)} %add_multiply_fusion, f32[256]{0:T(256)S(1)} %bitcast.14), kind=kLoop, calls=%fused_computation.10 | loop fusion | flops 917504 | bytes 1574912 | tf_op jit(solution)/shard_map/convert_element_type | solution.py:430
  52.4 1.6 %collective-permute-start.13 = (bf16[256,512]{1,0:T(8,128)(2,1)S(1)}, bf16[256,512]{1,0:T(8,128)(2,1)S(1)}, u32[]{:S(2)}, u32[]{:S(2)}) collective-permute-start(bf16[256,512]{1,0:T(8,128)(2,1)S(1)} %divide_convert_fusion.refs_0_), channel_id=1, source_target_pairs={{0,8},{4,12},{8,0},{12,4},{1,9},{5,13},{9,1},{13,5},{2,10},{6,14},... | collective-permute-start | bytes 786440 | tf_op jit(solution)/shard_map/ppermute | solution.py:319
  54.0 0.1 pad_add_fusion.columns_ref
  54.1 0.0 collective-permute-start.14
  54.1 0.0 collective-permute-done.1.refs_1_
  54.1 0.0 collective-permute-done.8.refs_2_
  54.1 3.4 %turned.1.held_ref = bf16[1024,1024]{1,0:T(8,128)(2,1)S(1)} custom-call(s32[4]{0:T(128)S(1)} %pad_add_fusion.columns_ref, bf16[256,1024]{1,0:T(8,128)(2,1)} %get-tuple-element.29.first_ref.refs_0_, bf16[512,1024]{1,0:T(8,128)(2,1)S(1)} %collective-permute-done.refs_0_, bf16[256,1024]{1,0:T(8,128)(2,1)} %collective-permute-done.1.refs_1_, ...), custom_call_target="tpu_custom_call" | custom-call | flops 1 | bytes 1 | tf_op jit(solution)/shard_map/turned/pallas_call | solution.py:35
  57.5 3.0 %collective-permute-done.13.refs_1_ = bf16[256,512]{1,0:T(8,128)(2,1)S(1)} collective-permute-done((bf16[256,512]{1,0:T(8,128)(2,1)S(1)}, bf16[256,512]{1,0:T(8,128)(2,1)S(1)}, u32[]{:S(2)}, u32[]{:S(2)}) %collective-permute-start.13) | collective-permute-done | bytes 262176 | tf_op jit(solution)/shard_map/ppermute | solution.py:319
  60.5 0.0 collective-permute-start.15
  60.5 0.0 collective-permute-done.14.refs_2_
  60.5 1.5 %collective-permute-done.15.refs_3_ = bf16[256,512]{1,0:T(8,128)(2,1)S(1)} collective-permute-done((bf16[256,512]{1,0:T(8,128)(2,1)S(1)}, bf16[256,512]{1,0:T(8,128)(2,1)S(1)}, u32[]{:S(2)}, u32[]{:S(2)}) %collective-permute-start.15) | collective-permute-done | bytes 262176 | tf_op jit(solution)/shard_map/ppermute | solution.py:319
  62.0 0.7 gradient_blocks.3
  62.8 2.1 %collective-permute-start.16 = (bf16[256,512]{1,0:T(8,128)(2,1)S(1)}, bf16[256,512]{1,0:T(8,128)(2,1)S(1)}, u32[]{:S(2)}, u32[]{:S(2)}) collective-permute-start(bf16[256,512]{1,0:T(8,128)(2,1)S(1)} %get-tuple-element.50), channel_id=1, source_target_pairs={{0,1},{1,0},{2,3},{3,2},{4,5},{5,4},{6,7},{7,6},{8,9},{9,8},{10,11... | collective-permute-start | bytes 786440 | tf_op jit(solution)/shard_map/ppermute | solution.py:319
  64.8 0.7 collective-permute-start.17
  65.5 4.6 %collective-permute-start.18 = (bf16[256,512]{1,0:T(8,128)(2,1)S(1)}, bf16[256,512]{1,0:T(8,128)(2,1)S(1)}, u32[]{:S(2)}, u32[]{:S(2)}) collective-permute-start(bf16[256,512]{1,0:T(8,128)(2,1)S(1)} %get-tuple-element.51), channel_id=1, source_target_pairs={{0,2},{3,1},{4,6},{7,5},{8,10},{11,9},{12,14},{15,13},{16,18},{19,... | collective-permute-start | bytes 786440 | tf_op jit(solution)/shard_map/ppermute | solution.py:458
  70.1 0.7 gradient_blocks.2
  70.9 0.6 collective-permute-done.16
  71.4 0.1 fusion.5
  71.5 2.3 %collective-permute-start.19 = (bf16[256,512]{1,0:T(8,128)(2,1)S(1)}, bf16[256,512]{1,0:T(8,128)(2,1)S(1)}, u32[]{:S(2)}, u32[]{:S(2)}) collective-permute-start(bf16[256,512]{1,0:T(8,128)(2,1)S(1)} %fusion.5), channel_id=1, source_target_pairs={{1,3},{2,0},{0,1},{3,2},{5,7},{6,4},{4,5},{7,6},{9,11},{10,8},{8,9... | collective-permute-start | bytes 786440 | tf_op jit(solution)/shard_map/ppermute | solution.py:461
  73.8 0.0 collective-permute-done.17
  73.8 3.0 %collective-permute-done.18 = bf16[256,512]{1,0:T(8,128)(2,1)S(1)} collective-permute-done((bf16[256,512]{1,0:T(8,128)(2,1)S(1)}, bf16[256,512]{1,0:T(8,128)(2,1)S(1)}, u32[]{:S(2)}, u32[]{:S(2)}) %collective-permute-start.18) | collective-permute-done | bytes 262176 | tf_op jit(solution)/shard_map/ppermute | solution.py:458
  76.9 8.9 %collective-permute-done.19 = bf16[256,512]{1,0:T(8,128)(2,1)S(1)} collective-permute-done((bf16[256,512]{1,0:T(8,128)(2,1)S(1)}, bf16[256,512]{1,0:T(8,128)(2,1)S(1)}, u32[]{:S(2)}, u32[]{:S(2)}) %collective-permute-start.19) | collective-permute-done | bytes 262176 | tf_op jit(solution)/shard_map/ppermute | solution.py:461
  85.7 1.0 %fusion.3 = f32[256,512]{1,0:T(8,128)} fusion(f32[256,512]{1,0:T(8,128)S(1)} %get-tuple-element.49, bf16[256,512]{1,0:T(8,128)(2,1)S(1)} %collective-permute-done.16, bf16[256,512]{1,0:T(8,128)(2,1)S(1)} %collective-permute-done.19, bf16[256,512]{1,0:T(8,128)(2,1)S(1)} %collective-permute-done.18, bf16[256,512]{1,0:T(8,128)(2,1)S(1)} %collective-permute-done.17, ...), kind=kLoop, calls=%fused_computation.6 | loop fusion | flops 1179648 | bytes 2097153 | tf_op jit(solution)/shard_map/add | solution.py:463
  (13 shorter events, 0.2 us)
Async XLA Ops:
  0.0 16.3 %collective-permute-start.2 = (bf16[256,512]{1,0:T(8,128)(2,1)}, bf16[256,512]{1,0:T(8,128)(2,1)S(1)}, u32[]{:S(2)}, u32[]{:S(2)}) collective-permute-start(bf16[256,512]{1,0:T(8,128)(2,1)} %param.12), channel_id=1, source_target_pairs={{0,1},{1,0},{2,3},{3,2},{4,5},{5,4},{6,7},{7,6},{8,9},{9,8},{10,11... | collective-permute-start | bytes 786440 | tf_op jit(solution)/shard_map/ppermute | solution.py:319
  3.0 14.6 %collective-permute-start.3 = (bf16[256,512]{1,0:T(8,128)(2,1)}, bf16[256,512]{1,0:T(8,128)(2,1)S(1)}, u32[]{:S(2)}, u32[]{:S(2)}) collective-permute-start(bf16[256,512]{1,0:T(8,128)(2,1)} %param.12), channel_id=1, source_target_pairs={{0,2},{1,3},{2,0},{3,1},{4,6},{5,7},{6,4},{7,5},{8,10},{9,11},{10,... | collective-permute-start | bytes 786440 | tf_op jit(solution)/shard_map/ppermute | solution.py:319
  14.6 7.8 %copy-start.3 = (bf16[256,512]{1,0:T(8,128)(2,1)S(1)}, bf16[256,512]{1,0:T(8,128)(2,1)}, u32[]{:S(2)}) copy-start(bf16[256,512]{1,0:T(8,128)(2,1)} %param.12) | copy-start | bytes 786436
  14.6 22.6 %copy-start.4 = (s32[1,1024]{1,0:T(1,128)S(1)}, s32[1,1024]{1,0:T(1,128)}, u32[]{:S(2)}) copy-start(s32[1,1024]{1,0:T(1,128)} %param.13) | copy-start | bytes 12292
  14.6 27.4 %copy-start.2 = (f32[264,512]{1,0:T(8,128)S(1)}, f32[264,512]{1,0:T(8,128)}, u32[]{:S(2)}) copy-start(f32[264,512]{1,0:T(8,128)} %get-tuple-element.42) | copy-start | bytes 1622020
  14.6 28.3 %collective-permute-start = (bf16[512,1024]{1,0:T(8,128)(2,1)}, bf16[512,1024]{1,0:T(8,128)(2,1)S(1)}, u32[]{:S(2)}, u32[]{:S(2)}) collective-permute-start(bf16[512,1024]{1,0:T(8,128)(2,1)} %get-tuple-element.30), channel_id=1, source_target_pairs={{0,8},{4,12},{8,0},{12,4},{1,9},{5,13},{9,1},{13,5},{2,10},{6,14},... | collective-permute-start | bytes 3145736 | tf_op jit(solution)/shard_map/ppermute | solution.py:319
  17.6 19.7 %collective-permute-start.5 = (f16[264,512]{1,0:T(8,128)(2,1)S(1)}, f16[264,512]{1,0:T(8,128)(2,1)S(1)}, u32[]{:S(2)}, u32[]{:S(2)}) collective-permute-start(f16[264,512]{1,0:T(8,128)(2,1)S(1)} %convert_element_type.58), channel_id=1, source_target_pairs={{0,1},{1,0},{2,3},{3,2},{4,5},{5,4},{6,7},{7,6},{8,9},{9,8},{10,11... | collective-permute-start | bytes 811016 | tf_op jit(solution)/shard_map/ppermute | solution.py:319
  18.0 19.0 %collective-permute-start.4 = (bf16[256,512]{1,0:T(8,128)(2,1)S(1)}, bf16[256,512]{1,0:T(8,128)(2,1)S(1)}, u32[]{:S(2)}, u32[]{:S(2)}) collective-permute-start(bf16[256,512]{1,0:T(8,128)(2,1)S(1)} %collective-permute-done.3), channel_id=1, source_target_pairs={{0,1},{1,0},{2,3},{3,2},{4,5},{5,4},{6,7},{7,6},{8,9},{9,8},{10,11... | collective-permute-start | bytes 786440 | tf_op jit(solution)/shard_map/ppermute | solution.py:319
  19.6 18.2 %collective-permute-start.10 = (f16[264,512]{1,0:T(8,128)(2,1)S(1)}, f16[264,512]{1,0:T(8,128)(2,1)S(1)}, u32[]{:S(2)}, u32[]{:S(2)}) collective-permute-start(f16[264,512]{1,0:T(8,128)(2,1)S(1)} %convert_element_type.56), channel_id=1, source_target_pairs={{0,2},{1,3},{2,0},{3,1},{4,6},{5,7},{6,4},{7,5},{8,10},{9,11},{10,... | collective-permute-start | bytes 811016 | tf_op jit(solution)/shard_map/ppermute | solution.py:319
  20.7 21.2 %collective-permute-start.11 = (f16[264,512]{1,0:T(8,128)(2,1)S(1)}, f16[264,512]{1,0:T(8,128)(2,1)S(1)}, u32[]{:S(2)}, u32[]{:S(2)}) collective-permute-start(f16[264,512]{1,0:T(8,128)(2,1)S(1)} %convert_element_type.57), channel_id=1, source_target_pairs={{0,3},{1,2},{2,1},{3,0},{4,7},{5,6},{6,5},{7,4},{8,11},{9,10},{10,... | collective-permute-start | bytes 811016 | tf_op jit(solution)/shard_map/ppermute | solution.py:319
  37.1 5.3 %collective-permute-start.6 = (bf16[768,512]{1,0:T(8,128)(2,1)S(1)}, bf16[768,512]{1,0:T(8,128)(2,1)S(1)}, u32[]{:S(2)}, u32[]{:S(2)}) collective-permute-start(bf16[768,512]{1,0:T(8,128)(2,1)S(1)} %constant_dynamic-update-slice_fusion.refs_1_.refs_2_), channel_id=1, source_target_pairs={{0,4},{4,0},{8,12},{12,8},{1,5},{5,1},{9,13},{13,9},{2,6},{6,2},{1... | collective-permute-start | bytes 2359304 | tf_op jit(solution)/shard_map/ppermute | solution.py:319
  37.3 16.8 %collective-permute-start.1 = (bf16[256,1024]{1,0:T(8,128)(2,1)}, bf16[256,1024]{1,0:T(8,128)(2,1)}, u32[]{:S(2)}, u32[]{:S(2)}) collective-permute-start(bf16[256,1024]{1,0:T(8,128)(2,1)} %get-tuple-element.31.refs_1_), channel_id=1, source_target_pairs={{0,4},{4,0},{8,12},{12,8},{1,5},{5,1},{9,13},{13,9},{2,6},{6,2},{1... | collective-permute-start | bytes 1572872 | tf_op jit(solution)/shard_map/ppermute | solution.py:319
  37.8 4.5 %collective-permute-start.7 = (bf16[256,512]{1,0:T(8,128)(2,1)S(1)}, bf16[256,512]{1,0:T(8,128)(2,1)S(1)}, u32[]{:S(2)}, u32[]{:S(2)}) collective-permute-start(bf16[256,512]{1,0:T(8,128)(2,1)S(1)} %collective-permute-done.4.refs_2_.refs_3_), channel_id=1, source_target_pairs={{0,4},{4,0},{8,12},{12,8},{1,5},{5,1},{9,13},{13,9},{2,6},{6,2},{1... | collective-permute-start | bytes 786440 | tf_op jit(solution)/shard_map/ppermute | solution.py:319
  42.1 0.8 copy-start
  44.8 6.5 %collective-permute-start.9 = (f16[256,512]{1,0:T(8,128)(2,1)S(1)}, f16[256,512]{1,0:T(8,128)(2,1)}, u32[]{:S(2)}, u32[]{:S(2)}) collective-permute-start(f16[256,512]{1,0:T(8,128)(2,1)S(1)} %convert_element_type.59), channel_id=1, source_target_pairs={{0,8},{4,12},{8,0},{12,4},{1,9},{5,13},{9,1},{13,5},{2,10},{6,14},... | collective-permute-start | bytes 786440 | tf_op jit(solution)/shard_map/ppermute | solution.py:319
  46.3 4.2 %collective-permute-start.12 = (f32[256]{0:T(256)S(1)}, f32[256]{0:T(256)S(1)}, u32[]{:S(2)}, u32[]{:S(2)}) collective-permute-start(f32[256]{0:T(256)S(1)} %multiply_reduce_fusion), channel_id=1, source_target_pairs={{0,16},{16,0},{1,17},{17,1},{2,18},{18,2},{3,19},{19,3},{4,20},{20... | collective-permute-start | bytes 3080 | tf_op jit(solution)/shard_map/ppermute | solution.py:319
  47.9 3.4 %copy-start.1 = (f32[264,512]{1,0:T(8,128)S(1)}, f32[264,512]{1,0:T(8,128)}, u32[]{:S(2)}) copy-start(f32[264,512]{1,0:T(8,128)} %copy-done) | copy-start | bytes 1622020
  47.9 6.2 %collective-permute-start.8 = (bf16[256,1024]{1,0:T(8,128)(2,1)}, bf16[256,1024]{1,0:T(8,128)(2,1)}, u32[]{:S(2)}, u32[]{:S(2)}) collective-permute-start(bf16[256,1024]{1,0:T(8,128)(2,1)} %get-tuple-element.40), channel_id=1, source_target_pairs={{0,4},{4,0},{8,12},{12,8},{1,5},{5,1},{9,13},{13,9},{2,6},{6,2},{1... | collective-permute-start | bytes 1572872 | tf_op jit(solution)/shard_map/ppermute | solution.py:319
  52.4 8.1 %collective-permute-start.13 = (bf16[256,512]{1,0:T(8,128)(2,1)S(1)}, bf16[256,512]{1,0:T(8,128)(2,1)S(1)}, u32[]{:S(2)}, u32[]{:S(2)}) collective-permute-start(bf16[256,512]{1,0:T(8,128)(2,1)S(1)} %divide_convert_fusion.refs_0_), channel_id=1, source_target_pairs={{0,8},{4,12},{8,0},{12,4},{1,9},{5,13},{9,1},{13,5},{2,10},{6,14},... | collective-permute-start | bytes 786440 | tf_op jit(solution)/shard_map/ppermute | solution.py:319
  54.1 6.4 %collective-permute-start.14 = (bf16[256,512]{1,0:T(8,128)(2,1)S(1)}, bf16[256,512]{1,0:T(8,128)(2,1)S(1)}, u32[]{:S(2)}, u32[]{:S(2)}) collective-permute-start(bf16[256,512]{1,0:T(8,128)(2,1)S(1)} %divide_convert_fusion.refs_0_), channel_id=1, source_target_pairs={{0,4},{4,0},{8,12},{12,8},{1,5},{5,1},{9,13},{13,9},{2,6},{6,2},{1... | collective-permute-start | bytes 786440 | tf_op jit(solution)/shard_map/ppermute | solution.py:319
  60.5 1.5 %collective-permute-start.15 = (bf16[256,512]{1,0:T(8,128)(2,1)S(1)}, bf16[256,512]{1,0:T(8,128)(2,1)S(1)}, u32[]{:S(2)}, u32[]{:S(2)}) collective-permute-start(bf16[256,512]{1,0:T(8,128)(2,1)S(1)} %collective-permute-done.13.refs_1_), channel_id=1, source_target_pairs={{0,4},{4,0},{8,12},{12,8},{1,5},{5,1},{9,13},{13,9},{2,6},{6,2},{1... | collective-permute-start | bytes 786440 | tf_op jit(solution)/shard_map/ppermute | solution.py:319
  62.8 8.7 %collective-permute-start.16 = (bf16[256,512]{1,0:T(8,128)(2,1)S(1)}, bf16[256,512]{1,0:T(8,128)(2,1)S(1)}, u32[]{:S(2)}, u32[]{:S(2)}) collective-permute-start(bf16[256,512]{1,0:T(8,128)(2,1)S(1)} %get-tuple-element.50), channel_id=1, source_target_pairs={{0,1},{1,0},{2,3},{3,2},{4,5},{5,4},{6,7},{7,6},{8,9},{9,8},{10,11... | collective-permute-start | bytes 786440 | tf_op jit(solution)/shard_map/ppermute | solution.py:319
  64.8 9.0 %collective-permute-start.17 = (bf16[256,512]{1,0:T(8,128)(2,1)S(1)}, bf16[256,512]{1,0:T(8,128)(2,1)S(1)}, u32[]{:S(2)}, u32[]{:S(2)}) collective-permute-start(bf16[256,512]{1,0:T(8,128)(2,1)S(1)} %get-tuple-element.51), channel_id=1, source_target_pairs={{1,2},{2,1},{5,6},{6,5},{9,10},{10,9},{13,14},{14,13},{17,18},{18,... | collective-permute-start | bytes 786440 | tf_op jit(solution)/shard_map/ppermute | solution.py:459
  65.5 11.4 %collective-permute-start.18 = (bf16[256,512]{1,0:T(8,128)(2,1)S(1)}, bf16[256,512]{1,0:T(8,128)(2,1)S(1)}, u32[]{:S(2)}, u32[]{:S(2)}) collective-permute-start(bf16[256,512]{1,0:T(8,128)(2,1)S(1)} %get-tuple-element.51), channel_id=1, source_target_pairs={{0,2},{3,1},{4,6},{7,5},{8,10},{11,9},{12,14},{15,13},{16,18},{19,... | collective-permute-start | bytes 786440 | tf_op jit(solution)/shard_map/ppermute | solution.py:458
  71.5 14.2 %collective-permute-start.19 = (bf16[256,512]{1,0:T(8,128)(2,1)S(1)}, bf16[256,512]{1,0:T(8,128)(2,1)S(1)}, u32[]{:S(2)}, u32[]{:S(2)}) collective-permute-start(bf16[256,512]{1,0:T(8,128)(2,1)S(1)} %fusion.5), channel_id=1, source_target_pairs={{1,3},{2,0},{0,1},{3,2},{5,7},{6,4},{4,5},{7,6},{9,11},{10,8},{8,9... | collective-permute-start | bytes 786440 | tf_op jit(solution)/shard_map/ppermute | solution.py:461
